TPU v7x, 32 devices: a whole 2x2x4 slice. The times are simulated.
32 devices in a mesh: dp: 4 (over y, x), seq: 2 (over core), head: 4 (over z).
Axes of the slice: x: 2, y: 2, z: 4, core: 2. Of those that a mesh axis runs over, the one named last changes fastest.
Arguments:
- x_in: bfloat16 [8, 1024, 1536], P('dp', 'seq'), may hold values from -6 to 6
- d_out: bfloat16 [8, 1024, 1536], P('dp', 'seq'), may hold values from -6 to 6
- log_decay: float32 [8, 1024, 48], P('dp', 'seq', 'head'), may hold values from -1 to 0
- routes: int32 [8, 1024, 6], P('dp', 'seq'), may hold values from 0 to 15, all different within a row; in each aligned block of 128 rows (0 to 127, 128 to 255, ..., all dimensions but the last counted through in order) at most 96 rows name the same one
- norm1_gain: float32 [1536], replicated, may hold values from 0.5 to 1.5
- w_in_zx: bfloat16 [2, 1536, 3072], P(None, None, 'head'), may hold values from -0.15625 to 0.15625
- w_in_bc: bfloat16 [1536, 256], replicated, may hold values from -0.0390625 to 0.0390625
- w_in_dt: bfloat16 [1536, 48], P(None, 'head'), may hold values from -0.15625 to 0.15625
- dt_bias: float32 [48], P('head'), may hold values from -1 to 1
- conv_x: float32 [4, 3072], P(None, 'head'), may hold values from -3 to 3
- conv_x_bias: float32 [3072], P('head'), may hold values from -1.5 to 1.5
- conv_bc: float32 [4, 256], replicated, may hold values from -3 to 3
- conv_bc_bias: float32 [256], replicated, may hold values from -0.25 to 0.25
- skip_d: float32 [48], P('head'), may hold values from 0.5 to 1.5
- gate_norm_gain: float32 [3072], P('head'), may hold values from 0.5 to 1.5
- w_out: bfloat16 [3072, 1536], P('head'), may hold values from -0.109375 to 0.109375
- norm2_gain: float32 [1536], replicated, may hold values from 0.5 to 1.5
- router: bfloat16 [1536, 16], replicated, may hold values from -0.078125 to 0.078125
- w_expert_gu: bfloat16 [16, 1536, 1024], P(('seq', 'head')), may hold values from -0.15625 to 0.15625
- w_expert_down: bfloat16 [16, 512, 1536], P(('seq', 'head')), may hold values from -0.25 to 0.25
- w_shared_gu: bfloat16 [2, 1536, 1024], P(None, None, 'head'), may hold values from -0.15625 to 0.15625
- w_shared_down: bfloat16 [1024, 1536], P('head'), may hold values from -0.1875 to 0.1875
Outputs:
- layer_out: bfloat16 [8, 1024, 1536], P('dp', 'seq')
- d_input: bfloat16 [8, 1024, 1536], P('dp', 'seq')
- grad_norm1_gain: float32 [1536], replicated
- grad_w_in_zx: float32 [2, 1536, 3072], P(None, ('dp', 'seq'), 'head')
- grad_w_in_bc: float32 [1536, 256], replicated
- grad_w_in_dt: float32 [1536, 48], P(('dp', 'seq'), 'head')
- grad_dt_bias: float32 [48], replicated
- grad_conv_x: float32 [4, 3072], replicated
- grad_conv_x_bias: float32 [3072], replicated
- grad_conv_bc: float32 [4, 256], replicated
- grad_conv_bc_bias: float32 [256], replicated
- grad_skip_d: float32 [48], replicated
- grad_gate_norm_gain: float32 [3072], replicated
- grad_w_out: float32 [3072, 1536], P('head', ('dp', 'seq'))
- grad_norm2_gain: float32 [1536], replicated
- grad_router: float32 [1536, 16], replicated
- grad_expert_gu: float32 [16, 1536, 1024], P(('seq', 'head'), 'dp')
- grad_expert_down: float32 [16, 512, 1536], P(('seq', 'head'), None, 'dp')
- grad_shared_gu: float32 [2, 1536, 1024], P(None, ('dp', 'seq'), 'head')
- grad_shared_down: float32 [1024, 1536], P('head', ('dp', 'seq'))
Inputs may be any that keep to these rules, and one draw needn't show every extreme that they name: `routes`: in each aligned block of 128 positions (sequence by sequence, in order), no expert is named by more than 96 positions; each position names 6 different experts.
All inputs are finite; a program needn't handle non-finite values.
Results may differ from a plain program's by a relative error of at most 0.015.
The roundings to bfloat16 on the way count: a program that leaves them out, or rounds other values in their place, can miss the bound.
Values may be sent and summed in bfloat16 or wider, within the bound.
No kernel may reach another device: no remote copies, remote signals or barrier semaphores. Data moves between devices by JAX's collectives and lax.ppermute only.
A program may use at most 384 MiB of HBM per device.

v0:
```python
import jax
import jax.numpy as jnp
from jax import lax
from jax.sharding import PartitionSpec as P

BLOCK = 256


norm_eps = 1e-05
highest = lax.Precision.HIGHEST


def shifted(array, axis, by):
    count = lax.axis_size(axis)
    pairs = [(i, i + by) for i in range(count) if 0 <= i + by < count]
    return lax.ppermute(array, axis, pairs)


def prefix(part, axis, combine, identity):
    place = lax.axis_index(axis)
    gathered = jax.tree.map(lambda a: lax.all_gather(a, axis), part)
    state = jax.tree.map(lambda a, e: jnp.zeros_like(a) + jnp.asarray(e, a.dtype), part, identity)

    def one(lap, state):
        return combine(
            state, jax.tree.map(lambda a: lax.dynamic_index_in_dim(a, lap, 0, False), gathered)
        )

    return lax.fori_loop(0, place, one, state)


def prefix_2(array, axis, combine, identity):
    count, place = (lax.axis_size(axis), lax.axis_index(axis))
    everything = jax.tree.map(
        lambda part, kind: lax.all_gather(part.astype(kind), axis),
        array,
        jax.tree.map(lambda a: jnp.bfloat16 if a.dtype == jnp.float32 else a.dtype, array),
    )
    start = jax.tree.map(
        lambda part, zero: jnp.broadcast_to(jnp.asarray(zero, part.dtype), part.shape),
        array,
        identity,
    )

    def lap(k, before):
        at = count - 1 - k
        reached = at > place
        new = combine(
            before, jax.tree.map(lambda part, own: part[at].astype(own.dtype), everything, array)
        )
        return jax.tree.map(lambda a, b: jnp.where(reached, a, b), new, before)

    return lax.fori_loop(0, count, lap, start)


def silu_slope(argument):
    sigma = jax.nn.sigmoid(argument)
    return sigma * (1.0 + argument * (1.0 - sigma))


def spread_last(local_part, rank_index, part_count):
    local_width = local_part.shape[-1]
    full_array = jnp.zeros(local_part.shape[:-1] + (local_width * part_count,), jnp.float32)
    return lax.dynamic_update_slice_in_dim(
        full_array, local_part, rank_index * local_width, local_part.ndim - 1
    )


def block_states(scaled, map_b, within, block_total):
    tail_decay = jnp.exp(block_total[:, :, None, :] - within)
    return jnp.einsum("bksh,bkshp,bksn->bkhpn", tail_decay, scaled, map_b, precision=highest)


def leaving_state(states, before, block_total, device_total):
    weights_out = jnp.exp(device_total[:, None, :] - before - block_total)
    return jnp.einsum("bjh,bjhpn->bhpn", weights_out, states, precision=highest)


def scan_output(scaled, map_b, map_c, within, before, block_total, states, entering):
    block_len = within.shape[2]
    causal = (jnp.arange(block_len)[:, None] >= jnp.arange(block_len)[None, :])[
        None, None, :, :, None
    ]
    pair_gaps = within[:, :, :, None, :] - within[:, :, None, :, :]
    decays = jnp.where(causal, jnp.exp(jnp.where(causal, pair_gaps, 0.0)), 0.0)
    scores = jnp.einsum("bkqn,bksn->bkqs", map_c, map_b, precision=highest)
    inside = jnp.einsum("bkqsh,bkshp->bkqhp", decays * scores[..., None], scaled, precision=highest)
    after_block = before + block_total
    block_count = before.shape[1]
    earlier = (jnp.arange(block_count)[:, None] > jnp.arange(block_count)[None, :])[
        None, :, :, None
    ]
    gap_spans = before[:, :, None, :] - after_block[:, None, :, :]
    link_weights = jnp.where(earlier, jnp.exp(jnp.where(earlier, gap_spans, 0.0)), 0.0)
    starting = jnp.exp(before)[..., None, None] * entering[:, None] + jnp.einsum(
        "bkjh,bjhpn->bkhpn", link_weights, states, precision=highest
    )
    carried = (
        jnp.einsum("bkqn,bkhpn->bkqhp", map_c, starting, precision=highest)
        * jnp.exp(within)[..., None]
    )
    return inside + carried


def chain_forward(earlier, later):
    return (earlier[0] * later[0], later[0][..., None, None] * earlier[1] + later[1])


def chain_backward(earlier, later):
    return (earlier[0] * later[0], later[1] + later[0][..., None, None] * earlier[1])


def local(
    x_in,
    d_out,
    log_decay,
    routes,
    norm1_gain,
    w_in_zx,
    w_in_bc,
    w_in_dt,
    dt_bias,
    conv_x,
    conv_x_bias,
    conv_bc,
    conv_bc_bias,
    skip_d,
    gate_norm_gain,
    w_out,
    norm2_gain,
    router,
    w_expert_gu,
    w_expert_down,
    w_shared_gu,
    w_shared_down,
):
    batch_size, tokens, model_width = x_in.shape
    inner_dev = w_in_zx.shape[2]
    heads_dev = w_in_dt.shape[1]
    head_size = inner_dev // heads_dev
    state_size = w_in_bc.shape[1] // 2
    conv_taps = conv_x.shape[0]
    experts_dev = w_expert_gu.shape[0]
    expert_ff = w_expert_down.shape[1]
    top_count = routes.shape[2]
    head_count = lax.axis_size("head")
    route_count = lax.axis_size(("seq", "head"))
    head_rank = lax.axis_index("head")
    inner_all = inner_dev * head_count
    experts_all = experts_dev * route_count
    share_rows = tokens // head_count
    capacity = min(
        share_rows, max(2, (2 * share_rows * top_count + experts_all - 1) // experts_all)
    )
    blocks = tokens // BLOCK

    def blockify(array_in):
        return array_in.reshape((batch_size, blocks, BLOCK) + array_in.shape[2:])

    input_wide = x_in.astype(jnp.float32)
    scale_one = lax.rsqrt(jnp.mean(input_wide * input_wide, axis=-1, keepdims=True) + norm_eps)
    normed_one = (input_wide * scale_one * norm1_gain).astype(jnp.bfloat16)
    proj_zx = jnp.einsum("btd,cdk->cbtk", normed_one, w_in_zx, preferred_element_type=jnp.float32)
    gate_z = proj_zx[0]
    bc_proj = jnp.einsum("btd,dn->btn", normed_one, w_in_bc, preferred_element_type=jnp.float32)
    step_raw = jnp.einsum("btd,dh->bth", normed_one, w_in_dt, preferred_element_type=jnp.float32)
    conv_in = jnp.concatenate([proj_zx[1], bc_proj], axis=-1).astype(jnp.bfloat16)
    edge_rows = shifted(conv_in[:, tokens - (conv_taps - 1) :, :], "seq", 1)
    padded = jnp.concatenate([edge_rows, conv_in], axis=1).astype(jnp.float32)
    conv_weight = jnp.concatenate([conv_x, conv_bc], axis=1)
    conv_bias = jnp.concatenate([conv_x_bias, conv_bc_bias])
    conv_pre = jnp.broadcast_to(conv_bias, padded[:, :tokens].shape)
    for offset in range(conv_taps):
        conv_pre = conv_pre + conv_weight[offset] * padded[:, offset : offset + tokens, :]
    conv_act = jax.nn.silu(conv_pre).astype(jnp.bfloat16)
    input_x = (
        conv_act[..., :inner_dev]
        .astype(jnp.float32)
        .reshape(batch_size, tokens, heads_dev, head_size)
    )
    input_b = conv_act[..., inner_dev : inner_dev + state_size].astype(jnp.float32)
    input_c = conv_act[..., inner_dev + state_size :].astype(jnp.float32)
    step_size = jax.nn.softplus(step_raw + dt_bias)
    within = jnp.cumsum(log_decay.reshape(batch_size, blocks, BLOCK, heads_dev), axis=2)
    block_total = within[:, :, -1, :]
    before = jnp.cumsum(block_total, axis=1) - block_total
    device_total = jnp.sum(block_total, axis=1)
    device_decay = jnp.exp(device_total)
    scaled = blockify(input_x * step_size[..., None])
    b_blocks = blockify(input_b)
    states = block_states(scaled, b_blocks, within, block_total)
    leaving = leaving_state(states, before, block_total, device_total)
    identity = (jnp.ones_like(device_decay), jnp.zeros_like(leaving))
    _, entering = prefix((device_decay, leaving), "seq", chain_forward, identity)
    scanned = scan_output(
        scaled, b_blocks, blockify(input_c), within, before, block_total, states, entering
    )
    mixed = scanned.reshape(batch_size, tokens, heads_dev, head_size) + skip_d[:, None] * input_x
    mixed_flat = mixed.reshape(batch_size, tokens, inner_dev)
    z_silu = jax.nn.silu(gate_z)
    gated = mixed_flat * z_silu
    squares = jnp.sum(gated * gated, axis=-1)
    gated_low = (gated * gate_norm_gain).astype(jnp.bfloat16)
    partial_out = jnp.einsum("btk,kd->btd", gated_low, w_out, preferred_element_type=jnp.float32)
    mix_out, squares = lax.psum((partial_out, squares), "head")
    gate_scale = lax.rsqrt(squares / inner_all + norm_eps)[..., None]
    hidden = input_wide + mix_out * gate_scale
    scale_two = lax.rsqrt(jnp.mean(hidden * hidden, axis=-1, keepdims=True) + norm_eps)
    normed_two = (hidden * scale_two * norm2_gain).astype(jnp.bfloat16)
    shared_gu = jnp.einsum(
        "btd,cdf->cbtf", normed_two, w_shared_gu, preferred_element_type=jnp.float32
    )
    shared_act = (jax.nn.silu(shared_gu[0]) * shared_gu[1]).astype(jnp.bfloat16)
    shared_out = jnp.einsum(
        "btf,fd->btd", shared_act, w_shared_down, preferred_element_type=jnp.float32
    )
    share_start = head_rank * share_rows
    normed_share = lax.dynamic_slice_in_dim(normed_two, share_start, share_rows, 1)
    grad_share = lax.dynamic_slice_in_dim(d_out, share_start, share_rows, 1)
    route_share = lax.dynamic_slice_in_dim(routes, share_start, share_rows, 1)
    logits = jnp.einsum("brd,de->bre", normed_share, router, preferred_element_type=jnp.float32)
    expert_ids = jnp.arange(experts_all, dtype=jnp.int32)
    chosen = (route_share[..., None] == expert_ids).astype(jnp.float32)
    picked = jnp.einsum("brke,bre->brk", chosen, logits, precision=highest)
    gate_weights = jax.nn.softmax(picked, axis=-1)
    flat_routes = route_share.reshape(batch_size, share_rows * top_count)
    route_hits = (flat_routes[..., None] == expert_ids).astype(jnp.int32)
    slot_ranks = jnp.sum((jnp.cumsum(route_hits, axis=1) - route_hits) * route_hits, axis=-1)
    owners = flat_routes // experts_dev
    local_ids = flat_routes % experts_dev
    seq_ids = jnp.arange(batch_size, dtype=jnp.int32)[:, None]
    slot_pos = (
        ((local_ids * route_count + owners) * batch_size + seq_ids) * capacity + slot_ranks
    ).reshape(-1)
    slot_total = experts_dev * route_count * batch_size * capacity
    assign_count = batch_size * share_rows * top_count
    filled = (
        jnp.zeros((slot_total,), jnp.int32)
        .at[slot_pos]
        .set(jnp.arange(assign_count, dtype=jnp.int32) + 1)
    )
    row_pick = jnp.where(filled > 0, (filled - 1) // top_count + 1, 0)
    zero_row = jnp.zeros((1, model_width), jnp.bfloat16)
    rows_pad = jnp.concatenate([zero_row, normed_share.reshape(-1, model_width)], axis=0)
    buffer_shape = (experts_dev, route_count, batch_size * capacity, model_width)
    send_rows = rows_pad[row_pick].reshape(buffer_shape)
    weighted = (gate_weights[..., None] * grad_share[:, :, None, :].astype(jnp.float32)).astype(
        jnp.bfloat16
    )
    grads_pad = jnp.concatenate([zero_row, weighted.reshape(-1, model_width)], axis=0)
    send_grads = grads_pad[filled].reshape(buffer_shape)
    got_rows, got_grads = (
        lax.all_to_all(send_rows, ("seq", "head"), split_axis=1, concat_axis=1, tiled=True),
        lax.all_to_all(send_grads, ("seq", "head"), split_axis=1, concat_axis=1, tiled=True),
    )
    rows_flat = got_rows.reshape(experts_dev, -1, model_width)
    push_flat = got_grads.reshape(experts_dev, -1, model_width)
    expert_gu = jnp.einsum(
        "esd,edf->esf", rows_flat, w_expert_gu, preferred_element_type=jnp.float32
    )
    expert_gate = expert_gu[..., :expert_ff]
    expert_up = expert_gu[..., expert_ff:]
    expert_act = (jax.nn.silu(expert_gate) * expert_up).astype(jnp.bfloat16)
    expert_out = jnp.einsum(
        "esf,efd->esd", expert_act, w_expert_down, preferred_element_type=jnp.float32
    ).astype(jnp.bfloat16)
    act_push = jnp.einsum(
        "esd,efd->esf", push_flat, w_expert_down, preferred_element_type=jnp.float32
    )
    grad_expert_down = jnp.einsum(
        "esf,esd->efd", expert_act, push_flat, preferred_element_type=jnp.float32
    )
    expert_gu_grad = jnp.concatenate(
        [act_push * expert_up * silu_slope(expert_gate), act_push * jax.nn.silu(expert_gate)],
        axis=-1,
    ).astype(jnp.bfloat16)
    grad_expert_gu = jnp.einsum(
        "esd,esf->edf", rows_flat, expert_gu_grad, preferred_element_type=jnp.float32
    )
    expert_dx = jnp.einsum(
        "esf,edf->esd", expert_gu_grad, w_expert_gu, preferred_element_type=jnp.float32
    ).astype(jnp.bfloat16)
    back_out, back_grad = (
        lax.all_to_all(
            expert_out.reshape(buffer_shape),
            ("seq", "head"),
            split_axis=1,
            concat_axis=1,
            tiled=True,
        ),
        lax.all_to_all(
            expert_dx.reshape(buffer_shape),
            ("seq", "head"),
            split_axis=1,
            concat_axis=1,
            tiled=True,
        ),
    )
    out_assign = (
        back_out.reshape(slot_total, model_width)[slot_pos]
        .reshape(batch_size, share_rows, top_count, model_width)
        .astype(jnp.float32)
    )
    dx_assign = (
        back_grad.reshape(slot_total, model_width)[slot_pos]
        .reshape(batch_size, share_rows, top_count, model_width)
        .astype(jnp.float32)
    )
    routed = jnp.sum(gate_weights[..., None] * out_assign, axis=2)
    placed = lax.dynamic_update_slice_in_dim(jnp.zeros_like(shared_out), routed, share_start, 1)
    ffn_total = lax.psum((shared_out + placed).astype(jnp.bfloat16), "head").astype(jnp.float32)
    layer_out = (hidden + ffn_total).astype(jnp.bfloat16)
    grad_wide = d_out.astype(jnp.float32)
    gate_push = jnp.sum(grad_share.astype(jnp.float32)[:, :, None, :] * out_assign, axis=-1)
    pick_grad = gate_weights * (
        gate_push - jnp.sum(gate_weights * gate_push, axis=-1, keepdims=True)
    )
    logit_grad = jnp.einsum("brk,brke->bre", pick_grad, chosen, precision=highest)
    grad_router = jnp.einsum(
        "brd,bre->de",
        normed_share,
        logit_grad,
        precision=highest,
        preferred_element_type=jnp.float32,
    )
    share_grad = jnp.sum(dx_assign, axis=2) + jnp.einsum(
        "bre,de->brd", logit_grad, router.astype(jnp.float32), precision=highest
    )
    shared_push = jnp.einsum(
        "btd,fd->btf", d_out, w_shared_down, preferred_element_type=jnp.float32
    )
    grad_shared_down = jnp.einsum(
        "btf,btd->fd", shared_act, d_out, preferred_element_type=jnp.float32
    )
    shared_gate = shared_gu[0]
    shared_up = shared_gu[1]
    shared_gu_grad = jnp.stack(
        [shared_push * shared_up * silu_slope(shared_gate), shared_push * jax.nn.silu(shared_gate)]
    ).astype(jnp.bfloat16)
    grad_shared_gu = jnp.einsum(
        "btd,cbtf->cdf", normed_two, shared_gu_grad, preferred_element_type=jnp.float32
    )
    normed_two_grad = jnp.einsum(
        "cbtf,cdf->btd", shared_gu_grad, w_shared_gu, preferred_element_type=jnp.float32
    )
    normed_two_grad = normed_two_grad + lax.dynamic_update_slice_in_dim(
        jnp.zeros_like(normed_two_grad), share_grad, share_start, 1
    )
    normed_two_grad = lax.psum(normed_two_grad, "head")
    gained_two = normed_two_grad * norm2_gain
    hidden_grad = grad_wide + scale_two * (
        gained_two
        - hidden * scale_two * scale_two * jnp.mean(gained_two * hidden, axis=-1, keepdims=True)
    )
    grad_norm_two = jnp.sum(normed_two_grad * hidden * scale_two, axis=(0, 1))
    out_push = (hidden_grad * gate_scale).astype(jnp.bfloat16)
    scale_push = jnp.sum(hidden_grad * mix_out, axis=-1)
    squares_grad = -0.5 * scale_push * gate_scale[..., 0] ** 3 / inner_all
    gated_grad_low = jnp.einsum("btd,kd->btk", out_push, w_out, preferred_element_type=jnp.float32)
    grad_w_out = jnp.einsum("btk,btd->kd", gated_low, out_push, preferred_element_type=jnp.float32)
    gated_grad = gated_grad_low * gate_norm_gain + 2.0 * gated * squares_grad[..., None]
    grad_gate_gain = jnp.sum(gated_grad_low * gated, axis=(0, 1))
    mixed_grad = (gated_grad * z_silu).reshape(batch_size, tokens, heads_dev, head_size)
    z_grad = (gated_grad * mixed_flat * silu_slope(gate_z)).astype(jnp.bfloat16)
    grad_skip = jnp.sum(mixed_grad * input_x, axis=(0, 1, 3))
    device_cum = jnp.exp(before[:, :, None, :] + within).reshape(batch_size, tokens, heads_dev)
    entering_grad = jnp.einsum(
        "bth,bthp,btn->bhpn", device_cum, mixed_grad, input_c, precision=highest
    )
    _, leaving_grad = prefix_2((device_decay, entering_grad), "seq", chain_backward, identity)

    def mixer_local(x_value, b_value, c_value, step_value):
        scaled_value = blockify(x_value * step_value[..., None])
        b_value_blocks = blockify(b_value)
        state_value = block_states(scaled_value, b_value_blocks, within, block_total)
        outputs = scan_output(
            scaled_value,
            b_value_blocks,
            blockify(c_value),
            within,
            before,
            block_total,
            state_value,
            entering,
        )
        return (
            outputs.reshape(x_value.shape),
            leaving_state(state_value, before, block_total, device_total),
        )

    _, pull_back = jax.vjp(mixer_local, input_x, input_b, input_c, step_size)
    x_grad, b_grad, c_grad, step_grad = pull_back((mixed_grad, leaving_grad))
    x_grad = x_grad + skip_d[:, None] * mixed_grad
    raw_grad = step_grad * jax.nn.sigmoid(step_raw + dt_bias)
    grad_dt_bias = jnp.sum(raw_grad, axis=(0, 1))
    act_grad = jnp.concatenate(
        [x_grad.reshape(batch_size, tokens, inner_dev), b_grad, c_grad], axis=-1
    )
    pre_grad = act_grad * silu_slope(conv_pre)
    grad_conv = jnp.stack(
        [
            jnp.sum(pre_grad * padded[:, offset : offset + tokens, :], axis=(0, 1))
            for offset in range(conv_taps)
        ]
    )
    grad_conv_bias = jnp.sum(pre_grad, axis=(0, 1))
    padded_grad = jnp.zeros_like(padded)
    for offset in range(conv_taps):
        padded_grad = padded_grad.at[:, offset : offset + tokens, :].add(
            conv_weight[offset] * pre_grad
        )
    tail_grad = shifted(padded_grad[:, : conv_taps - 1, :], "seq", -1)
    in_grad = padded_grad[:, conv_taps - 1 :, :]
    in_grad = in_grad.at[:, tokens - (conv_taps - 1) :, :].add(tail_grad)
    zx_grad = jnp.stack([z_grad, in_grad[..., :inner_dev].astype(jnp.bfloat16)])
    bc_grad = in_grad[..., inner_dev:]
    grad_w_zx = jnp.einsum("btd,cbtk->cdk", normed_one, zx_grad, preferred_element_type=jnp.float32)
    grad_w_bc = jnp.einsum(
        "btd,btn->dn", normed_one, bc_grad, precision=highest, preferred_element_type=jnp.float32
    )
    grad_w_dt = jnp.einsum(
        "btd,bth->dh", normed_one, raw_grad, precision=highest, preferred_element_type=jnp.float32
    )
    normed_one_grad = jnp.einsum(
        "cbtk,cdk->btd", zx_grad, w_in_zx, preferred_element_type=jnp.float32
    )
    normed_one_grad = normed_one_grad + jnp.einsum(
        "btn,dn->btd", bc_grad, w_in_bc.astype(jnp.float32), precision=highest
    )
    normed_one_grad = normed_one_grad + jnp.einsum(
        "bth,dh->btd", raw_grad, w_in_dt.astype(jnp.float32), precision=highest
    )
    normed_one_grad = lax.psum(normed_one_grad, "head")
    gained_one = normed_one_grad * norm1_gain
    input_grad = hidden_grad + scale_one * (
        gained_one
        - input_wide
        * scale_one
        * scale_one
        * jnp.mean(gained_one * input_wide, axis=-1, keepdims=True)
    )
    grad_norm_one = jnp.sum(normed_one_grad * input_wide * scale_one, axis=(0, 1))
    first_head = (head_rank == 0).astype(jnp.float32)
    small_sums = lax.psum(
        (
            grad_norm_one * first_head,
            grad_norm_two * first_head,
            grad_router,
            grad_w_bc,
            grad_conv[:, inner_dev:],
            grad_conv_bias[inner_dev:],
            spread_last(grad_conv[:, :inner_dev], head_rank, head_count),
            spread_last(grad_conv_bias[:inner_dev], head_rank, head_count),
            spread_last(grad_gate_gain, head_rank, head_count),
            spread_last(grad_dt_bias, head_rank, head_count),
            spread_last(grad_skip, head_rank, head_count),
        ),
        ("dp", "seq", "head"),
    )
    large_sums = (
        lax.psum_scatter(
            grad_w_zx.astype(jnp.bfloat16), ("dp", "seq"), scatter_dimension=1, tiled=True
        ).astype(jnp.float32),
        lax.psum_scatter(
            grad_w_out.astype(jnp.bfloat16), ("dp", "seq"), scatter_dimension=1, tiled=True
        ).astype(jnp.float32),
        lax.psum_scatter(
            grad_shared_gu.astype(jnp.bfloat16), ("dp", "seq"), scatter_dimension=1, tiled=True
        ).astype(jnp.float32),
        lax.psum_scatter(
            grad_shared_down.astype(jnp.bfloat16), ("dp", "seq"), scatter_dimension=1, tiled=True
        ).astype(jnp.float32),
        lax.psum_scatter(
            grad_w_dt.astype(jnp.bfloat16), ("dp", "seq"), scatter_dimension=0, tiled=True
        ).astype(jnp.float32),
    )
    expert_sums = (
        lax.psum_scatter(
            grad_expert_gu.astype(jnp.bfloat16), "dp", scatter_dimension=1, tiled=True
        ).astype(jnp.float32),
        lax.psum_scatter(
            grad_expert_down.astype(jnp.bfloat16), "dp", scatter_dimension=2, tiled=True
        ).astype(jnp.float32),
    )
    return (
        layer_out,
        input_grad.astype(jnp.bfloat16),
        small_sums[0],
        large_sums[0],
        small_sums[3],
        large_sums[4],
        small_sums[9],
        small_sums[6],
        small_sums[7],
        small_sums[4],
        small_sums[5],
        small_sums[10],
        small_sums[8],
        large_sums[1],
        small_sums[1],
        small_sums[2],
        expert_sums[0],
        expert_sums[1],
        large_sums[2],
        large_sums[3],
    )


def solution(mesh):
    placed = (
        P("dp", "seq", None),
        P("dp", "seq", None),
        P("dp", "seq", "head"),
        P("dp", "seq", None),
        P(),
        P(None, None, "head"),
        P(),
        P(None, "head"),
        P("head"),
        P(None, "head"),
        P("head"),
        P(),
        P(),
        P("head"),
        P("head"),
        P("head", None),
        P(),
        P(),
        P(("seq", "head"), None, None),
        P(("seq", "head"), None, None),
        P(None, None, "head"),
        P("head", None),
    )
    return jax.shard_map(
        local,
        mesh=mesh,
        in_specs=placed,
        out_specs=(
            P("dp", "seq", None),
            P("dp", "seq", None),
            P(),
            P(None, ("dp", "seq"), "head"),
            P(),
            P(("dp", "seq"), "head"),
            P(),
            P(),
            P(),
            P(),
            P(),
            P(),
            P(),
            P("head", ("dp", "seq")),
            P(),
            P(),
            P(("seq", "head"), "dp", None),
            P(("seq", "head"), None, "dp"),
            P(None, ("dp", "seq"), "head"),
            P("head", ("dp", "seq")),
        ),
        check_vma=False,
    )
```

profile of v0, /device:TPU:0, one launch (start us, length us, event | category | flops | bytes accessed | tf_op | source)
XLA Modules:
  0.0 2540.3 jit_solution(15369551000994845558)
XLA Ops:
  10.2 7.1 fusion.61
  62.2 6.5 fusion.106
  79.5 9.5 fusion.108
  89.1 15.6 fusion.6
  115.0 5.5 reshape.583
  140.1 6.2 scatter_custom_fusion
  146.4 13.6 psum.113
  160.6 201.8 %all-reduce.16.cloned.1.call-done = f32[2,512,1536]{2,1,0:T(8,128)} async-done(((f32[2,512,1536]{2,1,0:T(8,128)}), f32[2,512,1536]{2,1,0:T(8,128)}) %all-reduce.16.cloned.1.call-update) | async-done | bytes 6291472 | tf_op jit(solution)/shard_map/psum | solution.py:205
  372.2 20.6 gather_fusion
  392.8 8.1 copy.331
  408.3 6.2 mul.657
  414.5 11.8 mul.658
  437.7 22.3 gather_fusion.2
  460.0 8.1 copy.337
  468.1 143.7 %all-to-all-done = bf16[2,8,192,1536]{3,2,0,1:T(8,128)(2,1)} async-done(((bf16[2,8,192,1536]{3,2,0,1:T(8,128)(2,1)}), bf16[2,8,192,1536]{3,2,0,1:T(8,128)(2,1)}, u32[]{:S(2)}, u32[]{:S(2)}) %all-to-all-start) | async-done | bytes 9437216 | tf_op jit(solution)/shard_map/all_to_all | solution.py:253
  611.7 5.3 all-to-all-start.2
  617.0 8.1 copy.332
  625.1 17.5 fusion.197
  642.6 180.3 %all-to-all-done.2 = bf16[2,8,192,1536]{3,2,0,1:T(8,128)(2,1)} async-done(((bf16[2,8,192,1536]{3,2,0,1:T(8,128)(2,1)}), bf16[2,8,192,1536]{3,2,0,1:T(8,128)(2,1)}, u32[]{:S(2)}, u32[]{:S(2)}) %all-to-all-start.2) | async-done | bytes 9437216 | tf_op jit(solution)/shard_map/all_to_all | solution.py:254
  822.9 8.2 copy.338
  831.1 16.6 multiply_convert_fusion.3
  847.7 8.0 convolution_convert_fusion.1
  855.7 8.1 copy.335
  863.8 5.3 all-to-all-start.1
  869.1 16.5 convolution_convert_fusion
  885.6 8.2 copy.340
  893.8 181.2 %all-to-all-done.1 = bf16[2,8,192,1536]{3,2,0,1:T(8,128)(2,1)} async-done(((bf16[2,8,192,1536]{3,2,0,1:T(8,128)(2,1)}), bf16[2,8,192,1536]{3,2,0,1:T(8,128)(2,1)}, u32[]{:S(2)}, u32[]{:S(2)}) %all-to-all-start.1) | async-done | bytes 9437216 | tf_op jit(solution)/shard_map/all_to_all | solution.py:284
  1092.0 8.1 copy.336
  1100.1 15.5 gather_fusion.1
  1115.6 9.0 reshape.604
  1124.6 19.6 multiply_reduce_fusion
  1145.6 140.3 %all-to-all-done.3 = bf16[2,8,192,1536]{3,2,0,1:T(8,128)(2,1)} async-done(((bf16[2,8,192,1536]{3,2,0,1:T(8,128)(2,1)}), bf16[2,8,192,1536]{3,2,0,1:T(8,128)(2,1)}, u32[]{:S(2)}, u32[]{:S(2)}) %all-to-all-start.3) | async-done | bytes 9437216 | tf_op jit(solution)/shard_map/all_to_all | solution.py:291
  1285.9 8.2 copy.341
  1294.1 15.3 gather_fusion.3
  1309.4 9.0 reshape.605
  1318.4 8.5 reduce_sum.250
  1340.8 10.6 convolution_convert_fusion.3
  1351.4 7.1 copy.412
  1374.0 17.4 convolution_convert_fusion.2
  1391.4 160.4 %all-reduce.20.cloned.1.call-done = f32[2,512,1536]{2,1,0:T(8,128)} async-done(((f32[2,512,1536]{2,1,0:T(8,128)}), f32[2,512,1536]{2,1,0:T(8,128)}) %all-reduce.20.cloned.1.call-update) | async-done | bytes 6291472 | tf_op jit(solution)/shard_map/psum | solution.py:349
  1551.8 5.6 multiply_reduce_fusion.2
  1557.5 116.6 %all-reduce.18.cloned.1.call-done = bf16[2,512,1536]{2,1,0:T(8,128)(2,1)} async-done(((bf16[2,512,1536]{2,1,0:T(8,128)(2,1)}), bf16[2,512,1536]{2,1,0:T(8,128)(2,1)}) %all-reduce.18.cloned.1.call-update) | async-done | bytes 3145744 | tf_op jit(solution)/shard_map/psum | solution.py:311
  1674.1 11.5 multiply_reduce_fusion.3
  1686.0 8.9 multiply_reduce_fusion.11
  1716.8 9.2 add_bitcast_fusion
  1726.0 10.9 fusion.4
  1742.9 5.7 reshape.597
  1752.3 6.7 fusion.100
  1759.1 16.0 fusion.2
  1796.0 12.2 scatter-add.15
  1808.2 8.1 slice_add_fusion.1
  1816.3 12.3 scatter-add.16
  1847.6 7.4 fusion.36
  1855.0 12.6 copy.360
  1868.2 8.1 bitcast_convert_fusion.2
  1879.4 7.1 fusion.32
  1886.5 6.4 fusion.20
  1912.4 6.2 convolution_bitcast_fusion.2
  1920.3 61.6 %all-reduce.28.cloned.1.call-done = (bf16[2,1536,768]{2,0,1:T(2,128)(2,1)}, bf16[2,1536,256]{2,0,1:T(2,128)(2,1)}) async-done(((bf16[2,1536,768]{2,0,1:T(2,128)(2,1)}, bf16[2,1536,256]{2,0,1:T(2,128)(2,1)}), (bf16[2,1536,768]{2,0,1:T(2,128)(2,1)}, bf16[2,1536,256]{2,0,1:T(2,128)(2,1)})) %all-reduce.28.cloned.1.call-update) | async-done | bytes 6291472
  1986.2 42.4 %reduce-scatter.10.cloned.1.call-done = bf16[768,192]{0,1:T(8,128)(2,1)} async-done(((bf16[768,1536]{0,1:T(8,128)(2,1)}), bf16[768,192]{0,1:T(8,128)(2,1)}) %reduce-scatter.10.cloned.1.call-update) | async-done | bytes 294928 | tf_op jit(solution)/shard_map/reduce_scatter | solution.py:464
  2030.4 223.4 %all-reduce.22.cloned.1.call-done = f32[2,512,1536]{2,1,0:T(8,128)} async-done(((f32[2,512,1536]{2,1,0:T(8,128)}), f32[2,512,1536]{2,1,0:T(8,128)}) %all-reduce.22.cloned.1.call-update) | async-done | bytes 6291472 | tf_op jit(solution)/shard_map/psum | solution.py:433
  2258.3 8.4 fusion.15
  2266.7 125.0 %all-reduce.26.cloned.1.call-done = (f32[1536,256]{1,0:T(8,128)}, f32[1536,16]{0,1:T(8,128)}) async-done(((f32[1536,256]{1,0:T(8,128)}, f32[1536,16]{0,1:T(8,128)}), (f32[1536,256]{1,0:T(8,128)}, f32[1536,16]{0,1:T(8,128)})) %all-reduce.26.cloned.1.call-update) | async-done | bytes 1671184 | tf_op jit(solution)/shard_map/psum | solution.py:444
  2391.7 132.6 %all-reduce.24.cloned.1.call-done = (f32[1536]{0:T(1024)}, f32[48]{0:T(128)}, f32[4,3072]{1,0:T(4,128)}, f32[3072]{0:T(1024)}, f32[4,256]{1,0:T(4,128)}, /*index...) async-done(((f32[1536]{0:T(1024)}, f32[48]{0:T(128)}, f32[4,3072]{1,0:T(4,128)}, f32[3072]{0:T(1024)}, f32[4,256]{1,0:T(4,128)}, /*index=5*/f32[256]{0:T(256)}, ...) | async-done | bytes 91536 | tf_op jit(solution)/shard_map/psum | solution.py:444
  (536 shorter events, 284.8 us)
Async XLA Ops:
  7.2 823.9 %copy-start = (bf16[2,512,1536]{2,1,0:T(8,128)(2,1)S(1)}, bf16[2,512,1536]{2,1,0:T(8,128)(2,1)}, u32[]{:S(2)}) copy-start(bf16[2,512,1536]{2,1,0:T(8,128)(2,1)} %param.55) | copy-start | bytes 9437188
  7.2 97.4 %all-gather.8.cloned.1.call-start = ((), (), s32[]{:S(2)}) async-start(), calls=%async_computation.16 | async-start | bytes 2359296 | tf_op jit(solution)/shard_map/all_gather | solution.py:21
  10.2 24.0 copy-start.99
  20.5 13.7 copy-start.89
  20.5 13.7 copy-start.144
  21.3 17.9 collective-permute-start
  39.0 18.4 copy-start.54
  39.1 49.9 %copy-start.64 = (f32[2,2,256,12]{2,3,1,0:T(8,128)}, f32[2,2,256,12]{2,3,1,0:T(8,128)S(1)}, u32[]{:S(2)}) copy-start(f32[2,2,256,12]{2,3,1,0:T(8,128)S(1)} %copy.305) | copy-start | bytes 147460
  48.7 29.4 %copy-start.31 = (bf16[2,512,128]{2,1,0:T(8,128)(2,1)}, bf16[2,512,128]{2,1,0:T(8,128)(2,1)S(1)}, u32[]{:S(2)}) copy-start(bf16[2,512,128]{2,1,0:T(8,128)(2,1)S(1)} %get-tuple-element.442) | copy-start | bytes 786436
  62.2 11.1 copy-start.126
  68.8 293.7 %all-reduce.16.cloned.1.call-start = ((), (), s32[]{:S(2)}) async-start(), calls=%async_computation.9 | async-start | bytes 12582912 | tf_op jit(solution)/shard_map/psum | solution.py:205
  71.5 33.2 %copy-start.79 = (f32[2,2,12]{1,2,0:T(8,128)}, f32[2,2,12]{1,2,0:T(8,128)S(1)}, u32[]{:S(2)}) copy-start(f32[2,2,12]{1,2,0:T(8,128)S(1)} %copy.315) | copy-start | bytes 580
  75.3 30.6 %copy-start.56 = (f32[2,2,256,12]{2,3,1,0:T(8,128)}, f32[2,2,256,12]{2,3,1,0:T(8,128)S(1)}, u32[]{:S(2)}) copy-start(f32[2,2,256,12]{2,3,1,0:T(8,128)S(1)} %copy.320) | copy-start | bytes 147460
  78.0 11.1 copy-start.11
  78.0 11.1 copy-start.83
  78.0 11.0 copy-start.86
  135.7 292.0 %copy-start.47 = (s32[2,128,6]{2,1,0:T(8,128)}, s32[2,128,6]{2,1,0:T(8,128)S(1)}, u32[]{:S(2)}) copy-start(s32[2,128,6]{2,1,0:T(8,128)S(1)} %copy.324) | copy-start | bytes 18436
  160.6 206.7 %copy-start.119 = (f32[2,512]{1,0:T(2,128)}, f32[2,512]{1,0:T(2,128)S(1)}, u32[]{:S(2)}) copy-start(f32[2,512]{1,0:T(2,128)S(1)} %add_rsqrt_fusion.1) | copy-start | bytes 12292
  160.6 206.8 %copy-start.75 = (f32[1536]{0:T(1024)S(1)}, f32[1536]{0:T(1024)}, u32[]{:S(2)}) copy-start(f32[1536]{0:T(1024)} %param.52) | copy-start | bytes 18436
  400.8 210.9 %all-to-all-start = ((bf16[2,8,192,1536]{3,2,0,1:T(8,128)(2,1)}), bf16[2,8,192,1536]{3,2,0,1:T(8,128)(2,1)}, u32[]{:S(2)}, u32[]{:S(2)}) async-start(bf16[2,8,192,1536]{3,2,0,1:T(8,128)(2,1)} %copy.331), calls=%async_computation | async-start | bytes 18874368 | tf_op jit(solution)/shard_map/all_to_all | solution.py:253
  414.5 11.8 copy-start.71
  611.7 211.1 %all-to-all-start.2 = ((bf16[2,8,192,1536]{3,2,0,1:T(8,128)(2,1)}), bf16[2,8,192,1536]{3,2,0,1:T(8,128)(2,1)}, u32[]{:S(2)}, u32[]{:S(2)}) async-start(bf16[2,8,192,1536]{3,2,0,1:T(8,128)(2,1)} %copy.337), calls=%async_computation.2 | async-start | bytes 18874368 | tf_op jit(solution)/shard_map/all_to_all | solution.py:254
  863.8 211.2 %all-to-all-start.1 = ((bf16[2,8,192,1536]{3,2,0,1:T(8,128)(2,1)}), bf16[2,8,192,1536]{3,2,0,1:T(8,128)(2,1)}, u32[]{:S(2)}, u32[]{:S(2)}) async-start(bf16[2,8,192,1536]{3,2,0,1:T(8,128)(2,1)} %copy.335), calls=%async_computation.1 | async-start | bytes 18874368 | tf_op jit(solution)/shard_map/all_to_all | solution.py:284
  893.8 186.3 %copy-start.110 = (s32[1536]{0:T(1024)S(1)}, s32[1536]{0:T(1024)}, u32[]{:S(2)}) copy-start(s32[1536]{0:T(1024)} %copy-done.109) | copy-start | bytes 18436
  1075.0 210.9 %all-to-all-start.3 = ((bf16[2,8,192,1536]{3,2,0,1:T(8,128)(2,1)}), bf16[2,8,192,1536]{3,2,0,1:T(8,128)(2,1)}, u32[]{:S(2)}, u32[]{:S(2)}) async-start(bf16[2,8,192,1536]{3,2,0,1:T(8,128)(2,1)} %copy.340), calls=%async_computation.3 | async-start | bytes 18874368 | tf_op jit(solution)/shard_map/all_to_all | solution.py:291
  1080.0 471.8 %all-reduce.20.cloned.1.call-start = ((), (), s32[]{:S(2)}) async-start(), calls=%async_computation.11 | async-start | bytes 12582912 | tf_op jit(solution)/shard_map/psum | solution.py:349
  1124.6 19.6 copy-start.45
  1124.6 19.6 copy-start.118
  1124.6 19.9 copy-start.48
  1145.6 181.3 %copy-start.66 = (f32[2,128,1,16]{3,2,1,0:T(1,128)}, f32[2,128,1,16]{3,2,1,0:T(1,128)S(1)}, u32[]{:S(2)}) copy-start(f32[2,128,1,16]{3,2,1,0:T(1,128)S(1)} %fusion.112) | copy-start | bytes 49156
  1330.4 343.7 %all-reduce.18.cloned.1.call-start = ((), (), s32[]{:S(2)}) async-start(), calls=%async_computation.10 | async-start | bytes 6291456 | tf_op jit(solution)/shard_map/psum | solution.py:311
  1335.4 559.4 %reduce-scatter.14.cloned.1.call-start = ((), (), s32[]{:S(2)}) async-start(), calls=%async_computation.15 | async-start | bytes 884736 | tf_op jit(solution)/shard_map/reduce_scatter | solution.py:470
  1340.7 555.6 %reduce-scatter.18.cloned.1.call-start = ((), (), s32[]{:S(2)}) async-start(), calls=%async_computation.18 | async-start | bytes 3932160
  1361.1 544.0 %reduce-scatter.12.cloned.1.call-start = ((), (), s32[]{:S(2)}) async-start(), calls=%async_computation.14 | async-start | bytes 7864320 | tf_op jit(solution)/shard_map/reduce_scatter | solution.py:478
  1391.4 160.5 %copy-start.76 = (f32[1536]{0:T(1024)S(1)}, f32[1536]{0:T(1024)}, u32[]{:S(2)}) copy-start(f32[1536]{0:T(1024)} %param.52) | copy-start | bytes 18436
  1391.4 160.5 %copy-start.78 = (f32[2,512]{1,0:T(2,128)S(1)}, f32[2,512]{1,0:T(2,128)}, u32[]{:S(2)}) copy-start(f32[2,512]{1,0:T(2,128)} %copy-done.77) | copy-start | bytes 12292
  1391.4 527.4 %reduce-scatter.16.cloned.1.call-start = ((), (), s32[]{:S(2)}) async-start(), calls=%async_computation.17 | async-start | bytes 442368
  1557.5 128.2 %copy-start.98 = (f32[2,512]{1,0:T(2,128)S(1)}, f32[2,512]{1,0:T(2,128)}, u32[]{:S(2)}) copy-start(f32[2,512]{1,0:T(2,128)} %copy-done.97) | copy-start | bytes 12292
  1557.5 128.2 %copy-start.19 = (bf16[2,512,1024]{2,1,0:T(8,128)(2,1)S(1)}, bf16[2,512,1024]{2,1,0:T(8,128)(2,1)}, u32[]{:S(2)}) copy-start(bf16[2,512,1024]{2,1,0:T(8,128)(2,1)} %copy-done.18) | copy-start | bytes 6291460
  1557.5 128.2 %copy-start.96 = (f32[768]{0:T(1024)S(1)}, f32[768]{0:T(1024)}, u32[]{:S(2)}) copy-start(f32[768]{0:T(1024)} %mul.622) | copy-start | bytes 9220
  1557.5 128.2 %copy-start.120 = (f32[2,512]{1,0:T(2,128)S(1)}, f32[2,512]{1,0:T(2,128)}, u32[]{:S(2)}) copy-start(f32[2,512]{1,0:T(2,128)} %copy-done.119) | copy-start | bytes 12292
  1557.5 128.2 %copy-start.142 = (f32[768]{0:T(1024)S(1)}, f32[768]{0:T(1024)}, u32[]{:S(2)}) copy-start(f32[768]{0:T(1024)} %param.50) | copy-start | bytes 9220
  1674.1 11.6 copy-start.25
  1674.1 11.6 copy-start.43
  1674.1 11.9 copy-start.139
  1702.3 23.7 copy-start.14
  1725.9 11.0 copy-start.37
  1726.0 10.9 copy-start.32
  1726.0 10.9 copy-start.55
  1759.0 16.1 copy-start.35
  1759.0 17.1 copy-start.8
  1759.0 17.1 copy-start.15
  1759.1 17.1 copy-start.114
  1759.1 23.6 copy-start.28
  1796.0 12.2 copy-start.104
  1816.3 17.3 copy-start.10
  1829.4 12.4 collective-permute-start.1
  1841.8 140.0 %all-reduce.28.cloned.1.call-start = ((), (), s32[]{:S(2)}) async-start(), calls=%async_computation.21 | async-start | bytes 12582912
  1867.6 161.0 %reduce-scatter.10.cloned.1.call-start = ((), (), s32[]{:S(2)}) async-start(), calls=%async_computation.13 | async-start | bytes 2654208 | tf_op jit(solution)/shard_map/reduce_scatter | solution.py:464
  1876.4 377.5 %all-reduce.22.cloned.1.call-start = ((), (), s32[]{:S(2)}) async-start(), calls=%async_computation.12 | async-start | bytes 12582912 | tf_op jit(solution)/shard_map/psum | solution.py:433
  1892.9 498.8 %all-reduce.26.cloned.1.call-start = ((), (), s32[]{:S(2)}) async-start(), calls=%async_computation.20 | async-start | bytes 3342336 | tf_op jit(solution)/shard_map/psum | solution.py:444
  1918.7 605.6 %all-reduce.24.cloned.1.call-start = ((), (), s32[]{:S(2)}) async-start(), calls=%async_computation.19 | async-start | bytes 192512 | tf_op jit(solution)/shard_map/psum | solution.py:444
  2258.3 275.2 %copy-start.1 = (bf16[2,512,1536]{2,1,0:T(8,128)(2,1)S(1)}, bf16[2,512,1536]{2,1,0:T(8,128)(2,1)}, u32[]{:S(2)}) copy-start(bf16[2,512,1536]{2,1,0:T(8,128)(2,1)} %param.55) | copy-start | bytes 9437188
  2391.7 141.3 %copy-start.74 = (f32[1536,16]{0,1:T(8,128)S(1)}, f32[1536,16]{0,1:T(8,128)}, u32[]{:S(2)}) copy-start(f32[1536,16]{0,1:T(8,128)} %get-tuple-element.593) | copy-start | bytes 294916
  (111 other events, 507.1 us)
Sparse Core Ops, SparseCore 0:
  68.9 11.8 all-gather.7
  135.0 227.4 all-reduce.15
  1330.5 221.2 all-reduce.19
  1554.1 120.0 all-reduce.17
  1677.1 33.9 reduce-scatter.13
  1714.0 43.9 reduce-scatter.17
  1761.0 70.1 reduce-scatter.11
  1841.9 32.1 reduce-scatter.15
  1877.4 104.3 all-reduce.27
  1986.0 42.5 reduce-scatter.9
  2031.0 222.8 all-reduce.21
  2260.3 131.3 all-reduce.25
  2400.4 123.8 all-reduce.23
where the time goes:
time: 2550 us; the launch traced here: 2540 us
  waiting for transfers between devices  1710 us (67%)
  local copies, waits for them, and re-layouts  351 us (14%)
  matrix products  278 us (11%)
  other arithmetic  139 us (5%)
  starting transfers between devices  26 us (1%)
    psum x2, waiting for transfers between devices, local(): lax.psum((grad_norm_one * first_head, grad_norm_two * first_head, grad_ro...  258 us
    psum x1, waiting for transfers between devices, local(): normed_one_grad = lax.psum(normed_one_grad, 'head')  223 us
    psum x1, waiting for transfers between devices, local(): mix_out, squares = lax.psum((partial_out, squares), 'head')  202 us
    all_to_all x1, waiting for transfers between devices, local(): lax.all_to_all(expert_out.reshape(buffer_shape), ('seq', 'head'), split_a...  181 us
    all_to_all x1, waiting for transfers between devices, local(): lax.all_to_all(send_grads, ('seq', 'head'), split_axis=1, concat_axis=1,...  180 us
    psum x1, waiting for transfers between devices, local(): normed_two_grad = lax.psum(normed_two_grad, 'head')  160 us
    all_to_all x1, waiting for transfers between devices, local(): lax.all_to_all(send_rows, ('seq', 'head'), split_axis=1, concat_axis=1, t...  144 us
    all_to_all x1, waiting for transfers between devices, local(): lax.all_to_all(expert_dx.reshape(buffer_shape), ('seq', 'head'), split_ax...  140 us
  transfers between devices with their start and end apart: 19, of which 12 were waited for; matrix products, arithmetic and copies ran while one was open for 22% of the time, Pallas kernels for 0%

commit v1 on v0

v1 whole, which is shorter than its diff:
```python
import jax
import jax.numpy as jnp
from jax import lax
from jax.sharding import PartitionSpec as P

BLOCK = 256


norm_eps = 1e-05
highest = lax.Precision.HIGHEST


def shifted(array, axis, by):
    count = lax.axis_size(axis)
    pairs = [(i, i + by) for i in range(count) if 0 <= i + by < count]
    return lax.ppermute(array, axis, pairs)


def prefix(part, axis, combine, identity):
    place = lax.axis_index(axis)
    gathered = jax.tree.map(lambda a: lax.all_gather(a, axis), part)
    state = jax.tree.map(lambda a, e: jnp.zeros_like(a) + jnp.asarray(e, a.dtype), part, identity)

    def one(lap, state):
        return combine(
            state, jax.tree.map(lambda a: lax.dynamic_index_in_dim(a, lap, 0, False), gathered)
        )

    return lax.fori_loop(0, place, one, state)


def prefix_2(array, axis, combine, identity):
    count, place = (lax.axis_size(axis), lax.axis_index(axis))
    everything = jax.tree.map(
        lambda part, kind: lax.all_gather(part.astype(kind), axis),
        array,
        jax.tree.map(lambda a: jnp.bfloat16 if a.dtype == jnp.float32 else a.dtype, array),
    )
    start = jax.tree.map(
        lambda part, zero: jnp.broadcast_to(jnp.asarray(zero, part.dtype), part.shape),
        array,
        identity,
    )

    def lap(k, before):
        at = count - 1 - k
        reached = at > place
        new = combine(
            before, jax.tree.map(lambda part, own: part[at].astype(own.dtype), everything, array)
        )
        return jax.tree.map(lambda a, b: jnp.where(reached, a, b), new, before)

    return lax.fori_loop(0, count, lap, start)


def silu_slope(argument):
    sigma = jax.nn.sigmoid(argument)
    return sigma * (1.0 + argument * (1.0 - sigma))


def running_sum(values):
    count = values.shape[2]
    lower = (jnp.arange(count)[:, None] >= jnp.arange(count)[None, :]).astype(jnp.float32)
    return jnp.einsum("ts,bksh->bkth", lower, values, precision=highest)


def sum_shares(part):
    count = lax.axis_size("head")
    batch_size, tokens, width = part.shape
    pieces = part.reshape(batch_size, count, tokens // count, width)
    got = lax.all_to_all(pieces, "head", split_axis=1, concat_axis=1, tiled=True)
    return jnp.sum(got.astype(jnp.float32), axis=1)


def gather_shares(share):
    count = lax.axis_size("head")
    batch_size, rows, width = share.shape
    copies = jnp.broadcast_to(share[:, None], (batch_size, count, rows, width))
    got = lax.all_to_all(copies, "head", split_axis=1, concat_axis=1, tiled=True)
    return got.reshape(batch_size, count * rows, width)


def around(array, by):
    count = lax.axis_size("seq")
    if by % count == 0:
        return array
    return lax.ppermute(array, "seq", [(i, (i + by) % count) for i in range(count)])


def spread_last(local_part, rank_index, part_count):
    local_width = local_part.shape[-1]
    full_array = jnp.zeros(local_part.shape[:-1] + (local_width * part_count,), jnp.float32)
    return lax.dynamic_update_slice_in_dim(
        full_array, local_part, rank_index * local_width, local_part.ndim - 1
    )


def block_states(scaled, map_b, within, block_total):
    tail_decay = jnp.exp(block_total[:, :, None, :] - within)
    return jnp.einsum("bksh,bkshp,bksn->bkhpn", tail_decay, scaled, map_b, precision=highest)


def leaving_state(states, before, block_total, device_total):
    weights_out = jnp.exp(device_total[:, None, :] - before - block_total)
    return jnp.einsum("bjh,bjhpn->bhpn", weights_out, states, precision=highest)


def scan_output(scaled, map_b, map_c, within, before, block_total, states, entering):
    block_len = within.shape[2]
    causal = (jnp.arange(block_len)[:, None] >= jnp.arange(block_len)[None, :])[
        None, None, :, :, None
    ]
    pair_gaps = within[:, :, :, None, :] - within[:, :, None, :, :]
    decays = jnp.where(causal, jnp.exp(jnp.where(causal, pair_gaps, 0.0)), 0.0)
    scores = jnp.einsum("bkqn,bksn->bkqs", map_c, map_b, precision=highest)
    inside = jnp.einsum("bkqsh,bkshp->bkqhp", decays * scores[..., None], scaled, precision=highest)
    after_block = before + block_total
    block_count = before.shape[1]
    earlier = (jnp.arange(block_count)[:, None] > jnp.arange(block_count)[None, :])[
        None, :, :, None
    ]
    gap_spans = before[:, :, None, :] - after_block[:, None, :, :]
    link_weights = jnp.where(earlier, jnp.exp(jnp.where(earlier, gap_spans, 0.0)), 0.0)
    starting = jnp.exp(before)[..., None, None] * entering[:, None] + jnp.einsum(
        "bkjh,bjhpn->bkhpn", link_weights, states, precision=highest
    )
    carried = (
        jnp.einsum("bkqn,bkhpn->bkqhp", map_c, starting, precision=highest)
        * jnp.exp(within)[..., None]
    )
    return inside + carried


def chain_forward(earlier, later):
    return (earlier[0] * later[0], later[0][..., None, None] * earlier[1] + later[1])


def chain_backward(earlier, later):
    return (earlier[0] * later[0], later[1] + later[0][..., None, None] * earlier[1])


def local(
    x_in,
    d_out,
    log_decay,
    routes,
    norm1_gain,
    w_in_zx,
    w_in_bc,
    w_in_dt,
    dt_bias,
    conv_x,
    conv_x_bias,
    conv_bc,
    conv_bc_bias,
    skip_d,
    gate_norm_gain,
    w_out,
    norm2_gain,
    router,
    w_expert_gu,
    w_expert_down,
    w_shared_gu,
    w_shared_down,
):
    f32, bf16 = jnp.float32, jnp.bfloat16
    batch_size, tokens, model_width = x_in.shape
    inner_dev = w_in_zx.shape[2]
    heads_dev = w_in_dt.shape[1]
    head_size = inner_dev // heads_dev
    state_size = w_in_bc.shape[1] // 2
    conv_taps = conv_x.shape[0]
    experts_dev = w_expert_gu.shape[0]
    expert_ff = w_expert_down.shape[1]
    head_count = lax.axis_size("head")
    seq_count = lax.axis_size("seq")
    head_rank = lax.axis_index("head")
    seq_rank = lax.axis_index("seq")
    inner_all = inner_dev * head_count
    experts_all = experts_dev * seq_count * head_count
    share_rows = tokens // head_count
    share_start = head_rank * share_rows
    blocks = tokens // BLOCK

    def blockify(array_in):
        return array_in.reshape((batch_size, blocks, BLOCK) + array_in.shape[2:])

    def own_share(array):
        return lax.dynamic_slice_in_dim(array, share_start, share_rows, 1)

    grads_in = [around(d_out, k) for k in range(seq_count)]
    input_wide = x_in.astype(f32)
    scale_one = lax.rsqrt(jnp.mean(input_wide * input_wide, axis=-1, keepdims=True) + norm_eps)
    normed_one = (input_wide * scale_one * norm1_gain).astype(bf16)
    proj_zx = jnp.einsum("btd,cdk->cbtk", normed_one, w_in_zx, preferred_element_type=f32)
    gate_z = proj_zx[0]
    bc_proj = jnp.einsum("btd,dn->btn", normed_one, w_in_bc, preferred_element_type=f32)
    step_raw = jnp.einsum("btd,dh->bth", normed_one, w_in_dt, preferred_element_type=f32)
    conv_in = jnp.concatenate([proj_zx[1], bc_proj], axis=-1).astype(bf16)
    edge_rows = shifted(conv_in[:, tokens - (conv_taps - 1) :, :], "seq", 1)
    padded = jnp.concatenate([edge_rows, conv_in], axis=1).astype(f32)
    conv_weight = jnp.concatenate([conv_x, conv_bc], axis=1)
    conv_bias = jnp.concatenate([conv_x_bias, conv_bc_bias])
    conv_pre = jnp.broadcast_to(conv_bias, padded[:, :tokens].shape)
    for offset in range(conv_taps):
        conv_pre = conv_pre + conv_weight[offset] * padded[:, offset : offset + tokens, :]
    conv_act = jax.nn.silu(conv_pre).astype(bf16)
    input_x = (
        conv_act[..., :inner_dev].astype(f32).reshape(batch_size, tokens, heads_dev, head_size)
    )
    input_b = conv_act[..., inner_dev : inner_dev + state_size].astype(f32)
    input_c = conv_act[..., inner_dev + state_size :].astype(f32)
    step_size = jax.nn.softplus(step_raw + dt_bias)
    within = running_sum(log_decay.reshape(batch_size, blocks, BLOCK, heads_dev))
    block_total = within[:, :, -1, :]
    before = [jnp.zeros_like(block_total[:, 0])]
    for k in range(blocks - 1):
        before.append(before[-1] + block_total[:, k])
    before = jnp.stack(before, axis=1)
    device_total = jnp.sum(block_total, axis=1)
    device_decay = jnp.exp(device_total)
    scaled = blockify(input_x * step_size[..., None])
    b_blocks = blockify(input_b)
    states = block_states(scaled, b_blocks, within, block_total)
    leaving = leaving_state(states, before, block_total, device_total)
    identity = (jnp.ones_like(device_decay), jnp.zeros_like(leaving))
    if seq_count == 2:
        entering = shifted(leaving, "seq", 1)
    else:
        _, entering = prefix((device_decay, leaving), "seq", chain_forward, identity)
    scanned = scan_output(
        scaled, b_blocks, blockify(input_c), within, before, block_total, states, entering
    )
    mixed = scanned.reshape(batch_size, tokens, heads_dev, head_size) + skip_d[:, None] * input_x
    mixed_flat = mixed.reshape(batch_size, tokens, inner_dev)
    z_silu = jax.nn.silu(gate_z)
    gated = mixed_flat * z_silu
    squares = jnp.sum(gated * gated, axis=-1)
    gated_low = (gated * gate_norm_gain).astype(bf16)
    partial_out = jnp.einsum("btk,kd->btd", gated_low, w_out, preferred_element_type=f32)

    mix_out = sum_shares(partial_out.astype(bf16))
    squares = sum_shares(squares[..., None])[..., 0]
    gate_scale = lax.rsqrt(squares / inner_all + norm_eps)[..., None]
    hidden = own_share(x_in).astype(f32) + mix_out * gate_scale
    scale_two = lax.rsqrt(jnp.mean(hidden * hidden, axis=-1, keepdims=True) + norm_eps)
    normed_share = (hidden * scale_two * norm2_gain).astype(bf16)
    normed_two = gather_shares(normed_share)

    expert_ids = jnp.arange(experts_all, dtype=jnp.int32)
    used = jnp.any(routes[..., None] == expert_ids, axis=2)
    logits = jnp.einsum("btd,de->bte", normed_two, router, preferred_element_type=f32)
    top = jnp.max(jnp.where(used, logits, -jnp.inf), axis=-1, keepdims=True)
    powers = jnp.where(used, jnp.exp(jnp.where(used, logits - top, 0.0)), 0.0)
    gates = powers / jnp.sum(powers, axis=-1, keepdims=True)
    gates_across = jnp.transpose(gates, (0, 2, 1))

    shared_gu = jnp.einsum("btd,cdf->cbtf", normed_two, w_shared_gu, preferred_element_type=f32)
    shared_act = (jax.nn.silu(shared_gu[0]) * shared_gu[1]).astype(bf16)
    shared_out = jnp.einsum("btf,fd->btd", shared_act, w_shared_down, preferred_element_type=f32)
    shared_push = jnp.einsum("btd,fd->btf", d_out, w_shared_down, preferred_element_type=f32)
    shared_gu_grad = jnp.stack(
        [
            shared_push * shared_gu[1] * silu_slope(shared_gu[0]),
            shared_push * jax.nn.silu(shared_gu[0]),
        ]
    ).astype(bf16)
    shared_dx = jnp.einsum(
        "cbtf,cdf->btd", shared_gu_grad, w_shared_gu, preferred_element_type=f32
    )
    grad_shared_down = jnp.einsum(
        "btf,btd->df", shared_act, d_out, preferred_element_type=f32
    )
    grad_shared_gu = jnp.einsum(
        "btd,cbtf->dcf", normed_two, shared_gu_grad, preferred_element_type=f32
    )

    first_expert = (seq_rank * head_count + head_rank) * experts_dev
    ffn_out, ffn_dx = shared_out, shared_dx
    pushes = []
    grad_expert_gu = grad_expert_down = 0.0
    for k in range(seq_count):
        rows = around(normed_two, k)
        grads = grads_in[k]
        weights = lax.dynamic_slice_in_dim(around(gates_across, k), first_expert, experts_dev, 1)
        weights = jnp.transpose(weights, (1, 0, 2))[..., None]
        expert_gu = jnp.einsum("btd,edf->ebtf", rows, w_expert_gu, preferred_element_type=f32)
        gate_part, up_part = expert_gu[..., :expert_ff], expert_gu[..., expert_ff:]
        expert_act = (jax.nn.silu(gate_part) * up_part).astype(bf16)
        expert_out = jnp.einsum(
            "ebtf,efd->ebtd", expert_act, w_expert_down, preferred_element_type=f32
        ).astype(bf16)
        push = (weights * grads.astype(f32)).astype(bf16)
        act_push = jnp.einsum("ebtd,efd->ebtf", push, w_expert_down, preferred_element_type=f32)
        gu_grad = jnp.concatenate(
            [act_push * up_part * silu_slope(gate_part), act_push * jax.nn.silu(gate_part)],
            axis=-1,
        ).astype(bf16)
        expert_dx = jnp.einsum(
            "ebtf,edf->ebtd", gu_grad, w_expert_gu, preferred_element_type=f32
        ).astype(bf16)
        gate_push = jnp.sum(grads.astype(f32) * expert_out.astype(f32), axis=-1)
        routed = jnp.sum(weights * expert_out.astype(f32), axis=0)
        routed_dx = jnp.sum(expert_dx.astype(f32), axis=0)
        grad_expert_down = grad_expert_down + jnp.einsum(
            "ebtf,ebtd->edf", expert_act, push, preferred_element_type=f32
        )
        grad_expert_gu = grad_expert_gu + jnp.einsum(
            "btd,ebtf->edf", rows, gu_grad, preferred_element_type=f32
        )
        if k == 0:
            ffn_out, ffn_dx = ffn_out + routed, ffn_dx + routed_dx
        else:
            ffn_out = ffn_out + around(routed.astype(bf16), -k).astype(f32)
            ffn_dx = ffn_dx + around(routed_dx.astype(bf16), -k).astype(f32)
        pushes.append(around(gate_push, -k))

    pushes = jnp.stack(pushes + pushes)
    pushes = lax.dynamic_slice_in_dim(pushes, (seq_count - seq_rank) % seq_count, seq_count, 0)
    pushes = pushes.reshape(seq_count * experts_dev * batch_size, head_count, share_rows)
    pushes = lax.all_to_all(pushes, "head", split_axis=1, concat_axis=1, tiled=True)
    pushes = pushes.reshape(seq_count, experts_dev, batch_size, head_count, share_rows)
    pushes = jnp.transpose(pushes, (2, 4, 0, 3, 1)).reshape(batch_size, share_rows, experts_all)
    gates_share = own_share(gates)
    logit_grad = gates_share * (pushes - jnp.sum(gates_share * pushes, axis=-1, keepdims=True))
    grad_router = jnp.einsum(
        "brd,bre->de",
        normed_share,
        logit_grad,
        precision=highest,
        preferred_element_type=f32,
    )

    ffn_share = sum_shares(ffn_out.astype(bf16))
    layer_out = gather_shares((hidden + ffn_share).astype(bf16))

    normed_two_grad = sum_shares(ffn_dx.astype(bf16)) + jnp.einsum(
        "bre,de->brd", logit_grad, router.astype(f32), precision=highest
    )
    gained_two = normed_two_grad * norm2_gain
    hidden_grad = own_share(d_out).astype(f32) + scale_two * (
        gained_two
        - hidden * scale_two * scale_two * jnp.mean(gained_two * hidden, axis=-1, keepdims=True)
    )
    grad_norm_two = jnp.sum(normed_two_grad * hidden * scale_two, axis=(0, 1))
    scale_push = jnp.sum(hidden_grad * mix_out, axis=-1)
    squares_grad = -0.5 * scale_push * gate_scale[..., 0] ** 3 / inner_all
    squares_grad = gather_shares(squares_grad[..., None])
    out_push = gather_shares((hidden_grad * gate_scale).astype(bf16))

    gated_grad_low = jnp.einsum("btd,kd->btk", out_push, w_out, preferred_element_type=f32)
    grad_w_out = jnp.einsum("btk,btd->dk", gated_low, out_push, preferred_element_type=f32)
    gated_grad = gated_grad_low * gate_norm_gain + 2.0 * gated * squares_grad
    grad_gate_gain = jnp.sum(gated_grad_low * gated, axis=(0, 1))
    mixed_grad = (gated_grad * z_silu).reshape(batch_size, tokens, heads_dev, head_size)
    z_grad = (gated_grad * mixed_flat * silu_slope(gate_z)).astype(bf16)
    grad_skip = jnp.sum(mixed_grad * input_x, axis=(0, 1, 3))
    device_cum = jnp.exp(before[:, :, None, :] + within).reshape(batch_size, tokens, heads_dev)
    entering_grad = jnp.einsum(
        "bth,bthp,btn->bhpn", device_cum, mixed_grad, input_c, precision=highest
    )
    if seq_count == 2:
        leaving_grad = shifted(entering_grad.astype(bf16), "seq", -1).astype(f32)
    else:
        _, leaving_grad = prefix_2((device_decay, entering_grad), "seq", chain_backward, identity)

    def mixer_local(x_value, b_value, c_value, step_value):
        scaled_value = blockify(x_value * step_value[..., None])
        b_value_blocks = blockify(b_value)
        state_value = block_states(scaled_value, b_value_blocks, within, block_total)
        outputs = scan_output(
            scaled_value,
            b_value_blocks,
            blockify(c_value),
            within,
            before,
            block_total,
            state_value,
            entering,
        )
        return (
            outputs.reshape(x_value.shape),
            leaving_state(state_value, before, block_total, device_total),
        )

    _, pull_back = jax.vjp(mixer_local, input_x, input_b, input_c, step_size)
    x_grad, b_grad, c_grad, step_grad = pull_back((mixed_grad, leaving_grad))
    x_grad = x_grad + skip_d[:, None] * mixed_grad
    raw_grad = step_grad * jax.nn.sigmoid(step_raw + dt_bias)
    grad_dt_bias = jnp.sum(raw_grad, axis=(0, 1))
    act_grad = jnp.concatenate(
        [x_grad.reshape(batch_size, tokens, inner_dev), b_grad, c_grad], axis=-1
    )
    pre_grad = act_grad * silu_slope(conv_pre)
    grad_conv = jnp.stack(
        [
            jnp.sum(pre_grad * padded[:, offset : offset + tokens, :], axis=(0, 1))
            for offset in range(conv_taps)
        ]
    )
    grad_conv_bias = jnp.sum(pre_grad, axis=(0, 1))
    next_rows = shifted(pre_grad[:, : conv_taps - 1, :], "seq", -1)
    extended = jnp.concatenate([pre_grad, next_rows], axis=1)
    in_grad = sum(
        conv_weight[conv_taps - 1 - k] * extended[:, k : k + tokens, :] for k in range(conv_taps)
    )
    x_in_grad = in_grad[..., :inner_dev].astype(bf16)
    bc_grad = in_grad[..., inner_dev:]
    zx_grad = jnp.concatenate([z_grad, x_in_grad], axis=-1)
    grad_w_zx = jnp.einsum("btd,btk->dk", normed_one, zx_grad, preferred_element_type=f32)
    grad_w_bc = jnp.einsum(
        "btd,btn->dn", normed_one, bc_grad.astype(bf16), preferred_element_type=f32
    )
    grad_w_dt = jnp.einsum(
        "btd,bth->dh", normed_one, raw_grad.astype(bf16), preferred_element_type=f32
    )
    normed_one_grad = jnp.einsum(
        "btk,dk->btd", z_grad, w_in_zx[0], preferred_element_type=f32
    ) + jnp.einsum("btk,dk->btd", x_in_grad, w_in_zx[1], preferred_element_type=f32)
    small_grad = jnp.concatenate([bc_grad, raw_grad], axis=-1).astype(bf16)
    small_weight = jnp.concatenate([w_in_bc, w_in_dt], axis=-1)
    normed_one_grad = normed_one_grad + jnp.einsum(
        "btn,dn->btd", small_grad, small_weight, preferred_element_type=f32
    )
    normed_one_grad = sum_shares(normed_one_grad.astype(bf16))
    gained_one = normed_one_grad * norm1_gain
    input_share, scale_share = own_share(input_wide), own_share(scale_one)
    input_grad = hidden_grad + scale_share * (
        gained_one
        - input_share
        * scale_share
        * scale_share
        * jnp.mean(gained_one * input_share, axis=-1, keepdims=True)
    )
    grad_norm_one = jnp.sum(normed_one_grad * input_share * scale_share, axis=(0, 1))
    d_input = gather_shares(input_grad.astype(bf16))
    small_sums = lax.psum(
        (
            grad_norm_one,
            grad_norm_two,
            grad_router,
            grad_w_bc,
            grad_conv[:, inner_dev:],
            grad_conv_bias[inner_dev:],
            spread_last(grad_conv[:, :inner_dev], head_rank, head_count),
            spread_last(grad_conv_bias[:inner_dev], head_rank, head_count),
            spread_last(grad_gate_gain, head_rank, head_count),
            spread_last(grad_dt_bias, head_rank, head_count),
            spread_last(grad_skip, head_rank, head_count),
        ),
        ("dp", "seq", "head"),
    )

    def scattered(array, axes):
        return lax.psum_scatter(
            array.astype(bf16), axes, scatter_dimension=0, tiled=True
        ).astype(f32)

    grad_zx = scattered(grad_w_zx, ("dp", "seq"))
    grad_zx = jnp.stack([grad_zx[:, :inner_dev], grad_zx[:, inner_dev:]])
    grad_out = scattered(grad_w_out, ("dp", "seq")).T
    grad_gu = scattered(grad_shared_gu.reshape(model_width, -1), ("dp", "seq"))
    grad_gu = jnp.transpose(grad_gu.reshape(grad_gu.shape[0], 2, -1), (1, 0, 2))
    grad_down = scattered(grad_shared_down, ("dp", "seq")).T
    grad_dt = scattered(grad_w_dt, ("dp", "seq"))
    expert_gu_sum = lax.psum_scatter(
        grad_expert_gu.astype(bf16), "dp", scatter_dimension=1, tiled=True
    ).astype(f32)
    expert_down_sum = lax.psum_scatter(
        grad_expert_down.astype(bf16), "dp", scatter_dimension=1, tiled=True
    ).astype(f32)
    expert_down_sum = jnp.transpose(expert_down_sum, (0, 2, 1))
    return (
        layer_out,
        d_input,
        small_sums[0],
        grad_zx,
        small_sums[3],
        grad_dt,
        small_sums[9],
        small_sums[6],
        small_sums[7],
        small_sums[4],
        small_sums[5],
        small_sums[10],
        small_sums[8],
        grad_out,
        small_sums[1],
        small_sums[2],
        expert_gu_sum,
        expert_down_sum,
        grad_gu,
        grad_down,
    )


def solution(mesh):
    placed = (
        P("dp", "seq", None),
        P("dp", "seq", None),
        P("dp", "seq", "head"),
        P("dp", "seq", None),
        P(),
        P(None, None, "head"),
        P(),
        P(None, "head"),
        P("head"),
        P(None, "head"),
        P("head"),
        P(),
        P(),
        P("head"),
        P("head"),
        P("head", None),
        P(),
        P(),
        P(("seq", "head"), None, None),
        P(("seq", "head"), None, None),
        P(None, None, "head"),
        P("head", None),
    )
    return jax.shard_map(
        local,
        mesh=mesh,
        in_specs=placed,
        out_specs=(
            P("dp", "seq", None),
            P("dp", "seq", None),
            P(),
            P(None, ("dp", "seq"), "head"),
            P(),
            P(("dp", "seq"), "head"),
            P(),
            P(),
            P(),
            P(),
            P(),
            P(),
            P(),
            P("head", ("dp", "seq")),
            P(),
            P(),
            P(("seq", "head"), "dp", None),
            P(("seq", "head"), None, "dp"),
            P(None, ("dp", "seq"), "head"),
            P("head", ("dp", "seq")),
        ),
        check_vma=False,
    )
```

time: 2550 us -> 1260 us (0.49)
  waiting for transfers between devices: 1710 us -> 634 us
  local copies, waits for them, and re-layouts: 351 us -> 161 us
  other arithmetic: 139 us -> 78.8 us
  starting transfers between devices: 26 us -> 55.9 us
    psum x6 -> x2, waiting for transfers between devices: 960 us -> 231 us  [local(): lax.psum((grad_norm_one, grad_norm_two, grad_router, grad_w_bc, grad_conv...]
    all_to_all x4 -> x10, waiting for transfers between devices: 645 us -> 397 us  [the longest x5 225 us: sum_shares(): lax.all_to_all(pieces, 'head', split_axis=1, concat_axis=1, tiled=True)]
    gather x4 -> x0, local copies, waits for them, and re-layouts: 73.6 us -> none  [the longest x1 22.3 us: local(): send_grads = grads_pad[filled].reshape(buffer_shape)]
    unnamed x16 -> x12, waiting for transfers between devices: 61.8 us -> 0.19 us
    reduce_scatter x3 -> x4, waiting for transfers between devices: 42.4 us -> 0.03 us  [the longest x3 0.02 us: scattered(): lax.psum_scatter(array.astype(bf16), axes, scatter_dimension=0, tiled=True)]
    convert_element_type x5 -> x1, local copies, waits for them, and re-layouts: 37.1 us -> 3.54 us  [local(): conv_act[..., :inner_dev].astype(f32)]
    scatter-add x4 -> x0, local copies, waits for them, and re-layouts: 28.8 us -> none  [the longest x3 27.3 us: local(): padded_grad.at[:, offset:offset + tokens, :]]
    all_to_all x4 -> x10, starting transfers between devices: 20.7 us -> 47.8 us  [the longest x5 25.5 us: sum_shares(): lax.all_to_all(pieces, 'head', split_axis=1, concat_axis=1, tiled=True)]
  transfers between devices with their start and end apart: 19 -> 29, of which waited for: 12 -> 12; matrix products, arithmetic and copies ran while one was open for 22% -> 33% of each run, Pallas kernels for 0% -> 0%
where the time goes in v1:
time: 1260 us; the launch traced here: 1250 us
  waiting for transfers between devices  634 us (50%)
  matrix products  299 us (24%)
  local copies, waits for them, and re-layouts  161 us (13%)
  other arithmetic  78.8 us (6%)
  starting transfers between devices  55.9 us (4%)
  between operations  18 us (1%)
    psum x2, waiting for transfers between devices, local(): lax.psum((grad_norm_one, grad_norm_two, grad_router, grad_w_bc, grad_conv...  231 us
    all_to_all x5, waiting for transfers between devices, sum_shares(): lax.all_to_all(pieces, 'head', split_axis=1, concat_axis=1, tiled=True)  225 us
    all_to_all x4, waiting for transfers between devices, gather_shares(): lax.all_to_all(copies, 'head', split_axis=1, concat_axis=1, tiled=True)  171 us
    unnamed x325, local copies, waits for them, and re-layouts  72.9 us
    dot_general x3, matrix products, scan_output(): jnp.einsum('bkqsh,bkshp->bkqhp', decays * scores[..., None], scaled, prec...  40.9 us
    dot_general x2, matrix products, local(): jnp.einsum('ebtf,edf->ebtd', gu_grad, w_expert_gu, preferred_element_type...  26.3 us
    all_to_all x5, starting transfers between devices, sum_shares(): lax.all_to_all(pieces, 'head', split_axis=1, concat_axis=1, tiled=True)  25.5 us
  transfers between devices with their start and end apart: 29, of which 12 were waited for; matrix products, arithmetic and copies ran while one was open for 33% of the time, Pallas kernels for 0%

profile of v1, /device:TPU:0, one launch (start us, length us, event | category | flops | bytes accessed | tf_op | source)
XLA Modules:
  0.0 1254.0 jit_solution(1488618585968664656)
XLA Ops:
  11.0 7.2 fusion.84
  47.2 5.2 reshape.254
  56.2 5.8 fusion.139
  63.7 6.3 fusion.141
  70.1 14.2 %fusion.10 = f32[2,2,12,64,256]{4,3,2,1,0:T(8,128)S(1)} fusion(f32[2,2,256,256]{3,2,1,0:T(8,128)S(1)} %fusion.218, f32[2,2,256,12]{2,3,1,0:T(8,128)S(1)} %copy-done.63, pred[256,256]{1,0:T(8,128)(4,1)S(1)} %copy-done.79, f32[2,2,256,12,64]{2,1,4,3,0:T(2,128)S(1)} %copy-done.4, f32[2,2,256,12]{2,3,1,0:T(8,128)S(1)} %copy-done.58), kind=kOutput, calls=%fused_computation.19 | convolution fusion | flops 2429288448 | bytes 7503872 | tf_op jit(solution)/shard_map/bkqsh,bkshp->bkqhp/dot_general | solution.py:116
  86.5 4.1 copy.483
  90.6 5.5 reshape.258
  99.7 6.7 multiply_reduce_fusion.8
  106.4 5.7 all-to-all-start.1
  112.0 5.2 convolution_convert_fusion.2
  119.1 5.1 all-to-all-start
  124.3 69.8 %all-to-all-done = bf16[2,4,128,1536]{3,2,0,1:T(8,128)(2,1)} async-done(((bf16[2,4,128,1536]{3,2,0,1:T(8,128)(2,1)}), bf16[2,4,128,1536]{3,2,0,1:T(8,128)(2,1)}, u32[]{:S(2)}, u32[]{:S(2)}) %all-to-all-start) | async-done | bytes 3145760 | tf_op jit(solution)/shard_map/all_to_all | solution.py:71
  203.0 4.8 all-to-all-start.2
  207.9 5.4 convert_element_type.199
  213.9 5.4 convert_element_type.203
  219.3 58.8 %all-to-all-done.2 = bf16[2,4,128,1536]{3,2,0,1:T(8,128)(2,1)} async-done(((bf16[2,4,128,1536]{3,2,0,1:T(8,128)(2,1)}), bf16[2,4,128,1536]{3,2,0,1:T(8,128)(2,1)}, u32[]{:S(2)}, u32[]{:S(2)}) %all-to-all-start.2) | async-done | bytes 3145760 | tf_op jit(solution)/shard_map/all_to_all | solution.py:79
  282.0 11.4 fusion.56
  293.5 8.9 multiply_convert_fusion.6
  302.4 8.0 fusion.2
  310.5 12.0 fusion.59
  322.5 9.4 multiply_convert_fusion.4
  331.9 12.8 %convert_reduce_fusion.3 = bf16[2,512,1536]{2,1,0:T(8,128)(2,1)} fusion(bf16[2,1536,1024]{2,1,0:T(8,128)(2,1)} %param.40, bf16[2,2,512,512]{3,2,0,1:T(8,128)(2,1)} %get-tuple-element.201, bf16[2,2,512,512]{3,2,0,1:T(8,128)(2,1)} %get-tuple-element.200), kind=kOutput, calls=%fused_computation.41 | convolution fusion | flops 6455558144 | bytes 13631488 | tf_op jit(solution)/shard_map/ebtf,edf->ebtd/dot_general | solution.py:299
  344.7 4.6 convolution_bitcast_fusion.5
  349.3 13.6 %convert_reduce_fusion = f32[2,512,1536]{2,1,0:T(8,128)} fusion(bf16[2,1536,1024]{2,1,0:T(8,128)(2,1)} %param.40, bf16[2,2,512,512]{3,2,0,1:T(8,128)(2,1)} %get-tuple-element.203, bf16[2,2,512,512]{3,2,0,1:T(8,128)(2,1)} %get-tuple-element.202), kind=kOutput, calls=%fused_computation.14 | convolution fusion | flops 6458703872 | bytes 16777216 | tf_op jit(solution)/shard_map/ebtf,edf->ebtd/dot_general | solution.py:299
  362.9 7.1 fusion.4
  376.8 6.3 fusion.18
  385.0 5.0 all-to-all-start.5
  390.0 5.9 collective-permute-done.4
  395.9 4.3 add_convert_fusion.1
  402.1 58.5 %all-to-all-done.5 = bf16[2,4,128,1536]{3,2,0,1:T(8,128)(2,1)S(1)} async-done(((bf16[2,4,128,1536]{3,2,0,1:T(8,128)(2,1)}), bf16[2,4,128,1536]{3,2,0,1:T(8,128)(2,1)S(1)}, u32[]{:S(2)}, u32[]{:S(2)}) %all-to-all-start.5) | async-done | bytes 3145760 | tf_op jit(solution)/shard_map/all_to_all | solution.py:71
  462.2 4.7 all-to-all-start.3
  477.9 8.6 fusion.103
  486.5 8.1 fusion.12
  500.3 36.8 %all-to-all-done.3 = bf16[2,4,128,1536]{3,2,0,1:T(8,128)(2,1)} async-done(((bf16[2,4,128,1536]{3,2,0,1:T(8,128)(2,1)}), bf16[2,4,128,1536]{3,2,0,1:T(8,128)(2,1)}, u32[]{:S(2)}, u32[]{:S(2)}) %all-to-all-start.3) | async-done | bytes 3145760 | tf_op jit(solution)/shard_map/all_to_all | solution.py:71
  543.7 8.0 all_to_all.55
  553.7 4.8 all-to-all-start.7
  565.8 8.9 fusion.208
  574.7 11.0 fusion.43
  585.8 16.5 %copy.592 = bf16[2,1536,1024]{2,0,1:T(2,128)(2,1)} copy(bf16[2,1536,1024]{1,2,0:T(8,128)(2,1)} %fusion.43) | data formatting | bytes 12582912
  602.3 8.0 copy.601
  610.3 17.0 %all-to-all-done.7 = bf16[2,4,128,1536]{3,2,0,1:T(8,128)(2,1)} async-done(((bf16[2,4,128,1536]{3,2,0,1:T(8,128)(2,1)}), bf16[2,4,128,1536]{3,2,0,1:T(8,128)(2,1)}, u32[]{:S(2)}, u32[]{:S(2)}) %all-to-all-start.7) | async-done | bytes 3145760 | tf_op jit(solution)/shard_map/all_to_all | solution.py:79
  630.2 10.0 multiply_reduce_fusion.6
  653.0 15.8 %fusion.6 = f32[2,2,256,256]{3,2,1,0:T(8,128)S(1)} fusion(f32[2,2,256,12]{2,3,1,0:T(8,128)S(1)} %copy-done.64, pred[256,256]{1,0:T(8,128)(4,1)S(1)} %copy-done.80, f32[2,2,12,64,256]{4,1,3,2,0:T(2,128)} %bitcast.398, f32[2,2,256,12,64]{2,1,4,3,0:T(2,128)S(1)} %copy-done.5, f32[2,2,256,12]{2,3,1,0:T(8,128)S(1)} %copy-done.59), kind=kOutput, calls=%fused_computation.12 | convolution fusion | flops 2432172032 | bytes 7503872 | tf_op jit(solution)/shard_map/transpose(jvp(bkqsh,bkshp->bkqhp))/dot_general | solution.py:116
  671.2 6.4 fusion.93
  677.7 10.9 fusion.8
  690.4 6.3 fusion.132
  696.8 6.7 add_bitcast_fusion
  708.1 4.1 copy.517
  712.2 5.9 reshape.270
  721.6 6.7 fusion.133
  728.4 4.5 multiply_add_fusion.1
  742.8 7.5 fusion.47
  751.8 4.4 fusion.91
  760.0 5.0 all-to-all-start.9
  767.0 7.0 bitcast_convert_fusion.1
  776.6 60.2 %all-to-all-done.9 = bf16[2,4,128,1536]{3,2,0,1:T(8,128)(2,1)} async-done(((bf16[2,4,128,1536]{3,2,0,1:T(8,128)(2,1)}), bf16[2,4,128,1536]{3,2,0,1:T(8,128)(2,1)}, u32[]{:S(2)}, u32[]{:S(2)}) %all-to-all-start.9) | async-done | bytes 3145760 | tf_op jit(solution)/shard_map/all_to_all | solution.py:71
  839.9 4.7 all-to-all-start.4
  844.6 9.2 bitcast_convert_fusion
  859.9 56.0 %all-to-all-done.4 = bf16[2,4,128,1536]{3,2,0,1:T(8,128)(2,1)} async-done(((bf16[2,4,128,1536]{3,2,0,1:T(8,128)(2,1)}), bf16[2,4,128,1536]{3,2,0,1:T(8,128)(2,1)}, u32[]{:S(2)}, u32[]{:S(2)}) %all-to-all-start.4) | async-done | bytes 3145760 | tf_op jit(solution)/shard_map/all_to_all | solution.py:79
  918.9 4.8 all-to-all-start.10
  939.1 4.9 copy.593
  962.6 39.7 %all-to-all-done.10 = bf16[2,4,128,1536]{3,2,0,1:T(8,128)(2,1)} async-done(((bf16[2,4,128,1536]{3,2,0,1:T(8,128)(2,1)}), bf16[2,4,128,1536]{3,2,0,1:T(8,128)(2,1)}, u32[]{:S(2)}, u32[]{:S(2)}) %all-to-all-start.10) | async-done | bytes 3145760 | tf_op jit(solution)/shard_map/all_to_all | solution.py:79
  1006.2 98.5 %all-reduce.8.cloned.1.call-done = (f32[1536,256]{1,0:T(8,128)}, f32[1536,16]{0,1:T(8,128)}) async-done(((f32[1536,256]{1,0:T(8,128)}, f32[1536,16]{0,1:T(8,128)}), (f32[1536,256]{1,0:T(8,128)}, f32[1536,16]{0,1:T(8,128)})) %all-reduce.8.cloned.1.call-update) | async-done | bytes 1671184 | tf_op jit(solution)/shard_map/psum | solution.py:437
  1104.7 132.3 %all-reduce.6.cloned.1.call-done = (f32[1536]{0:T(1024)}, f32[48]{0:T(128)}, f32[4,3072]{1,0:T(4,128)}, f32[3072]{0:T(1024)}, f32[4,256]{1,0:T(4,128)}, /*index=...) async-done(((f32[1536]{0:T(1024)}, f32[48]{0:T(128)}, f32[4,3072]{1,0:T(4,128)}, f32[3072]{0:T(1024)}, f32[4,256]{1,0:T(4,128)}, /*index=5*/f32[256]{0:T(256)}, ...) | async-done | bytes 91536 | tf_op jit(solution)/shard_map/psum | solution.py:437
  (510 shorter events, 209.2 us)
Async XLA Ops:
  8.0 285.4 %copy-start = (bf16[2,512,1536]{2,1,0:T(8,128)(2,1)S(1)}, bf16[2,512,1536]{2,1,0:T(8,128)(2,1)}, u32[]{:S(2)}) copy-start(bf16[2,512,1536]{2,1,0:T(8,128)(2,1)} %param.41) | copy-start | bytes 9437188
  11.0 14.8 %copy-start.117 = (f32[2,512]{1,0:T(2,128)}, f32[2,512]{1,0:T(2,128)S(1)}, u32[]{:S(2)}) copy-start(f32[2,512]{1,0:T(2,128)S(1)} %add_rsqrt_fusion) | copy-start | bytes 12292
  22.2 11.8 collective-permute-start
  30.3 22.1 %copy-start.49 = (f32[2,2,256,12]{2,3,1,0:T(8,128)}, f32[2,2,256,12]{2,3,1,0:T(8,128)S(1)}, u32[]{:S(2)}) copy-start(f32[2,2,256,12]{2,3,1,0:T(8,128)S(1)} %get-tuple-element.217) | copy-start | bytes 147460
  30.3 54.0 %copy-start.51 = (f32[2,2,256,12]{2,3,1,0:T(8,128)}, f32[2,2,256,12]{2,3,1,0:T(8,128)S(1)}, u32[]{:S(2)}) copy-start(f32[2,2,256,12]{2,3,1,0:T(8,128)S(1)} %get-tuple-element.216) | copy-start | bytes 147460
  31.2 32.5 %copy-start.75 = (f32[2,2,12]{1,2,0:T(8,128)}, f32[2,2,12]{1,2,0:T(8,128)S(1)}, u32[]{:S(2)}) copy-start(f32[2,2,12]{1,2,0:T(8,128)S(1)} %copy.478) | copy-start | bytes 580
  41.8 21.5 %copy-start.32 = (bf16[2,512,128]{2,1,0:T(8,128)(2,1)}, bf16[2,512,128]{2,1,0:T(8,128)(2,1)S(1)}, u32[]{:S(2)}) copy-start(bf16[2,512,128]{2,1,0:T(8,128)(2,1)S(1)} %get-tuple-element.210) | copy-start | bytes 786436
  56.2 13.9 %copy-start.4 = (f32[2,2,256,12,64]{2,1,4,3,0:T(2,128)S(1)}, f32[2,2,256,12,64]{2,1,4,3,0:T(2,128)}, u32[]{:S(2)}) copy-start(f32[2,2,256,12,64]{2,1,4,3,0:T(2,128)} %reshape.254) | copy-start | bytes 9437188
  56.2 13.9 %copy-start.58 = (f32[2,2,256,12]{2,3,1,0:T(8,128)S(1)}, f32[2,2,256,12]{2,3,1,0:T(8,128)}, u32[]{:S(2)}) copy-start(f32[2,2,256,12]{2,3,1,0:T(8,128)} %copy.475) | copy-start | bytes 147460
  56.2 13.9 %copy-start.63 = (f32[2,2,256,12]{2,3,1,0:T(8,128)S(1)}, f32[2,2,256,12]{2,3,1,0:T(8,128)}, u32[]{:S(2)}) copy-start(f32[2,2,256,12]{2,3,1,0:T(8,128)} %copy-done.62) | copy-start | bytes 147460
  56.2 13.9 %copy-start.79 = (pred[256,256]{1,0:T(8,128)(4,1)S(1)}, pred[256,256]{1,0:T(8,128)(4,1)}, u32[]{:S(2)}) copy-start(pred[256,256]{1,0:T(8,128)(4,1)} %iota_compare_fusion.1) | copy-start | bytes 196612
  62.0 22.3 %collective-permute-start.1 = (f32[2,12,64,128]{3,2,1,0:T(8,128)S(1)}, f32[2,12,64,128]{3,2,1,0:T(8,128)S(1)}, u32[]{:S(2)}, u32[]{:S(2)}) collective-permute-start(f32[2,12,64,128]{3,2,1,0:T(8,128)S(1)} %bitcast.458), channel_id=1, source_target_pairs={{0,4},{1,5},{2,6},{3,7},{8,12},{9,13},{10,14},{11,15},{16,20},{17,... | collective-permute-start | bytes 2359304 | tf_op jit(solution)/shard_map/ppermute | solution.py:16
  63.7 20.6 %copy-start.53 = (f32[2,2,256,256]{3,2,1,0:T(8,128)}, f32[2,2,256,256]{3,2,1,0:T(8,128)S(1)}, u32[]{:S(2)}) copy-start(f32[2,2,256,256]{3,2,1,0:T(8,128)S(1)} %fusion.218) | copy-start | bytes 3145732
  70.1 14.2 %copy-start.18 = (f32[2,12,64,128,2]{3,4,2,1,0:T(2,128)}, f32[2,12,64,128,2]{3,4,2,1,0:T(2,128)S(1)}, u32[]{:S(2)}) copy-start(f32[2,12,64,128,2]{3,4,2,1,0:T(2,128)S(1)} %fusion.141) | copy-start | bytes 4718596
  70.1 14.2 %copy-start.106 = (f32[2,2,12]{2,1,0:T(2,128)S(1)}, f32[2,2,12]{2,1,0:T(2,128)}, u32[]{:S(2)}) copy-start(f32[2,2,12]{2,1,0:T(2,128)} %get-tuple-element.225) | copy-start | bytes 580
  99.7 12.3 copy-start.135
  106.4 12.8 %all-to-all-start.1 = ((f32[2,4,128,1]{2,0,3,1:T(2,128)}), f32[2,4,128,1]{2,0,3,1:T(2,128)S(1)}, u32[]{:S(2)}, u32[]{:S(2)}) async-start(f32[2,4,128,1]{2,0,3,1:T(2,128)} %bitcast.29), calls=%async_computation.1 | async-start | bytes 8192 | tf_op jit(solution)/shard_map/all_to_all | solution.py:71
  119.1 74.9 %all-to-all-start = ((bf16[2,4,128,1536]{3,2,0,1:T(8,128)(2,1)}), bf16[2,4,128,1536]{3,2,0,1:T(8,128)(2,1)}, u32[]{:S(2)}, u32[]{:S(2)}) async-start(bf16[2,4,128,1536]{3,2,0,1:T(8,128)(2,1)} %copy.485), calls=%async_computation | async-start | bytes 6291456 | tf_op jit(solution)/shard_map/all_to_all | solution.py:71
  124.2 74.5 %copy-start.112 = (f32[2,128]{1,0:T(2,128)}, f32[2,128]{1,0:T(2,128)S(1)}, u32[]{:S(2)}) copy-start(f32[2,128]{1,0:T(2,128)S(1)} %reduce_sum.310) | copy-start | bytes 3076
  203.0 75.1 %all-to-all-start.2 = ((bf16[2,4,128,1536]{3,2,0,1:T(8,128)(2,1)}), bf16[2,4,128,1536]{3,2,0,1:T(8,128)(2,1)}, u32[]{:S(2)}, u32[]{:S(2)}) async-start(bf16[2,4,128,1536]{3,2,0,1:T(8,128)(2,1)} %broadcast_in_dim.81), calls=%async_computation.2 | async-start | bytes 6291456 | tf_op jit(solution)/shard_map/all_to_all | solution.py:79
  207.8 6.1 collective-permute-start.5
  219.3 60.9 %copy-start.71 = (bf16[1536,16]{0,1:T(8,128)(2,1)S(1)}, bf16[1536,16]{0,1:T(8,128)(2,1)}, u32[]{:S(2)}) copy-start(bf16[1536,16]{0,1:T(8,128)(2,1)} %param.39) | copy-start | bytes 147460
  280.1 64.6 %copy-start.25 = (bf16[2,4,128,1536]{3,2,1,0:T(8,128)(2,1)}, bf16[2,4,128,1536]{3,2,1,0:T(8,128)(2,1)S(1)}, u32[]{:S(2)}) copy-start(bf16[2,4,128,1536]{3,2,1,0:T(8,128)(2,1)S(1)} %copy.486) | copy-start | bytes 9437188
  280.1 30.4 %collective-permute-start.3 = (bf16[2,512,1536]{2,1,0:T(8,128)(2,1)S(1)}, bf16[2,512,1536]{2,1,0:T(8,128)(2,1)}, u32[]{:S(2)}, u32[]{:S(2)}) collective-permute-start(bf16[2,512,1536]{2,1,0:T(8,128)(2,1)S(1)} %bitcast.405), channel_id=1, source_target_pairs={{0,4},{4,0},{1,5},{5,1},{2,6},{6,2},{3,7},{7,3},{8,12},{12,8},{9,1... | collective-permute-start | bytes 9437192 | tf_op jit(solution)/shard_map/ppermute | solution.py:87
  280.2 13.3 %slice-start.2 = ((s8[6291456]{0:T(1024)(128)(4,1)}), s8[4194304]{0:T(1024)(128)(4,1)S(1)}, s32[]{:S(2)}) async-start(s8[6291456]{0:T(1024)(128)(4,1)} %bitcast.393), calls=%async_computation.29 | async-start | bytes 8388608
  281.4 29.0 %collective-permute-start.2 = (f32[2,16,512]{2,1,0:T(8,128)S(1)}, f32[2,16,512]{2,1,0:T(8,128)S(1)}, u32[]{:S(2)}, u32[]{:S(2)}) collective-permute-start(f32[2,16,512]{2,1,0:T(8,128)S(1)} %fusion.168), channel_id=1, source_target_pairs={{0,4},{4,0},{1,5},{5,1},{2,6},{6,2},{3,7},{7,3},{8,12},{12,8},{9,1... | collective-permute-start | bytes 196616 | tf_op jit(solution)/shard_map/ppermute | solution.py:87
  293.4 204.0 %copy-start.70 = (f32[2,512,16]{1,2,0:T(8,128)}, f32[2,512,16]{1,2,0:T(8,128)S(1)}, u32[]{:S(2)}) copy-start(f32[2,512,16]{1,2,0:T(8,128)S(1)} %fusion.175) | copy-start | bytes 196612
  310.4 12.0 slice-start.4
  310.5 12.0 slice-start.5
  344.7 32.1 %collective-permute-start.6 = (bf16[2,512,1536]{2,1,0:T(8,128)(2,1)}, bf16[2,512,1536]{2,1,0:T(8,128)(2,1)}, u32[]{:S(2)}, u32[]{:S(2)}) collective-permute-start(bf16[2,512,1536]{2,1,0:T(8,128)(2,1)} %convert_reduce_fusion.3), channel_id=1, source_target_pairs={{0,4},{4,0},{1,5},{5,1},{2,6},{6,2},{3,7},{7,3},{8,12},{12,8},{9,1... | collective-permute-start | bytes 9437192 | tf_op jit(solution)/shard_map/ppermute | solution.py:87
  349.3 13.6 %copy-start.47 = (bf16[2,2,512,512]{3,2,0,1:T(8,128)(2,1)S(1)}, bf16[2,2,512,512]{3,2,0,1:T(8,128)(2,1)}, u32[]{:S(2)}) copy-start(bf16[2,2,512,512]{3,2,0,1:T(8,128)(2,1)} %get-tuple-element.204) | copy-start | bytes 6291460
  370.0 2.9 collective-permute-start.7
  373.5 11.4 all-to-all-start.6
  385.0 75.6 %all-to-all-start.5 = ((bf16[2,4,128,1536]{3,2,0,1:T(8,128)(2,1)}), bf16[2,4,128,1536]{3,2,0,1:T(8,128)(2,1)S(1)}, u32[]{:S(2)}, u32[]{:S(2)}) async-start(bf16[2,4,128,1536]{3,2,0,1:T(8,128)(2,1)} %copy.504), calls=%async_computation.5 | async-start | bytes 6291456 | tf_op jit(solution)/shard_map/all_to_all | solution.py:71
  390.0 5.9 collective-permute-start.4
  462.2 74.9 %all-to-all-start.3 = ((bf16[2,4,128,1536]{3,2,0,1:T(8,128)(2,1)}), bf16[2,4,128,1536]{3,2,0,1:T(8,128)(2,1)}, u32[]{:S(2)}, u32[]{:S(2)}) async-start(bf16[2,4,128,1536]{3,2,0,1:T(8,128)(2,1)} %copy.495), calls=%async_computation.3 | async-start | bytes 6291456 | tf_op jit(solution)/shard_map/all_to_all | solution.py:71
  466.9 456.9 %reduce-scatter.26.cloned.1.call-start = ((), (), s32[]{:S(2)}) async-start(), calls=%async_computation.24 | async-start | bytes 884736
  473.4 452.3 %reduce-scatter.20.cloned.1.call-start = ((), (), s32[]{:S(2)}) async-start(), calls=%async_computation.21 | async-start | bytes 1769472 | tf_op jit(solution)/shard_map/reduce_scatter | solution.py:455
  477.9 451.8 %reduce-scatter.18.cloned.1.call-start = ((), (), s32[]{:S(2)}) async-start(), calls=%async_computation.20 | async-start | bytes 3932160 | tf_op jit(solution)/shard_map/reduce_scatter | solution.py:469
  553.7 73.7 %all-to-all-start.7 = ((bf16[2,4,128,1536]{3,2,0,1:T(8,128)(2,1)}), bf16[2,4,128,1536]{3,2,0,1:T(8,128)(2,1)}, u32[]{:S(2)}, u32[]{:S(2)}) async-start(bf16[2,4,128,1536]{3,2,0,1:T(8,128)(2,1)} %broadcast_in_dim.86), calls=%async_computation.7 | async-start | bytes 6291456 | tf_op jit(solution)/shard_map/all_to_all | solution.py:79
  558.5 376.8 %reduce-scatter.24.cloned.1.call-start = ((), (), s32[]{:S(2)}) async-start(), calls=%async_computation.23 | async-start | bytes 7864320
  610.3 19.3 %copy-start.13 = (bf16[2,512,1024]{2,1,0:T(8,128)(2,1)S(1)}, bf16[2,512,1024]{2,1,0:T(8,128)(2,1)}, u32[]{:S(2)}) copy-start(bf16[2,512,1024]{2,1,0:T(8,128)(2,1)} %copy-done.12) | copy-start | bytes 6291460
  610.3 19.3 %copy-start.88 = (f32[768]{0:T(1024)S(1)}, f32[768]{0:T(1024)}, u32[]{:S(2)}) copy-start(f32[768]{0:T(1024)} %mul.586) | copy-start | bytes 9220
  610.3 19.3 %copy-start.136 = (f32[768]{0:T(1024)S(1)}, f32[768]{0:T(1024)}, u32[]{:S(2)}) copy-start(f32[768]{0:T(1024)} %param.36) | copy-start | bytes 9220
  651.6 45.1 %collective-permute-start.8 = (bf16[2,12,64,128]{3,2,1,0:T(8,128)(2,1)S(1)}, bf16[2,12,64,128]{3,2,1,0:T(8,128)(2,1)S(1)}, u32[]{:S(2)}, u32[]{:S(2)}) collective-permute-start(bf16[2,12,64,128]{3,2,1,0:T(8,128)(2,1)S(1)} %fusion.123), channel_id=1, source_target_pairs={{4,0},{5,1},{6,2},{7,3},{12,8},{13,9},{14,10},{15,11},{20,16},{21,... | collective-permute-start | bytes 1179656 | tf_op jit(solution)/shard_map/ppermute | solution.py:16
  652.9 15.9 %copy-start.33 = (bf16[2,512,128]{2,1,0:T(8,128)(2,1)S(1)}, bf16[2,512,128]{2,1,0:T(8,128)(2,1)}, u32[]{:S(2)}) copy-start(bf16[2,512,128]{2,1,0:T(8,128)(2,1)} %copy-done.32) | copy-start | bytes 786436
  652.9 16.5 %copy-start.6 = (f32[2,2,256,12,64]{2,1,4,3,0:T(2,128)S(1)}, f32[2,2,256,12,64]{2,1,4,3,0:T(2,128)}, u32[]{:S(2)}) copy-start(f32[2,2,256,12,64]{2,1,4,3,0:T(2,128)} %reshape_reshape.3) | copy-start | bytes 9437188
  652.9 16.5 %copy-start.35 = (bf16[2,512,128]{2,1,0:T(8,128)(2,1)S(1)}, bf16[2,512,128]{2,1,0:T(8,128)(2,1)}, u32[]{:S(2)}) copy-start(bf16[2,512,128]{2,1,0:T(8,128)(2,1)} %get-tuple-element.211) | copy-start | bytes 786436
  652.9 16.5 %copy-start.52 = (f32[2,2,256,12]{2,3,1,0:T(8,128)S(1)}, f32[2,2,256,12]{2,3,1,0:T(8,128)}, u32[]{:S(2)}) copy-start(f32[2,2,256,12]{2,3,1,0:T(8,128)} %copy-done.51) | copy-start | bytes 147460
  677.7 12.7 %copy-start.19 = (f32[2,12,64,128,2]{3,4,2,1,0:T(2,128)S(1)}, f32[2,12,64,128,2]{3,4,2,1,0:T(2,128)}, u32[]{:S(2)}) copy-start(f32[2,12,64,128,2]{3,4,2,1,0:T(2,128)} %copy-done.18) | copy-start | bytes 4718596
  677.7 12.7 %copy-start.42 = (f32[2,12,64,128]{3,2,1,0:T(8,128)S(1)}, f32[2,12,64,128]{3,2,1,0:T(8,128)}, u32[]{:S(2)}) copy-start(f32[2,12,64,128]{3,2,1,0:T(8,128)} %copy-done.41) | copy-start | bytes 2359300
  677.7 12.7 %copy-start.107 = (f32[2,2,12]{2,1,0:T(2,128)S(1)}, f32[2,2,12]{2,1,0:T(2,128)}, u32[]{:S(2)}) copy-start(f32[2,2,12]{2,1,0:T(2,128)} %get-tuple-element.225) | copy-start | bytes 580
  737.5 5.2 collective-permute-start.9
  742.8 13.4 %slice-start.6 = ((s8[6291456]{0:T(1024)(128)(4,1)}), s8[4194304]{0:T(1024)(128)(4,1)S(1)}, s32[]{:S(2)}) async-start(s8[6291456]{0:T(1024)(128)(4,1)} %bitcast.423), calls=%async_computation.33 | async-start | bytes 8388608
  760.0 76.8 %all-to-all-start.9 = ((bf16[2,4,128,1536]{3,2,0,1:T(8,128)(2,1)}), bf16[2,4,128,1536]{3,2,0,1:T(8,128)(2,1)}, u32[]{:S(2)}, u32[]{:S(2)}) async-start(bf16[2,4,128,1536]{3,2,0,1:T(8,128)(2,1)} %copy.530), calls=%async_computation.9 | async-start | bytes 6291456 | tf_op jit(solution)/shard_map/all_to_all | solution.py:71
  764.9 191.8 %reduce-scatter.22.cloned.1.call-start = ((), (), s32[]{:S(2)}) async-start(), calls=%async_computation.22 | async-start | bytes 442368
  766.9 191.4 %reduce-scatter.16.cloned.1.call-start = ((), (), s32[]{:S(2)}) async-start(), calls=%async_computation.19 | async-start | bytes 2654208 | tf_op jit(solution)/shard_map/reduce_scatter | solution.py:455
  839.9 76.0 %all-to-all-start.4 = ((bf16[2,4,128,1536]{3,2,0,1:T(8,128)(2,1)}), bf16[2,4,128,1536]{3,2,0,1:T(8,128)(2,1)}, u32[]{:S(2)}, u32[]{:S(2)}) async-start(bf16[2,4,128,1536]{3,2,0,1:T(8,128)(2,1)} %broadcast_in_dim.85), calls=%async_computation.4 | async-start | bytes 6291456 | tf_op jit(solution)/shard_map/all_to_all | solution.py:79
  844.6 115.6 %reduce-scatter.14.cloned.1.call-start = ((), (), s32[]{:S(2)}) async-start(), calls=%async_computation.18 | async-start | bytes 5308416 | tf_op jit(solution)/shard_map/reduce_scatter | solution.py:455
  918.9 83.4 %all-to-all-start.10 = ((bf16[2,4,128,1536]{3,2,0,1:T(8,128)(2,1)}), bf16[2,4,128,1536]{3,2,0,1:T(8,128)(2,1)}, u32[]{:S(2)}, u32[]{:S(2)}) async-start(bf16[2,4,128,1536]{3,2,0,1:T(8,128)(2,1)} %broadcast_in_dim.88), calls=%async_computation.10 | async-start | bytes 6291456 | tf_op jit(solution)/shard_map/all_to_all | solution.py:79
  923.8 181.0 %all-reduce.8.cloned.1.call-start = ((), (), s32[]{:S(2)}) async-start(), calls=%async_computation.26 | async-start | bytes 3342336 | tf_op jit(solution)/shard_map/psum | solution.py:437
  955.1 281.9 %all-reduce.6.cloned.1.call-start = ((), (), s32[]{:S(2)}) async-start(), calls=%async_computation.25 | async-start | bytes 192512 | tf_op jit(solution)/shard_map/psum | solution.py:437
  1002.3 244.1 %copy-start.1 = (bf16[2,512,1536]{2,1,0:T(8,128)(2,1)S(1)}, bf16[2,512,1536]{2,1,0:T(8,128)(2,1)}, u32[]{:S(2)}) copy-start(bf16[2,512,1536]{2,1,0:T(8,128)(2,1)} %param.41) | copy-start | bytes 9437188
  1104.7 141.0 %copy-start.73 = (f32[1536,16]{0,1:T(8,128)S(1)}, f32[1536,16]{0,1:T(8,128)}, u32[]{:S(2)}) copy-start(f32[1536,16]{0,1:T(8,128)} %get-tuple-element.247) | copy-start | bytes 294916
  (115 other events, 555.6 us)
Sparse Core Ops, SparseCore 0:
  473.5 36.3 reduce-scatter.25
  513.2 38.4 reduce-scatter.19
  554.7 43.9 reduce-scatter.17
  610.4 71.4 reduce-scatter.23
  769.1 35.6 reduce-scatter.21
  808.0 42.4 reduce-scatter.15
  854.3 54.8 reduce-scatter.13
Sparse Core Ops, SparseCore 1:
  955.2 149.5 all-reduce.7
  1113.3 123.7 all-reduce.5

commit v2 on v1

v2 whole, which is shorter than its diff:
```python
import jax
import jax.numpy as jnp
from jax import lax
from jax.experimental import pallas as pl
from jax.experimental.pallas import tpu as pltpu
from jax.sharding import PartitionSpec as P

BLOCK = 256
ROWS = 256

bf16, f32 = jnp.bfloat16, jnp.float32
norm_eps = 1e-05
highest = lax.Precision.HIGHEST


def dot_nn(a, b):
    return lax.dot_general(a, b, (((1,), (0,)), ((), ())), preferred_element_type=f32)


def dot_nt(a, b):
    return lax.dot_general(a, b, (((1,), (1,)), ((), ())), preferred_element_type=f32)


def dot_tn(a, b):
    return lax.dot_general(a, b, (((0,), (0,)), ((), ())), preferred_element_type=f32)


def lower_mask(count, flip=False):
    rows = lax.broadcasted_iota(jnp.int32, (count, count), 0)
    columns = lax.broadcasted_iota(jnp.int32, (count, count), 1)
    return columns >= rows if flip else rows >= columns


def sum_down(values):
    lower = lower_mask(values.shape[0]).astype(f32)
    return jnp.dot(lower, values, precision=highest, preferred_element_type=f32)


def sum_right(values):
    upper = lower_mask(values.shape[1], True).astype(f32)
    return jnp.dot(values, upper, precision=highest, preferred_element_type=f32)


def first_half(rows, width=128):
    return lax.broadcasted_iota(jnp.int32, (rows, width), 1) < width // 2


def per_channel(values, head_size):
    rows, heads = values.shape
    left = first_half(rows, 2 * head_size)
    return jnp.concatenate(
        [jnp.where(left, values[:, h : h + 1], values[:, h + 1 : h + 2]) for h in range(0, heads, 2)],
        axis=1,
    )


def joined(ref):
    return ref[...].reshape(-1, ref.shape[-1])


def softplus(v):
    return jnp.maximum(v, 0.0) + jnp.log1p(jnp.exp(-jnp.abs(v)))


def scan_kernel(cin, edge, taps, raw, bias, decay, decay_t, act_ref, y_ref, start_ref, leave_ref, buf, prev, state):
    heads = decay.shape[1]
    block = BLOCK
    inner = y_ref.shape[2]
    size = state.shape[0]
    head_size = inner // heads
    pair = 2 * head_size
    count = 4

    @pl.when(pl.program_id(1) == 0)
    def _():
        prev[...] = edge[...]
        state[...] = jnp.zeros_like(state)

    buf[0:8, :] = prev[...]
    buf[8 : 8 + block, :] = joined(cin).astype(f32)
    pre = taps[4:5, :] + sum(taps[k : k + 1, :] * buf[5 + k : 5 + k + block, :] for k in range(count))
    prev[...] = buf[block : block + 8, :]
    act = (pre * jax.nn.sigmoid(pre)).astype(bf16)
    act_ref[...] = act.reshape(act_ref.shape)
    map_b, map_c = act[:, inner : inner + size], act[:, inner + size :]
    step = softplus(joined(raw) + bias[...])
    scaled = act[:, :inner].astype(f32) * per_channel(step, head_size)
    within, across = sum_down(decay[...]), sum_right(decay_t[...])
    grown = per_channel(jnp.exp(within), head_size)
    tail = per_channel(jnp.exp(within[block - 1 :, :] - within), head_size)
    before = state[...]
    start_ref[...] = before
    carried = grown * dot_nn(map_c, before.astype(bf16))
    scores = dot_nt(map_c, map_b)
    causal = lower_mask(block)
    low = scaled.astype(bf16)
    left = first_half(block, pair)
    for h in range(0, heads, 2):
        columns = slice(h * head_size, h * head_size + pair)
        halves = []
        for a in (h, h + 1):
            gap = jnp.where(causal, within[:, a : a + 1] - across[a : a + 1, :], -1e30)
            halves.append(dot_nn((jnp.exp(gap) * scores).astype(bf16), low[:, columns]))
        y_pair = carried[:, columns] + jnp.where(left, halves[0], halves[1])
        y_ref[:, :, columns] = y_pair.reshape(y_ref.shape[:2] + (pair,))
    after = grown[block - 1 :, :] * before + dot_tn(map_b, (scaled * tail).astype(bf16))
    state[...] = after
    leave_ref[...] = after


def gate_kernel(y, act_in, z, decay, lead, entering, skip, gain, w_out, mixed_ref, low_ref, squares_ref, out_ref):
    heads = decay.shape[1]
    inner = y.shape[2]
    size = entering.shape[0]
    grown = per_channel(jnp.exp(sum_down(decay[...])), inner // heads) * lead[...]
    act = joined(act_in)
    map_c = act[:, inner + size :]
    carried = grown * dot_nn(map_c, entering[...].astype(bf16))
    mixed = joined(y) + carried + skip[...] * act[:, :inner].astype(f32)
    gate = joined(z)
    gated = mixed * (gate * jax.nn.sigmoid(gate))
    mixed_ref[...] = mixed.astype(bf16).reshape(mixed_ref.shape)
    low = (gated * gain[...]).astype(bf16)
    low_ref[...] = low.reshape(low_ref.shape)
    squares = jnp.sum(gated * gated, axis=1, keepdims=True)
    squares_ref[...] = jnp.broadcast_to(squares, (BLOCK, squares_ref.shape[2])).reshape(squares_ref.shape)
    out_ref[...] = dot_nn(low, w_out[...]).astype(bf16).reshape(out_ref.shape)


def gate_back_kernel(push, w_out, mixed_in, z, act_in, decay, lead, slope_in, gain, dy_ref, dz_ref, enter_ref, sums_ref):
    heads = decay.shape[1]
    inner = mixed_in.shape[2]
    size = enter_ref.shape[0]
    mixed = joined(mixed_in).astype(f32)
    act = joined(act_in)
    gate = joined(z)
    sigma = jax.nn.sigmoid(gate)
    silu = gate * sigma
    gated = mixed * silu
    low_grad = dot_nt(joined(push), w_out[...])
    gated_grad = low_grad * gain[...] + 2.0 * gated * joined(slope_in)
    dy = gated_grad * silu
    dy_ref[...] = dy.astype(bf16).reshape(dy_ref.shape)
    dz_ref[...] = (gated_grad * mixed * (sigma + silu * (1.0 - sigma))).astype(bf16).reshape(dz_ref.shape)
    grown = per_channel(jnp.exp(sum_down(decay[...])), inner // heads) * lead[...]
    part = dot_tn(act[:, inner + size :], (grown * dy).astype(bf16))
    gain_sum = jnp.sum(low_grad * gated, axis=0, keepdims=True)
    skip_sum = jnp.sum(dy * act[:, :inner].astype(f32), axis=0, keepdims=True)

    @pl.when(pl.program_id(1) == 0)
    def _():
        enter_ref[...] = jnp.zeros_like(enter_ref)

    @pl.when((pl.program_id(0) == 0) & (pl.program_id(1) == 0))
    def _():
        sums_ref[...] = jnp.zeros_like(sums_ref)

    enter_ref[...] += part
    sums_ref[0:1, :] += gain_sum
    sums_ref[1:2, :] += skip_sum


def scan_back_kernel(cin, cin_before, edge, taps, raw, bias, decay, decay_t, act_in, dy_in, start, lead, entering, leave_grad, skip,
                     in_ref, head_ref, tail_ref, taps_ref, buf, nextp, state_grad):
    heads = decay.shape[1]
    block = BLOCK
    inner = dy_in.shape[2]
    width = taps.shape[1]
    size = state_grad.shape[0]
    head_size = inner // heads
    pair = 2 * head_size
    count = 4
    turn, turns = pl.program_id(1), pl.num_programs(1)

    @pl.when(turn == 0)
    def _():
        state_grad[...] = leave_grad[...]
        nextp[...] = jnp.zeros_like(nextp)

    @pl.when((pl.program_id(0) == 0) & (turn == 0))
    def _():
        taps_ref[...] = jnp.zeros_like(taps_ref)

    buf[8 : 8 + block, :] = joined(cin).astype(f32)

    @pl.when(turn == turns - 1)
    def _():
        buf[0:8, :] = edge[...]

    @pl.when(turn < turns - 1)
    def _():
        buf[0:8, :] = cin_before[...].astype(f32)[8:, :]

    pre = taps[4:5, :] + sum(taps[k : k + 1, :] * buf[5 + k : 5 + k + block, :] for k in range(count))
    sigma = jax.nn.sigmoid(pre)
    slope = sigma * (1.0 + pre * (1.0 - sigma))
    act = joined(act_in)
    map_b, map_c = act[:, inner : inner + size], act[:, inner + size :]
    value = act[:, :inner].astype(f32)
    raw_full = joined(raw) + bias[...]
    step = per_channel(softplus(raw_full), head_size)
    scaled = value * step
    low = scaled.astype(bf16)
    dy_low = joined(dy_in)
    dy = dy_low.astype(f32)
    within, across = sum_down(decay[...]), sum_right(decay_t[...])
    grown = per_channel(jnp.exp(within), head_size)
    tail = per_channel(jnp.exp(within[block - 1 :, :] - within), head_size)
    before = (start[...] + lead[...] * entering[...]).astype(bf16)
    after_grad = state_grad[...]
    after_low = after_grad.astype(bf16)
    grown_dy = (grown * dy).astype(bf16)
    c_grad = dot_nt(grown_dy, before)
    b_grad = dot_nt((tail * scaled).astype(bf16), after_low)
    scaled_grad = tail * dot_nn(map_b, after_low)
    state_grad[...] = grown[block - 1 :, :] * after_grad + dot_tn(map_c, grown_dy)
    scores_t = dot_nt(map_b, map_c)
    causal_t = lower_mask(block, True)
    left = first_half(block, pair)
    zero = jnp.zeros((block, pair), bf16)
    scores_grad_t = jnp.zeros((block, block), f32)
    parts = []
    for h in range(0, heads, 2):
        columns = slice(h * head_size, h * head_size + pair)
        dy_pair, low_pair = dy_low[:, columns], low[:, columns]
        halves = []
        for a in (h, h + 1):
            gap = jnp.where(causal_t, across[a : a + 1, :] - within[:, a : a + 1], -1e30)
            fade = jnp.exp(gap)
            own = jnp.where(left, low_pair, zero) if a == h else jnp.where(left, zero, low_pair)
            scores_grad_t = scores_grad_t + fade * dot_nt(own, dy_pair)
            halves.append(dot_nn((fade * scores_t).astype(bf16), dy_pair))
        parts.append(jnp.where(left, halves[0], halves[1]))
    scaled_grad = scaled_grad + jnp.concatenate(parts, axis=1)
    scores_low = scores_grad_t.astype(bf16)
    b_grad = b_grad + dot_nn(scores_low, map_c)
    c_grad = c_grad + dot_tn(scores_low, map_b)
    x_grad = scaled_grad * step + skip[...] * dy
    lanes = in_ref.shape[2] - width
    rows = lax.broadcasted_iota(jnp.int32, (inner, lanes), 0)
    columns = lax.broadcasted_iota(jnp.int32, (inner, lanes), 1)
    member = ((rows >= columns * head_size) & (rows < (columns + 1) * head_size)).astype(bf16)
    step_grad = dot_nn((scaled_grad * value).astype(bf16), member)
    raw_grad = step_grad[:, :heads] * jax.nn.sigmoid(raw_full)
    taps_ref[5:6, :heads] += jnp.sum(raw_grad, axis=0, keepdims=True)
    raw_grad = jnp.concatenate([raw_grad, jnp.zeros((block, lanes - heads), f32)], axis=1)
    in_ref[:, :, width:] = raw_grad.astype(bf16).reshape(in_ref.shape[:2] + (lanes,))
    pre_grad = jnp.concatenate([x_grad, b_grad, c_grad], axis=1) * slope
    for k in range(count):
        taps_ref[k : k + 1, :] += jnp.sum(pre_grad * buf[5 + k : 5 + k + block, :], axis=0, keepdims=True)
    taps_ref[4:5, :] += jnp.sum(pre_grad, axis=0, keepdims=True)
    buf[0:block, :] = pre_grad
    buf[block : block + 8, :] = nextp[...]
    nextp[...] = buf[0:8, :]
    head_ref[...] = buf[0:8, :]
    in_grad = sum(taps[k : k + 1, :] * buf[3 - k : 3 - k + block, :] for k in range(count))
    in_ref[:, :, :width] = in_grad.astype(bf16).reshape(in_ref.shape[:2] + (width,))

    @pl.when(turn == 0)
    def _():
        tail_ref[...] = in_grad[block - 8 :, :]


def params():
    return pltpu.CompilerParams(vmem_limit_bytes=56 * 2**20)


def cost(flops, moved, powers):
    return pl.CostEstimate(flops=int(flops), bytes_accessed=int(moved), transcendentals=int(powers))


def rows_of(share, width, flip=0):
    per = BLOCK // share
    if flip:
        return pl.BlockSpec((per, None, share, width), lambda b, k: (flip - 1 - k, b, 0, 0))
    return pl.BlockSpec((per, None, share, width), lambda b, k: (k, b, 0, 0))


def each(height, width):
    return pl.BlockSpec((None, height, width), lambda b, k: (b, 0, 0))


def only(height, width):
    return pl.BlockSpec((height, width), lambda b, k: (0, 0))


def at_block(height, width, flip=0):
    if flip:
        return pl.BlockSpec((None, None, height, width), lambda b, k: (b, flip - 1 - k, 0, 0))
    return pl.BlockSpec((None, None, height, width), lambda b, k: (b, k, 0, 0))


def in_order(width, flip=0):
    if flip:
        return pl.BlockSpec((None, BLOCK, width), lambda b, k: (b, flip - 1 - k, 0))
    return pl.BlockSpec((None, BLOCK, width), lambda b, k: (b, k, 0))


def made(*shape, kind=bf16):
    return jax.ShapeDtypeStruct(shape, kind)


def scan_forward(cin, edge, taps, raw, bias, decay, decay_t, inner, size):
    shares, batch, share, width = cin.shape
    heads = raw.shape[3]
    tokens = shares * share
    blocks = tokens // BLOCK
    return pl.pallas_call(
        scan_kernel,
        grid=(batch, blocks),
        in_specs=[
            rows_of(share, width),
            each(8, width),
            only(8, width),
            rows_of(share, heads),
            only(1, heads),
            in_order(heads),
            pl.BlockSpec((None, heads, BLOCK), lambda b, k: (b, 0, k)),
        ],
        out_specs=[rows_of(share, width), rows_of(share, inner), at_block(size, inner), each(size, inner)],
        out_shape=[
            made(shares, batch, share, width),
            made(shares, batch, share, inner, kind=f32),
            made(batch, blocks, size, inner, kind=f32),
            made(batch, size, inner, kind=f32),
        ],
        scratch_shapes=[
            pltpu.VMEM((BLOCK + 8, width), f32),
            pltpu.VMEM((8, width), f32),
            pltpu.VMEM((size, inner), f32),
        ],
        compiler_params=params(),
        cost_estimate=cost(
            batch * tokens * inner * (4 * BLOCK + 4 * size), 10 * batch * tokens * inner, batch * tokens * heads * BLOCK
        ),
    )(cin, edge, taps, raw, bias, decay, decay_t)


def gate_forward(y, act, z, decay, lead, entering, skip, gain, w_out):
    shares, batch, share, inner = y.shape
    width, heads, size = act.shape[3], decay.shape[2], entering.shape[1]
    model = w_out.shape[1]
    tokens = shares * share
    return pl.pallas_call(
        gate_kernel,
        grid=(batch, tokens // BLOCK),
        in_specs=[
            rows_of(share, inner),
            rows_of(share, width),
            rows_of(share, inner),
            in_order(heads),
            at_block(1, inner),
            each(size, inner),
            only(1, inner),
            only(1, inner),
            only(inner, model),
        ],
        out_specs=[rows_of(share, inner), rows_of(share, inner), rows_of(share, 128), rows_of(share, model)],
        out_shape=[
            made(shares, batch, share, inner),
            made(shares, batch, share, inner),
            made(shares, batch, share, 128, kind=f32),
            made(shares, batch, share, model),
        ],
        compiler_params=params(),
        cost_estimate=cost(
            2 * batch * tokens * inner * (model + size), batch * tokens * inner * 18, batch * tokens * inner
        ),
    )(y, act, z, decay, lead, entering, skip, gain, w_out)


def gate_backward(push, w_out, mixed, z, act, decay, lead, slope, gain):
    shares, batch, share, inner = mixed.shape
    width, heads, model = act.shape[3], decay.shape[2], w_out.shape[1]
    size = (width - inner) // 2
    tokens = shares * share
    return pl.pallas_call(
        gate_back_kernel,
        grid=(batch, tokens // BLOCK),
        in_specs=[
            rows_of(share, model),
            only(inner, model),
            rows_of(share, inner),
            rows_of(share, inner),
            rows_of(share, width),
            in_order(heads),
            at_block(1, inner),
            rows_of(share, 1),
            only(1, inner),
        ],
        out_specs=[rows_of(share, inner), rows_of(share, inner), each(size, inner), only(8, inner)],
        out_shape=[
            made(shares, batch, share, inner),
            made(shares, batch, share, inner),
            made(batch, size, inner, kind=f32),
            made(8, inner, kind=f32),
        ],
        compiler_params=params(),
        cost_estimate=cost(
            2 * batch * tokens * inner * (model + size), batch * tokens * inner * 18, batch * tokens * inner
        ),
    )(push, w_out, mixed, z, act, decay, lead, slope, gain)


def scan_backward(cin, edge, taps, raw, bias, decay, decay_t, act, dy, start, lead, entering, leave_grad, skip):
    shares, batch, share, width = cin.shape
    heads, inner, size = raw.shape[3], dy.shape[3], entering.shape[1]
    tokens = shares * share
    blocks = tokens // BLOCK
    per = BLOCK // share
    return pl.pallas_call(
        scan_back_kernel,
        grid=(batch, blocks),
        in_specs=[
            rows_of(share, width, blocks),
            pl.BlockSpec(
                (None, None, 16, width),
                lambda b, k: (jnp.maximum((blocks - 1 - k) * per - 1, 0), b, share // 16 - 1, 0),
            ),
            each(8, width),
            only(8, width),
            rows_of(share, heads, blocks),
            only(1, heads),
            in_order(heads, blocks),
            pl.BlockSpec((None, heads, BLOCK), lambda b, k: (b, 0, blocks - 1 - k)),
            rows_of(share, width, blocks),
            rows_of(share, inner, blocks),
            at_block(size, inner, blocks),
            at_block(1, inner, blocks),
            each(size, inner),
            each(size, inner),
            only(1, inner),
        ],
        out_specs=[rows_of(share, width + 128, blocks), each(8, width), each(8, width), only(8, width)],
        out_shape=[
            made(shares, batch, share, width + 128),
            made(batch, 8, width, kind=f32),
            made(batch, 8, width, kind=f32),
            made(8, width, kind=f32),
        ],
        scratch_shapes=[
            pltpu.VMEM((BLOCK + 8, width), f32),
            pltpu.VMEM((8, width), f32),
            pltpu.VMEM((size, inner), f32),
        ],
        compiler_params=params(),
        cost_estimate=cost(
            batch * tokens * inner * (8 * BLOCK + 10 * size), 15 * batch * tokens * inner, batch * tokens * heads * BLOCK
        ),
    )(cin, cin, edge, taps, raw, bias, decay, decay_t, act, dy, start, lead, entering, leave_grad, skip)


def weight_grads(groups, tile, extra=None):
    depth = groups[0][0][0].shape[1]
    rows = groups[0][0][0].shape[0]
    tiles = [group[0][1].shape[1] // tile for group in groups]
    starts = [sum(tiles[:g]) for g in range(len(groups) + 1)]
    terms = max(len(group) for group in groups)
    flat = [array for group in groups for term in group for array in term]
    count = len(flat)

    def kernel(*refs):
        out, turned = refs[-2], refs[-1]
        j = pl.program_id(0)
        place = 0
        for g, group in enumerate(groups):
            mine = refs[place : place + 2 * len(group)]
            place += 2 * len(group)

            @pl.when(j == starts[g])
            def _(mine=mine):
                for t in range(len(mine) // 2):
                    turned[t] = mine[2 * t][...].T

            @pl.when((j >= starts[g]) & (j < starts[g + 1]))
            def _(mine=mine):
                total = sum(dot_nn(turned[t], mine[2 * t + 1][...]) for t in range(len(mine) // 2))
                out[...] = total.astype(bf16)

        if extra is not None:

            @pl.when(j >= starts[-1])
            def _():
                out[...] = refs[count][...]

    specs = []
    for g, group in enumerate(groups):
        for _ in group:
            specs.append(pl.BlockSpec((rows, depth), lambda j: (0, 0), pipeline_mode=pl.Buffered(1)))
            specs.append(
                pl.BlockSpec((rows, tile), lambda j, a=starts[g], n=tiles[g]: (0, jnp.clip(j - a, 0, n - 1)))
            )
    steps = starts[-1]
    if extra is not None:
        flat = flat + [extra]
        specs.append(pl.BlockSpec((depth, tile), lambda j, a=steps: (0, jnp.maximum(j - a, 0))))
        steps += extra.shape[1] // tile
    return pl.pallas_call(
        kernel,
        grid=(steps,),
        in_specs=specs,
        out_specs=pl.BlockSpec((depth, tile), lambda j: (0, j)),
        out_shape=jax.ShapeDtypeStruct((depth, steps * tile), bf16),
        scratch_shapes=[pltpu.VMEM((terms, depth, rows), bf16)],
        compiler_params=params(),
        cost_estimate=cost(2 * terms * rows * depth * tile * steps, 2 * (count * rows * depth + depth * tile * steps), 0),
    )(*flat)


def expert_kernel(shared, x_ref, grad_ref, gates_ref, mine, w_gu, w_down, *refs):
    if shared:
        ws_gu, ws_down, out_ref, dx_ref, logit_ref, act_ref, gu_ref, s_act_ref, s_gu_ref = refs
    else:
        out_ref, dx_ref, logit_ref, act_ref, gu_ref = refs
    x, grad, gates = x_ref[...], grad_ref[...], gates_ref[...]
    wide = grad.astype(f32)

    def back(gate, up, act_push):
        sigma = jax.nn.sigmoid(gate)
        silu = gate * sigma
        slope = sigma + silu * (1.0 - sigma)
        return silu, jnp.concatenate([act_push * up * slope, act_push * silu], axis=1).astype(bf16)

    out = dx = 0.0
    width = w_down.shape[1]
    own = total = 0.0
    for e in range(w_gu.shape[0]):
        weight = jnp.sum(gates * mine[e : e + 1, :], axis=1, keepdims=True)
        both = dot_nn(x, w_gu[e])
        gate, up = both[:, :width], both[:, width:]
        act_push = dot_nt((weight * wide).astype(bf16), w_down[e])
        silu, gu_grad = back(gate, up, act_push)
        act = (silu * up).astype(bf16)
        act_ref[:, e * width : (e + 1) * width] = (weight * act.astype(f32)).astype(bf16)
        gu_ref[:, 2 * e * width : 2 * (e + 1) * width] = gu_grad
        result = dot_nn(act, w_down[e]).astype(bf16).astype(f32)
        push = jnp.sum(wide * result, axis=1, keepdims=True)
        own = own + push * mine[e : e + 1, :]
        total = total + weight * push
        out = out + weight * result
        dx = dx + dot_nt(gu_grad, w_gu[e]).astype(bf16).astype(f32)
    if shared:
        width = ws_down.shape[0]
        gate, up = dot_nn(x, ws_gu[0]), dot_nn(x, ws_gu[1])
        silu, gu_grad = back(gate, up, dot_nt(grad, ws_down[...]))
        act = (silu * up).astype(bf16)
        s_act_ref[...] = act
        s_gu_ref[...] = gu_grad
        out = out + dot_nn(act, ws_down[...])
        dx = dx + dot_nt(gu_grad[:, :width], ws_gu[0]) + dot_nt(gu_grad[:, width:], ws_gu[1])
    out_ref[...] = out.astype(bf16)
    dx_ref[...] = dx.astype(bf16)
    logit_ref[...] = gates * (own - total)


def experts(x, grad, gates, mine, w_gu, w_down, shared=()):
    rows, model = x.shape
    count, _, double = w_gu.shape
    width = double // 2
    every = gates.shape[1]

    def row(columns):
        return pl.BlockSpec((ROWS, columns), lambda i: (i, 0))

    def whole(array):
        zeros = (0,) * array.ndim
        return pl.BlockSpec(array.shape, lambda i: zeros, pipeline_mode=pl.Buffered(1))

    widths = [model, model, every, count * width, count * double]
    hidden = count * width
    if shared:
        ff = shared[1].shape[0]
        hidden += ff
        widths += [ff, 2 * ff]
    return pl.pallas_call(
        lambda *refs: expert_kernel(bool(shared), *refs),
        grid=(rows // ROWS,),
        in_specs=[row(model), row(model), row(every), whole(mine), whole(w_gu), whole(w_down)]
        + [whole(w) for w in shared],
        out_specs=[row(w) for w in widths],
        out_shape=[made(rows, w, kind=f32 if i == 2 else bf16) for i, w in enumerate(widths)],
        compiler_params=params(),
        cost_estimate=cost(
            rows * hidden * model * 12, 6 * hidden * model + rows * (8 * model + 6 * hidden), rows * hidden
        ),
    )(x, grad, gates, mine, w_gu, w_down, *shared)


def shifted(array, axis, by):
    count = lax.axis_size(axis)
    pairs = [(i, i + by) for i in range(count) if 0 <= i + by < count]
    return lax.ppermute(array, axis, pairs)


def prefix(part, axis, combine, identity):
    place = lax.axis_index(axis)
    gathered = jax.tree.map(lambda a: lax.all_gather(a, axis), part)
    state = jax.tree.map(lambda a, e: jnp.zeros_like(a) + jnp.asarray(e, a.dtype), part, identity)

    def one(lap, state):
        return combine(
            state, jax.tree.map(lambda a: lax.dynamic_index_in_dim(a, lap, 0, False), gathered)
        )

    return lax.fori_loop(0, place, one, state)


def prefix_2(array, axis, combine, identity):
    count, place = (lax.axis_size(axis), lax.axis_index(axis))
    everything = jax.tree.map(
        lambda part, kind: lax.all_gather(part.astype(kind), axis),
        array,
        jax.tree.map(lambda a: jnp.bfloat16 if a.dtype == jnp.float32 else a.dtype, array),
    )
    start = jax.tree.map(
        lambda part, zero: jnp.broadcast_to(jnp.asarray(zero, part.dtype), part.shape),
        array,
        identity,
    )

    def lap(k, before):
        at = count - 1 - k
        reached = at > place
        new = combine(
            before, jax.tree.map(lambda part, own: part[at].astype(own.dtype), everything, array)
        )
        return jax.tree.map(lambda a, b: jnp.where(reached, a, b), new, before)

    return lax.fori_loop(0, count, lap, start)


def sum_shares(part):
    got = lax.all_to_all(part, "head", split_axis=0, concat_axis=0, tiled=True)
    return jnp.sum(got.astype(f32), axis=0)


def gather_shares(share):
    copies = jnp.broadcast_to(share[None], (lax.axis_size("head"),) + share.shape)
    return lax.all_to_all(copies, "head", split_axis=0, concat_axis=0, tiled=True)


def relay(parts):
    count, place = lax.axis_size("head"), lax.axis_index("head")

    def passed(array, by):
        return lax.ppermute(
            array, "head", [(i, i + by) for i in range(count) if 0 <= i + by < count]
        )

    up, down = [[p] for p in parts], [[p] for p in parts]
    for _ in range(count - 1):
        for k in range(len(parts)):
            up[k].append(passed(up[k][-1], 1))
            down[k].append(passed(down[k][-1], -1))
    return [
        [p] + [jnp.where(place >= d, up[k][d], down[k][count - d]) for d in range(1, count)]
        for k, p in enumerate(parts)
    ]


def laid(pieces, lists, shares_first=True):
    count, place = lax.axis_size("head"), lax.axis_index("head")
    batch_size = len(lists)
    lead = (count, batch_size) if shares_first else (batch_size, count)
    out = jnp.zeros(lead + pieces.shape[1:], pieces.dtype)
    for b, row in enumerate(lists):
        for d, piece in enumerate(row):
            slot = (place + count - d) % count
            at = (slot, b) if shares_first else (b, slot)
            out = lax.dynamic_update_slice(out, piece[None, None], at + (0,) * piece.ndim)
    return out


def relay_shares(share, *extras, shares_first=True):
    batch_size = share.shape[0]
    lists = relay([share[b] for b in range(batch_size)] + list(extras))
    whole = laid(share, lists[:batch_size], shares_first)
    others = []
    for row in lists[batch_size:]:
        out = jnp.zeros((len(row),) + row[0].shape, row[0].dtype)
        for d, piece in enumerate(row):
            slot = (lax.axis_index("head") + len(row) - d) % len(row)
            out = lax.dynamic_update_index_in_dim(out, piece, slot, 0)
        others.append(out)
    return (whole, *others) if extras else whole


def bits_of(axis):
    count = lax.axis_size(axis)
    return [(1 << k) for k in range(count.bit_length() - 1)]


def across(array, axis, bit):
    return lax.ppermute(array, axis, [(i, i ^ bit) for i in range(lax.axis_size(axis))])


def add_over(array, *axes):
    for axis in axes:
        for bit in bits_of(axis):
            array = array + across(array, axis, bit)
    return array


def join_over(array, dimension, *axes):
    for axis in axes:
        place = lax.axis_index(axis)
        for bit in bits_of(axis):
            other = across(array, axis, bit)
            array = jnp.where(
                (place & bit) == 0,
                jnp.concatenate([array, other], axis=dimension),
                jnp.concatenate([other, array], axis=dimension),
            )
    return array


def tie(*arrays):
    return lax.optimization_barrier(arrays)


def around(array, by):
    count = lax.axis_size("seq")
    if by % count == 0:
        return array
    return lax.ppermute(array, "seq", [(i, (i + by) % count) for i in range(count)])


def spread_last(local_part, rank_index, part_count):
    local_width = local_part.shape[-1]
    full_array = jnp.zeros(local_part.shape[:-1] + (local_width * part_count,), jnp.float32)
    return lax.dynamic_update_slice_in_dim(
        full_array, local_part, rank_index * local_width, local_part.ndim - 1
    )


def chain_forward(earlier, later):
    return (earlier[0] * later[0], later[0] * earlier[1] + later[1])


def chain_backward(earlier, later):
    return (earlier[0] * later[0], later[1] + later[0] * earlier[1])


def local(
    x_in,
    d_out,
    log_decay,
    routes,
    norm1_gain,
    w_in_zx,
    w_in_bc,
    w_in_dt,
    dt_bias,
    conv_x,
    conv_x_bias,
    conv_bc,
    conv_bc_bias,
    skip_d,
    gate_norm_gain,
    w_out,
    norm2_gain,
    router,
    w_expert_gu,
    w_expert_down,
    w_shared_gu,
    w_shared_down,
):
    batch_size, tokens, model_width = x_in.shape
    inner_dev = w_in_zx.shape[2]
    heads_dev = w_in_dt.shape[1]
    head_size = inner_dev // heads_dev
    state_size = w_in_bc.shape[1] // 2
    conv_taps = conv_x.shape[0]
    experts_dev = w_expert_gu.shape[0]
    head_count = lax.axis_size("head")
    seq_count = lax.axis_size("seq")
    head_rank = lax.axis_index("head")
    seq_rank = lax.axis_index("seq")
    inner_all = inner_dev * head_count
    experts_all = experts_dev * seq_count * head_count
    share_rows = tokens // head_count
    rows_all = batch_size * tokens
    conv_width = inner_dev + 2 * state_size
    edge = conv_taps - 1

    def by_share(array):
        array = array.reshape((batch_size, head_count, share_rows) + array.shape[2:])
        return jnp.swapaxes(array, 0, 1)

    def by_position(array):
        return jnp.swapaxes(array, 0, 1).reshape(batch_size, tokens, array.shape[-1])

    def own_share(array):
        return lax.dynamic_index_in_dim(array, head_rank, 0, keepdims=False)

    def flat(array):
        return array.reshape(-1, array.shape[-1])

    def times(a, b):
        return lax.dot_general(a, b, (((a.ndim - 1,), (0,)), ((), ())), preferred_element_type=f32)

    def times_t(a, b):
        return lax.dot_general(a, b, (((a.ndim - 1,), (1,)), ((), ())), preferred_element_type=f32)

    def scattered(array, axes):
        return lax.psum_scatter(array, axes, scatter_dimension=0, tiled=True)

    x_rows, grad_rows = by_share(x_in), by_share(d_out)
    grads_in = [flat(around(grad_rows, k)) for k in range(seq_count)]
    input_wide = x_rows.astype(f32)
    scale_one = lax.rsqrt(jnp.mean(input_wide * input_wide, axis=-1, keepdims=True) + norm_eps)
    normed_one = (input_wide * scale_one * norm1_gain).astype(bf16)
    w_conv = jnp.concatenate([w_in_zx[1], w_in_bc], axis=-1)
    w_step = jnp.pad(w_in_dt, ((0, 0), (0, 128 - heads_dev)))
    w_late = jnp.concatenate([w_conv, w_step], axis=-1)
    conv_in = times(normed_one, w_conv).astype(bf16)
    step_raw = times(normed_one, w_step)[..., :heads_dev]
    gate_z = times(normed_one, w_in_zx[0])
    edge_rows = shifted(conv_in[head_count - 1, :, share_rows - edge :], "seq", 1).astype(f32)
    edge_rows = jnp.pad(edge_rows, ((0, 0), (8 - edge, 0), (0, 0)))
    taps = jnp.concatenate([conv_x, conv_bc], axis=1)
    bias = jnp.concatenate([conv_x_bias, conv_bc_bias])
    taps_bias = jnp.concatenate([taps, bias[None], jnp.zeros((7 - conv_taps, conv_width), f32)])
    decay_across = jnp.transpose(log_decay, (0, 2, 1))
    step_bias = dt_bias[None]
    totals = jnp.sum(log_decay.reshape(batch_size, -1, BLOCK, heads_dev), axis=2)
    before = [jnp.zeros_like(totals[:, 0])]
    for k in range(totals.shape[1]):
        before.append(before[-1] + totals[:, k])
    lead = jnp.repeat(jnp.exp(jnp.stack(before, axis=1)), head_size, axis=-1)
    device_decay, lead = lead[:, -1:], lead[:, :-1, None]
    skip = jnp.repeat(skip_d, head_size)[None]
    gate_gain = gate_norm_gain[None]

    conv_act, scanned, starts, leaving = scan_forward(
        conv_in, edge_rows, taps_bias, step_raw, step_bias, log_decay, decay_across, inner_dev, state_size
    )
    identity = (jnp.ones_like(device_decay), jnp.zeros_like(leaving))
    if seq_count == 2:
        entering = shifted(leaving, "seq", 1)
    else:
        _, entering = prefix((device_decay, leaving), "seq", chain_forward, identity)
    mixed, gated_low, squares, partial_out = gate_forward(
        scanned, conv_act, gate_z, log_decay, lead, entering, skip, gate_gain, w_out
    )

    mix_out = sum_shares(partial_out)
    squares = own_share(add_over(squares[..., 0], "head"))
    gate_scale = lax.rsqrt(squares / inner_all + norm_eps)[..., None]
    hidden = own_share(x_rows).astype(f32) + mix_out * gate_scale
    scale_two = lax.rsqrt(jnp.mean(hidden * hidden, axis=-1, keepdims=True) + norm_eps)
    normed_share = (hidden * scale_two * norm2_gain).astype(bf16)

    expert_ids = jnp.arange(experts_all, dtype=jnp.int32)
    used = jnp.any(own_share(by_share(routes))[..., None] == expert_ids, axis=2)
    logits = times(normed_share, router)
    top = jnp.max(jnp.where(used, logits, -jnp.inf), axis=-1, keepdims=True)
    powers = jnp.where(used, jnp.exp(jnp.where(used, logits - top, 0.0)), 0.0)
    gates = powers / jnp.sum(powers, axis=-1, keepdims=True)
    normed_two, gates = relay_shares(normed_share, flat(gates).T)

    first = (seq_rank * head_count + head_rank) * experts_dev
    mine = (jnp.arange(8)[:, None] + first == expert_ids) & (jnp.arange(8)[:, None] < experts_dev)
    mine = mine.astype(f32)
    ffn_out, ffn_dx, logit_grad = [], [], []
    up_terms, down_terms = [], []
    for k in [*range(1, seq_count), 0]:
        rows = flat(around(normed_two, k))
        weights = flat(jnp.swapaxes(around(gates, k), 1, 2))
        shared = (w_shared_gu, w_shared_down) if k == 0 else ()
        pieces = experts(rows, grads_in[k], weights, mine, w_expert_gu, w_expert_down, shared)
        ffn_out.append(around(pieces[0], -k))
        ffn_dx.append(around(pieces[1], -k))
        logit_grad.append(around(pieces[2], -k))
        down_terms.append((grads_in[k], pieces[3]))
        up_terms.append((rows, pieces[4]))
    shared_terms = [[(rows, pieces[6])], [(grads_in[0], pieces[5])]]
    expert_grads = [
        weight_grads([up_terms[k : k + 2], down_terms[k : k + 2]], 512) for k in range(0, seq_count, 2)
    ]
    if len(expert_grads) > 1:
        expert_grads = [sum(g.astype(f32) for g in expert_grads).astype(bf16)]
    logit_grad = sum(logit_grad).astype(bf16)
    ffn_dx = sum(d.astype(f32) for d in ffn_dx) + times_t(logit_grad, router)
    ffn_dx = ffn_dx.astype(bf16).reshape(normed_two.shape)
    expert_sum = scattered(expert_grads[0], "dp")
    dx_share, _, logit_grad = tie(sum_shares(ffn_dx), expert_grads[0], logit_grad)
    grad_router = lax.dot_general(
        logit_grad, flat(normed_two), (((0,), (0,)), ((), ())), preferred_element_type=f32
    )
    gained_two = dx_share * norm2_gain
    hidden_grad = own_share(grad_rows).astype(f32) + scale_two * (
        gained_two
        - hidden * scale_two * scale_two * jnp.mean(gained_two * hidden, axis=-1, keepdims=True)
    )
    grad_norm_two = jnp.sum(dx_share * hidden * scale_two, axis=(0, 1))
    scale_push = jnp.sum(hidden_grad * mix_out, axis=-1)
    squares_grad = -0.5 * scale_push * gate_scale[..., 0] ** 3 / inner_all
    out_push, squares_grad = relay_shares((hidden_grad * gate_scale).astype(bf16), squares_grad)
    out_push, expert_sum = tie(out_push, expert_sum)
    ffn_low = sum(f.astype(f32) for f in ffn_out).astype(bf16).reshape(normed_two.shape)
    ffn_low, out_push = tie(ffn_low, out_push)
    ffn_share = sum_shares(ffn_low)

    mixed_grad, z_grad, entering_grad, channel_sums = gate_backward(
        out_push, w_out, mixed, gate_z, conv_act, log_decay, lead, squares_grad[..., None], gate_gain
    )
    if seq_count == 2:
        leaving_grad = shifted(entering_grad.astype(bf16), "seq", -1).astype(f32)
    else:
        _, leaving_grad = prefix_2((device_decay, entering_grad), "seq", chain_backward, identity)
    in_grad, first_rows, last_rows, tap_sums = scan_backward(
        conv_in,
        edge_rows,
        taps_bias,
        step_raw,
        step_bias,
        log_decay,
        decay_across,
        conv_act,
        mixed_grad,
        starts,
        lead,
        entering,
        leaving_grad,
        skip,
    )
    early_dx = times_t(z_grad, w_in_zx[0])
    in_grad, ffn_share = tie(in_grad, ffn_share)
    next_rows = shifted(first_rows[:, :edge], "seq", -1)
    late = [
        sum(taps[edge - k] * next_rows[:, k + i - edge] for k in range(conv_taps) if k + i >= edge)
        for i in range(edge)
    ]
    late = last_rows.at[:, 8 - edge :].add(jnp.stack(late, axis=1)).astype(bf16)
    in_grad = in_grad.at[head_count - 1, :, share_rows - 8 :, :conv_width].set(late)
    normed_one_grad = early_dx + times_t(in_grad, w_late)
    grad_norm_one = jnp.sum(normed_one_grad * input_wide * scale_one, axis=(0, 1, 2))
    normed_one_grad = normed_one_grad.astype(bf16)
    dn_share = sum_shares(normed_one_grad)

    def whole(array):
        return spread_last(array, head_rank, head_count).reshape(-1)

    small = [
        grad_norm_two,
        grad_router.reshape(-1),
        whole(tap_sums[:conv_taps, :inner_dev]),
        whole(tap_sums[conv_taps, :inner_dev]),
        whole(channel_sums[0]),
        grad_norm_one,
        tap_sums[:conv_taps, inner_dev:].reshape(-1),
        tap_sums[conv_taps, inner_dev:],
        whole(tap_sums[conv_taps + 1, :heads_dev]),
        whole(jnp.sum(channel_sums[1].reshape(heads_dev, head_size), axis=-1)),
    ]
    sizes = [a.shape[0] for a in small]
    small = jnp.concatenate(small + [jnp.zeros((128 * model_width - sum(sizes),), f32)])
    small = small.reshape(128, model_width).T.astype(bf16)
    grad_late = weight_grads([[(flat(normed_one), flat(in_grad))]], 128, small)
    early_terms = [[(flat(out_push), flat(gated_low))], [(flat(normed_one), flat(z_grad))]]
    grad_early = weight_grads(early_terms + shared_terms, 256)
    late_sum = scattered(grad_late, ("dp", "seq")).astype(f32)
    merged = jnp.concatenate([late_sum[:, inner_dev:conv_width], late_sum[:, conv_width + 128 :]], axis=1)
    merged = add_over(merged, "head")
    merged = join_over(merged, 0, "seq", "dp")
    early_sum = scattered(grad_early, ("dp", "seq"))

    layer_share, dn_share, early_sum = tie((hidden + ffn_share).astype(bf16), dn_share, early_sum)
    early_sum = early_sum.astype(f32)
    layer_out = by_position(gather_shares(layer_share))
    gained_one = dn_share * norm1_gain
    input_share, scale_share = own_share(input_wide), own_share(scale_one)
    input_grad = hidden_grad + scale_share * (
        gained_one
        - input_share
        * scale_share
        * scale_share
        * jnp.mean(gained_one * input_share, axis=-1, keepdims=True)
    )
    d_input = relay_shares(input_grad.astype(bf16), shares_first=False)
    d_input = d_input.reshape(batch_size, tokens, model_width)

    grad_bc = merged[:, : 2 * state_size]
    small = merged[:, 2 * state_size :].T.reshape(-1)
    ends = [sum(sizes[:k]) for k in range(len(sizes) + 1)]
    small = [small[ends[k] : ends[k + 1]] for k in range(len(sizes))]
    expert_sum = expert_sum.astype(f32)
    double = w_expert_gu.shape[2]
    grad_gu = [expert_sum[:, e * double : (e + 1) * double] for e in range(experts_dev)]
    expert_sum = expert_sum[:, experts_dev * double :]
    width = double // 2
    grad_down = [expert_sum[:, e * width : (e + 1) * width].T for e in range(experts_dev)]
    shared_sum = early_sum[:, 2 * inner_dev :]
    ff_dev = w_shared_down.shape[0]
    return (
        layer_out,
        d_input,
        small[5],
        jnp.stack([early_sum[:, inner_dev : 2 * inner_dev], late_sum[:, :inner_dev]]),
        grad_bc,
        late_sum[:, conv_width : conv_width + heads_dev],
        small[8],
        small[2].reshape(conv_taps, inner_all),
        small[3],
        small[6].reshape(conv_taps, 2 * state_size),
        small[7],
        small[9],
        small[4],
        early_sum[:, :inner_dev].T,
        small[0],
        small[1].reshape(experts_all, model_width).T,
        jnp.stack(grad_gu),
        jnp.stack(grad_down),
        jnp.stack([shared_sum[:, :ff_dev], shared_sum[:, ff_dev : 2 * ff_dev]]),
        shared_sum[:, 2 * ff_dev :].T,
    )


def solution(mesh):
    placed = (
        P("dp", "seq", None),
        P("dp", "seq", None),
        P("dp", "seq", "head"),
        P("dp", "seq", None),
        P(),
        P(None, None, "head"),
        P(),
        P(None, "head"),
        P("head"),
        P(None, "head"),
        P("head"),
        P(),
        P(),
        P("head"),
        P("head"),
        P("head", None),
        P(),
        P(),
        P(("seq", "head"), None, None),
        P(("seq", "head"), None, None),
        P(None, None, "head"),
        P("head", None),
    )
    return jax.shard_map(
        local,
        mesh=mesh,
        in_specs=placed,
        out_specs=(
            P("dp", "seq", None),
            P("dp", "seq", None),
            P(),
            P(None, ("dp", "seq"), "head"),
            P(),
            P(("dp", "seq"), "head"),
            P(),
            P(),
            P(),
            P(),
            P(),
            P(),
            P(),
            P("head", ("dp", "seq")),
            P(),
            P(),
            P(("seq", "head"), "dp", None),
            P(("seq", "head"), None, "dp"),
            P(None, ("dp", "seq"), "head"),
            P("head", ("dp", "seq")),
        ),
        check_vma=False,
    )
```

time: 1260 us -> 898 us (0.71)
  waiting for transfers between devices: 634 us -> 284 us
  matrix products: 299 us -> 30.6 us
  Pallas kernels: 0 us -> 191 us
  starting transfers between devices: 55.9 us -> 187 us
  local copies, waits for them, and re-layouts: 161 us -> 100 us
    all_to_all x10 -> x5, waiting for transfers between devices: 397 us -> 104 us  [the longest x4 104 us: sum_shares(): got = lax.all_to_all(part, 'head', split_axis=0, concat_axis=0, tiled=True)]
    dot_general x50 -> x8, matrix products: 299 us -> 30.6 us  [the longest x4 14.6 us: times(): lax.dot_general(a, b, (((a.ndim - 1,), (0,)), ((), ())), preferred_elemen...]
    psum x2 -> x0, waiting for transfers between devices: 231 us -> none  [local(): lax.psum((grad_norm_one, grad_norm_two, grad_router, grad_w_bc, grad_conv...]
    pallas_call x0 -> x9, Pallas kernels: none -> 191 us  [the longest x3 66 us: weight_grads(): pl.pallas_call(kernel, grid=(steps,), in_specs=specs, out_specs=pl.BlockS...]
    ppermute x0 -> x55, waiting for transfers between devices: none -> 168 us  [the longest x7 143 us: across(): lax.ppermute(array, axis, [(i, i ^ bit) for i in range(lax.axis_size(axis...]
    ppermute x0 -> x55, starting transfers between devices: none -> 153 us  [the longest x48 136 us: passed(): lax.ppermute(array, 'head', [(i, i + by) for i in range(count) if 0 <= i...]
    unnamed x325 -> x100, local copies, waits for them, and re-layouts: 72.9 us -> 19.1 us
    reshape x15 -> x7, local copies, waits for them, and re-layouts: 32.3 us -> 1.87 us  [the longest x1 0.94 us: local(): small = merged[:, 2 * state_size:].T.reshape(-1)]
  transfers between devices with their start and end apart: 29 -> 73, of which waited for: 12 -> 17; matrix products, arithmetic and copies ran while one was open for 33% -> 21% of each run, Pallas kernels for 0% -> 8%
where the time goes in v2:
time: 898 us; the launch traced here: 885 us
  waiting for transfers between devices  284 us (32%)
  Pallas kernels  191 us (21%)
  starting transfers between devices  187 us (21%)
  local copies, waits for them, and re-layouts  100 us (11%)
  other arithmetic  77.5 us (9%)
  matrix products  30.6 us (3%)
  between operations  15.7 us (2%)
    ppermute x7, waiting for transfers between devices, across(): lax.ppermute(array, axis, [(i, i ^ bit) for i in range(lax.axis_size(axis...  143 us
    ppermute x48, starting transfers between devices, passed(): lax.ppermute(array, 'head', [(i, i + by) for i in range(count) if 0 <= i...  136 us
    all_to_all x4, waiting for transfers between devices, sum_shares(): got = lax.all_to_all(part, 'head', split_axis=0, concat_axis=0, tiled=True)  104 us
    pallas_call x3, Pallas kernels, weight_grads(): pl.pallas_call(kernel, grid=(steps,), in_specs=specs, out_specs=pl.BlockS...  66 us
    pallas_call x2, Pallas kernels, experts(): pl.pallas_call(lambda *refs: expert_kernel(bool(shared), *refs), grid=(ro...  61.1 us
    pallas_call x1, Pallas kernels, scan_backward(): pl.pallas_call(scan_back_kernel, grid=(batch, blocks), in_specs=[rows_of(...  25.8 us
    ppermute x48, waiting for transfers between devices, passed(): lax.ppermute(array, 'head', [(i, i + by) for i in range(count) if 0 <= i...  25.3 us
    dynamic_update_slice x18, other arithmetic, laid(): lax.dynamic_update_slice(out, piece[None, None], at + (0,) * piece.ndim)  23.7 us
  transfers between devices with their start and end apart: 73, of which 17 were waited for; matrix products, arithmetic and copies ran while one was open for 21% of the time, Pallas kernels for 8%

profile of v2, /device:TPU:0, one launch (start us, length us, event | category | flops | bytes accessed | tf_op | source)
XLA Modules:
  0.0 885.3 jit_solution(17451198020154063965)
XLA Ops:
  14.1 3.7 fusion.20.cin.cin_before
  24.4 3.7 fusion.34.raw
  31.9 14.4 %shard_map.365 = (bf16[4,2,128,1024]{3,2,1,0:T(8,128)(2,1)}, f32[4,2,128,768]{3,2,1,0:T(8,128)}, f32[2,2,128,768]{3,2,1,0:T(8,128)}, f32[2,128,768]{2,1,0:T(8,128)}) custom-call(bf16[4,2,128,1024]{3,2,1,0:T(8,128)(2,1)} %copy-done.8, f32[2,8,1024]{2,1,0:T(8,128)} %pad_convert_fusion.edge, f32[8,1024]{1,0:T(8,128)} %maximum_maximum_fusion.taps, ...), custom_call_target="tpu_custom_call" | custom-call | flops 1207959552 | bytes 7864320 | tf_op jit(solution)/shard_map/pallas_call | solution.py:308
  50.3 6.9 fusion.16.z
  57.2 12.2 %shard_map.366 = (bf16[4,2,128,768]{3,2,1,0:T(8,128)(2,1)}, bf16[4,2,128,768]{3,2,1,0:T(8,128)(2,1)}, f32[4,2,128,128]{3,2,1,0:T(8,128)}, bf16[4,2,128,1536]{3,2,1,0:T(8,128)(2,1)}) custom-call(f32[4,2,128,768]{3,2,1,0:T(8,128)} %get-tuple-element.83.y, bf16[4,2,128,1024]{3,2,1,0:T(8,128)(2,1)} %get-tuple-element.84.act_in, f32[4,2,128,768]{3,2,1,0:T(8,128)} %fusion.16.z, ...), custom_call_target="tpu_custom_call" | custom-call | flops 2617245696 | bytes 14155776 | tf_op jit(solution)/shard_map/pallas_call | solution.py:344
  69.4 5.7 all-to-all-start
  78.8 45.9 %collective-permute-done.2 = f32[4,2,128]{2,1,0:T(2,128)S(1)} collective-permute-done((f32[4,2,128]{2,1,0:T(2,128)S(1)}, f32[4,2,128]{2,1,0:T(2,128)S(1)}, u32[]{:S(2)}, u32[]{:S(2)}) %collective-permute-start.2) | collective-permute-done | bytes 4128 | tf_op jit(solution)/shard_map/ppermute | solution.py:694
  124.7 4.7 collective-permute-start.3
  129.4 4.6 copy_convert_fusion
  134.1 10.7 %collective-permute-done.3 = f32[4,2,128]{2,1,0:T(2,128)S(1)} collective-permute-done((f32[4,2,128]{2,1,0:T(2,128)S(1)}, f32[4,2,128]{2,1,0:T(2,128)S(1)}, u32[]{:S(2)}, u32[]{:S(2)}) %collective-permute-start.3) | collective-permute-done | bytes 4128 | tf_op jit(solution)/shard_map/ppermute | solution.py:694
  151.9 5.3 collective-permute-start.4
  164.7 4.5 collective-permute-start.18
  169.9 3.8 copy.356
  173.7 3.8 copy.348
  178.8 5.3 collective-permute-start.8
  185.4 5.3 collective-permute-start.14
  196.2 6.6 collective-permute-done.20
  206.3 4.6 collective-permute-start.9
  212.2 4.6 collective-permute-start.15
  226.9 4.5 collective-permute-start.23
  233.8 33.5 %shard_map.368 = (bf16[1024,1536]{1,0:T(8,128)(2,1)}, bf16[1024,1536]{1,0:T(8,128)(2,1)}, f32[1024,16]{1,0:T(8,128)}, bf16[1024,1024]{1,0:T(8,128)(2,1)}, bf16[1...) custom-call(bf16[1024,1536]{1,0:T(8,128)(2,1)} %bitcast.38.refs_0_.refs_2_.refs_4_, ...), custom_call_target="tpu_custom_call" | custom-call | flops 24159191040 | bytes 32243712 | tf_op jit(solution)/shard_map/pallas_call | solution.py:575
  268.1 27.6 %shard_map.367 = (bf16[1024,1536]{1,0:T(8,128)(2,1)}, bf16[1024,1536]{1,0:T(8,128)(2,1)}, f32[1024,16]{1,0:T(8,128)}, bf16[1024,1024]{1,0:T(8,128)(2,1)}, bf16[1024,2048]{1,0:T(8,128)(2,1)}) custom-call(bf16[1024,1536]{1,0:T(8,128)(2,1)} %bitcast.25.refs_0_, bf16[1024,1536]{1,0:T(8,128)(2,1)} %bitcast.276, f32[1024,16]{1,0:T(8,128)} %bitcast.302, ...), custom_call_target="tpu_custom_call" | custom-call | flops 19327352832 | bytes 28311552 | tf_op jit(solution)/shard_map/pallas_call | solution.py:575
  295.7 32.4 %shard_map.369 = bf16[1536,3072]{1,0:T(8,128)(2,1)} custom-call(bf16[1024,1536]{1,0:T(8,128)(2,1)} %bitcast.25.refs_0_, bf16[1024,2048]{1,0:T(8,128)(2,1)} %get-tuple-element.94.refs_1_, bf16[1024,1536]{1,0:T(8,128)(2,1)} %bitcast.38.refs_0_.refs_2_.refs_4_, bf16[1024,2048]{1,0:T(8,128)(2,1)} %get-tuple-element.95.refs_3_, bf16[1024,1536]{1,0:T(8,128)(2,1)} %bitcast.277, ...), custom_call_target="tpu_custom_call" | custom-call | flops 19327352832 | bytes 34603008 | tf_op jit(solution)/shard_map/pallas_call | solution.py:498
  329.1 5.5 collective-permute-done.27
  336.8 3.0 add_convert_fusion
  339.8 4.7 all-to-all-start.1
  345.3 5.6 collective-permute-done.25
  350.9 4.5 add_convert_fusion.1
  355.4 60.5 %all-to-all-done.1 = bf16[4,2,128,1536]{3,2,1,0:T(8,128)(2,1)} async-done(((bf16[4,2,128,1536]{3,2,1,0:T(8,128)(2,1)}), bf16[4,2,128,1536]{3,2,1,0:T(8,128)(2,1)}, u32[]{:S(2)}, u32[]{:S(2)}) %all-to-all-start.1) | async-done | bytes 3145760 | tf_op jit(solution)/shard_map/all_to_all | solution.py:633
  425.6 4.5 collective-permute-start.40
  434.1 5.3 collective-permute-start.34
  441.5 4.5 collective-permute-start.44
  453.3 9.6 %collective-permute-done.43 = f32[2,128]{1,0:T(2,128)S(1)} collective-permute-done((f32[2,128]{1,0:T(2,128)S(1)}, f32[2,128]{1,0:T(2,128)S(1)}, u32[]{:S(2)}, u32[]{:S(2)}) %collective-permute-start.43) | collective-permute-done | bytes 1056 | tf_op jit(solution)/shard_map/ppermute | solution.py:646
  465.4 4.7 collective-permute-start.32
  471.3 5.3 collective-permute-start.38
  484.4 4.6 collective-permute-start.33
  490.2 4.6 collective-permute-start.39
  505.7 11.5 %shard_map.370 = (bf16[4,2,128,768]{3,2,1,0:T(8,128)(2,1)}, bf16[4,2,128,768]{3,2,1,0:T(8,128)(2,1)}, f32[2,128,768]{2,1,0:T(8,128)}, f32[8,768]{1,0:T(8,128)}) custom-call(bf16[4,2,128,1536]{3,2,1,0:T(8,128)(2,1)} %bitcast_dynamic-update-slice_fusion.8.push, bf16[768,1536]{1,0:T(8,128)(2,1)} %w_out.3, bf16[4,2,128,768]{3,2,1,0:T(8,128)(2,1)} %get-tuple-element.101.mixed_in, ...), custom_call_target="tpu_custom_call" | custom-call | flops 2617245696 | bytes 14155776 | tf_op jit(solution)/shard_map/pallas_call | solution.py:377
  517.2 20.2 %shard_map.372 = bf16[1536,2304]{1,0:T(8,128)(2,1)} custom-call(bf16[1024,1536]{1,0:T(8,128)(2,1)} %bitcast.69.refs_0_, bf16[1024,768]{1,0:T(8,128)(2,1)} %bitcast.300, bf16[1024,1536]{1,0:T(8,128)(2,1)} %bitcast.267, bf16[1024,768]{1,0:T(8,128)(2,1)} %bitcast.301, bf16[1024,1536]{1,0:T(8,128)(2,1)} %bitcast.38.refs_0_.refs_2_.refs_4_, ...), custom_call_target="tpu_custom_call" | custom-call | flops 7247757312 | bytes 32243712 | tf_op jit(solution)/shard_map/pallas_call | solution.py:498
  537.4 4.7 all-to-all-start.2
  545.4 2.9 convolution_convert_fusion
  552.0 25.8 %shard_map.371 = (bf16[4,2,128,1152]{3,2,1,0:T(8,128)(2,1)}, f32[2,8,1024]{2,1,0:T(8,128)}, f32[2,8,1024]{2,1,0:T(8,128)}, f32[8,1024]{1,0:T(8,128)}) custom-call(bf16[4,2,128,1024]{3,2,1,0:T(8,128)(2,1)} %copy-done.8, bf16[4,2,128,1024]{3,2,1,0:T(8,128)(2,1)} %copy-done.8, f32[2,8,1024]{2,1,0:T(8,128)} %pad_convert_fusion.edge, ...), custom_call_target="tpu_custom_call" | custom-call | flops 2617245696 | bytes 11796480 | tf_op jit(solution)/shard_map/pallas_call | solution.py:411
  585.2 19.2 %all-to-all-done.2 = bf16[4,2,128,1536]{3,2,1,0:T(8,128)(2,1)} async-done(((bf16[4,2,128,1536]{3,2,1,0:T(8,128)(2,1)}), bf16[4,2,128,1536]{3,2,1,0:T(8,128)(2,1)}, u32[]{:S(2)}, u32[]{:S(2)}) %all-to-all-start.2) | async-done | bytes 3145760 | tf_op jit(solution)/shard_map/all_to_all | solution.py:633
  604.4 3.8 convert_reduce_fusion.1
  608.8 6.1 fusion.7
  615.0 6.0 fusion.6
  621.0 5.0 all-to-all-start.3
  627.6 11.5 %concatenate.51 = bf16[196608]{0:T(1024)(128)(2,1)} concatenate(bf16[1536]{0:T(1024)(128)(2,1)S(1)} %get-tuple-element.322, bf16[24576]{0:T(1024)(128)(2,1)S(1)} %reshape.369, bf16[12288]{0:T(1024)(128)(2,1)S(1)} %bitcast.284, bf16[3072]{0:T(1024)(128)(2,1)S(1)} %dynamic_update_slice.150, bf16[3072]{0:T(1024)(128)(2,1)S(1)} %dynamic_update_slice.151, ...), dimensions={0} | concatenate | bytes 786432 | tf_op jit(solution)/shard_map/concatenate | solution.py:958
  643.2 13.4 %shard_map.373 = bf16[1536,1280]{1,0:T(8,128)(2,1)} custom-call(bf16[1024,1536]{1,0:T(8,128)(2,1)} %bitcast.268, bf16[1024,1152]{1,0:T(8,128)(2,1)} %bitcast.299, bf16[1536,128]{1,0:T(8,128)(2,1)} %bitcast.281), custom_call_target="tpu_custom_call" | custom-call | flops 4026531840 | bytes 10223616 | tf_op jit(solution)/shard_map/pallas_call | solution.py:498
  662.4 3.3 copy.373
  671.6 24.2 %all-to-all-done.3 = bf16[4,2,128,1536]{3,2,1,0:T(8,128)(2,1)} async-done(((bf16[4,2,128,1536]{3,2,1,0:T(8,128)(2,1)}), bf16[4,2,128,1536]{3,2,1,0:T(8,128)(2,1)}, u32[]{:S(2)}, u32[]{:S(2)}) %all-to-all-start.3) | async-done | bytes 3145760 | tf_op jit(solution)/shard_map/all_to_all | solution.py:633
  707.2 5.3 collective-permute-start.54
  715.7 5.2 all-to-all-start.4
  725.5 53.3 %collective-permute-done.60 = f32[192,384]{1,0:T(8,128)S(1)} collective-permute-done((f32[192,384]{1,0:T(8,128)S(1)}, f32[192,384]{1,0:T(8,128)S(1)}, u32[]{:S(2)}, u32[]{:S(2)}) %collective-permute-start.60) | collective-permute-done | bytes 294944 | tf_op jit(solution)/shard_map/ppermute | solution.py:694
  778.8 5.1 collective-permute-start.61
  786.9 5.3 collective-permute-start.52
  793.5 5.3 collective-permute-start.58
  798.8 9.0 %collective-permute-done.61 = f32[192,384]{1,0:T(8,128)S(1)} collective-permute-done((f32[192,384]{1,0:T(8,128)S(1)}, f32[192,384]{1,0:T(8,128)S(1)}, u32[]{:S(2)}, u32[]{:S(2)}) %collective-permute-start.61) | collective-permute-done | bytes 294944 | tf_op jit(solution)/shard_map/ppermute | solution.py:694
  807.9 5.2 collective-permute-done.50
  817.1 6.3 collective-permute-start.53
  824.7 4.8 collective-permute-start.59
  834.4 5.9 collective-permute-done.63
  844.3 18.4 %collective-permute-done.64 = f32[768,384]{1,0:T(8,128)S(1)} collective-permute-done((f32[768,384]{1,0:T(8,128)S(1)}, f32[768,384]{1,0:T(8,128)S(1)}, u32[]{:S(2)}, u32[]{:S(2)}) %collective-permute-start.64) | collective-permute-done | bytes 1179680 | tf_op jit(solution)/shard_map/ppermute | solution.py:694
  874.6 3.8 copy.364
  (391 shorter events, 198.0 us)
Async XLA Ops:
  19.2 12.1 %collective-permute-start = (bf16[2,3,1024]{2,1,0:T(4,128)(2,1)S(1)}, bf16[2,3,1024]{2,1,0:T(4,128)(2,1)S(1)}, u32[]{:S(2)}, u32[]{:S(2)}) collective-permute-start(bf16[2,3,1024]{2,1,0:T(4,128)(2,1)S(1)} %slice_bitcast_fusion.19), channel_id=1, source_target_pairs={{0,4},{1,5},{2,6},{3,7},{8,12},{9,13},{10,14},{11,15},{16,20},{17,... | collective-permute-start | bytes 36872 | tf_op jit(solution)/shard_map/ppermute | solution.py:592
  46.2 11.0 %collective-permute-start.1 = (f32[2,128,768]{2,1,0:T(8,128)}, f32[2,128,768]{2,1,0:T(8,128)}, u32[]{:S(2)}, u32[]{:S(2)}) collective-permute-start(f32[2,128,768]{2,1,0:T(8,128)} %get-tuple-element.85), channel_id=1, source_target_pairs={{0,4},{1,5},{2,6},{3,7},{8,12},{9,13},{10,14},{11,15},{16,20},{17,... | collective-permute-start | bytes 2359304 | tf_op jit(solution)/shard_map/ppermute | solution.py:592
  69.4 75.3 %all-to-all-start = ((bf16[4,2,128,1536]{3,2,1,0:T(8,128)(2,1)}), bf16[4,2,128,1536]{3,2,1,0:T(8,128)(2,1)}, u32[]{:S(2)}, u32[]{:S(2)}) async-start(bf16[4,2,128,1536]{3,2,1,0:T(8,128)(2,1)} %get-tuple-element.86), calls=%async_computation | async-start | bytes 6291456 | tf_op jit(solution)/shard_map/all_to_all | solution.py:633
  75.1 430.5 %reduce-scatter.4.cloned.1.call-start = ((), (), s32[]{:S(2)}) async-start(), calls=%async_computation.8 | async-start | bytes 11796480 | tf_op jit(solution)/shard_map/reduce_scatter | solution.py:806
  76.7 48.0 %collective-permute-start.2 = (f32[4,2,128]{2,1,0:T(2,128)S(1)}, f32[4,2,128]{2,1,0:T(2,128)S(1)}, u32[]{:S(2)}, u32[]{:S(2)}) collective-permute-start(f32[4,2,128]{2,1,0:T(2,128)S(1)} %slice_reduce_fusion.2), channel_id=1, source_target_pairs={{0,1},{1,0},{2,3},{3,2},{4,5},{5,4},{6,7},{7,6},{8,9},{9,8},{10,11... | collective-permute-start | bytes 12296 | tf_op jit(solution)/shard_map/ppermute | solution.py:694
  78.8 85.8 %collective-permute-start.17 = (bf16[4,2,128,1536]{3,2,0,1:T(8,128)(2,1)}, bf16[4,2,128,1536]{3,2,0,1:T(8,128)(2,1)}, u32[]{:S(2)}, u32[]{:S(2)}) collective-permute-start(bf16[4,2,128,1536]{3,2,0,1:T(8,128)(2,1)} %bitcast.270), channel_id=1, source_target_pairs={{0,4},{4,0},{1,5},{5,1},{2,6},{6,2},{3,7},{7,3},{8,12},{12,8},{9,1... | collective-permute-start | bytes 9437192 | tf_op jit(solution)/shard_map/ppermute | solution.py:725
  124.7 20.0 %collective-permute-start.3 = (f32[4,2,128]{2,1,0:T(2,128)S(1)}, f32[4,2,128]{2,1,0:T(2,128)S(1)}, u32[]{:S(2)}, u32[]{:S(2)}) collective-permute-start(f32[4,2,128]{2,1,0:T(2,128)S(1)} %add.277), channel_id=1, source_target_pairs={{0,2},{1,3},{2,0},{3,1},{4,6},{5,7},{6,4},{7,5},{8,10},{9,11},{10,... | collective-permute-start | bytes 12296 | tf_op jit(solution)/shard_map/ppermute | solution.py:694
  150.5 12.5 %collective-permute-start.5 = (bf16[128,1536]{1,0:T(8,128)(2,1)}, bf16[128,1536]{1,0:T(8,128)(2,1)S(1)}, u32[]{:S(2)}, u32[]{:S(2)}) collective-permute-start(bf16[128,1536]{1,0:T(8,128)(2,1)} %get-tuple-element.354), channel_id=1, source_target_pairs={{1,0},{2,1},{3,2},{5,4},{6,5},{7,6},{9,8},{10,9},{11,10},{13,12},{... | collective-permute-start | bytes 1179656 | tf_op jit(solution)/shard_map/ppermute | solution.py:646
  151.9 26.9 %collective-permute-start.4 = (bf16[128,1536]{1,0:T(8,128)(2,1)}, bf16[128,1536]{1,0:T(8,128)(2,1)}, u32[]{:S(2)}, u32[]{:S(2)}) collective-permute-start(bf16[128,1536]{1,0:T(8,128)(2,1)} %get-tuple-element.354), channel_id=1, source_target_pairs={{0,1},{1,2},{2,3},{4,5},{5,6},{6,7},{8,9},{9,10},{10,11},{12,13},{... | collective-permute-start | bytes 1179656 | tf_op jit(solution)/shard_map/ppermute | solution.py:646
  157.2 28.2 %collective-permute-start.10 = (bf16[128,1536]{1,0:T(8,128)(2,1)S(1)}, bf16[128,1536]{1,0:T(8,128)(2,1)}, u32[]{:S(2)}, u32[]{:S(2)}) collective-permute-start(bf16[128,1536]{1,0:T(8,128)(2,1)S(1)} %get-tuple-element.353), channel_id=1, source_target_pairs={{0,1},{1,2},{2,3},{4,5},{5,6},{6,7},{8,9},{9,10},{10,11},{12,13},{... | collective-permute-start | bytes 1179656 | tf_op jit(solution)/shard_map/ppermute | solution.py:646
  159.2 24.9 %collective-permute-start.11 = (bf16[128,1536]{1,0:T(8,128)(2,1)S(1)}, bf16[128,1536]{1,0:T(8,128)(2,1)}, u32[]{:S(2)}, u32[]{:S(2)}) collective-permute-start(bf16[128,1536]{1,0:T(8,128)(2,1)S(1)} %get-tuple-element.353), channel_id=1, source_target_pairs={{1,0},{2,1},{3,2},{5,4},{6,5},{7,6},{9,8},{10,9},{11,10},{13,12},{... | collective-permute-start | bytes 1179656 | tf_op jit(solution)/shard_map/ppermute | solution.py:646
  163.0 27.7 %collective-permute-start.6 = (bf16[128,1536]{1,0:T(8,128)(2,1)S(1)}, bf16[128,1536]{1,0:T(8,128)(2,1)}, u32[]{:S(2)}, u32[]{:S(2)}) collective-permute-start(bf16[128,1536]{1,0:T(8,128)(2,1)S(1)} %collective-permute-done.5), channel_id=1, source_target_pairs={{1,0},{2,1},{3,2},{5,4},{6,5},{7,6},{9,8},{10,9},{11,10},{13,12},{... | collective-permute-start | bytes 1179656 | tf_op jit(solution)/shard_map/ppermute | solution.py:646
  164.7 12.8 %collective-permute-start.18 = (f32[16,256]{1,0:T(8,128)S(1)}, f32[16,256]{1,0:T(8,128)S(1)}, u32[]{:S(2)}, u32[]{:S(2)}) collective-permute-start(f32[16,256]{1,0:T(8,128)S(1)} %bitcast.286), channel_id=1, source_target_pairs={{0,1},{1,2},{2,3},{4,5},{5,6},{6,7},{8,9},{9,10},{10,11},{12,13},{... | collective-permute-start | bytes 49160 | tf_op jit(solution)/shard_map/ppermute | solution.py:646
  177.5 17.3 %collective-permute-start.19 = (f32[16,256]{1,0:T(8,128)S(1)}, f32[16,256]{1,0:T(8,128)S(1)}, u32[]{:S(2)}, u32[]{:S(2)}) collective-permute-start(f32[16,256]{1,0:T(8,128)S(1)} %bitcast.287), channel_id=1, source_target_pairs={{1,0},{2,1},{3,2},{5,4},{6,5},{7,6},{9,8},{10,9},{11,10},{13,12},{... | collective-permute-start | bytes 49160 | tf_op jit(solution)/shard_map/ppermute | solution.py:646
  178.8 26.2 %collective-permute-start.8 = (bf16[128,1536]{1,0:T(8,128)(2,1)}, bf16[128,1536]{1,0:T(8,128)(2,1)}, u32[]{:S(2)}, u32[]{:S(2)}) collective-permute-start(bf16[128,1536]{1,0:T(8,128)(2,1)} %collective-permute-done.4), channel_id=1, source_target_pairs={{0,1},{1,2},{2,3},{4,5},{5,6},{6,7},{8,9},{9,10},{10,11},{12,13},{... | collective-permute-start | bytes 1179656 | tf_op jit(solution)/shard_map/ppermute | solution.py:646
  184.1 22.2 %collective-permute-start.12 = (bf16[128,1536]{1,0:T(8,128)(2,1)}, bf16[128,1536]{1,0:T(8,128)(2,1)}, u32[]{:S(2)}, u32[]{:S(2)}) collective-permute-start(bf16[128,1536]{1,0:T(8,128)(2,1)} %collective-permute-done.11), channel_id=1, source_target_pairs={{1,0},{2,1},{3,2},{5,4},{6,5},{7,6},{9,8},{10,9},{11,10},{13,12},{... | collective-permute-start | bytes 1179656 | tf_op jit(solution)/shard_map/ppermute | solution.py:646
  185.4 25.5 %collective-permute-start.14 = (bf16[128,1536]{1,0:T(8,128)(2,1)}, bf16[128,1536]{1,0:T(8,128)(2,1)}, u32[]{:S(2)}, u32[]{:S(2)}) collective-permute-start(bf16[128,1536]{1,0:T(8,128)(2,1)} %collective-permute-done.10), channel_id=1, source_target_pairs={{0,1},{1,2},{2,3},{4,5},{5,6},{6,7},{8,9},{9,10},{10,11},{12,13},{... | collective-permute-start | bytes 1179656 | tf_op jit(solution)/shard_map/ppermute | solution.py:646
  190.7 21.5 %collective-permute-start.7 = (bf16[128,1536]{1,0:T(8,128)(2,1)}, bf16[128,1536]{1,0:T(8,128)(2,1)}, u32[]{:S(2)}, u32[]{:S(2)}) collective-permute-start(bf16[128,1536]{1,0:T(8,128)(2,1)} %collective-permute-done.6), channel_id=1, source_target_pairs={{1,0},{2,1},{3,2},{5,4},{6,5},{7,6},{9,8},{10,9},{11,10},{13,12},{... | collective-permute-start | bytes 1179656 | tf_op jit(solution)/shard_map/ppermute | solution.py:646
  202.8 24.0 %collective-permute-start.22 = (f32[16,256]{1,0:T(8,128)S(1)}, f32[16,256]{1,0:T(8,128)S(1)}, u32[]{:S(2)}, u32[]{:S(2)}) collective-permute-start(f32[16,256]{1,0:T(8,128)S(1)} %collective-permute-done.18), channel_id=1, source_target_pairs={{0,1},{1,2},{2,3},{4,5},{5,6},{6,7},{8,9},{9,10},{10,11},{12,13},{... | collective-permute-start | bytes 49160 | tf_op jit(solution)/shard_map/ppermute | solution.py:646
  205.0 26.4 %collective-permute-start.21 = (f32[16,256]{1,0:T(8,128)S(1)}, f32[16,256]{1,0:T(8,128)S(1)}, u32[]{:S(2)}, u32[]{:S(2)}) collective-permute-start(f32[16,256]{1,0:T(8,128)S(1)} %collective-permute-done.20), channel_id=1, source_target_pairs={{1,0},{2,1},{3,2},{5,4},{6,5},{7,6},{9,8},{10,9},{11,10},{13,12},{... | collective-permute-start | bytes 49160 | tf_op jit(solution)/shard_map/ppermute | solution.py:646
  206.3 14.2 %collective-permute-start.9 = (bf16[128,1536]{1,0:T(8,128)(2,1)}, bf16[128,1536]{1,0:T(8,128)(2,1)S(1)}, u32[]{:S(2)}, u32[]{:S(2)}) collective-permute-start(bf16[128,1536]{1,0:T(8,128)(2,1)} %collective-permute-done.8), channel_id=1, source_target_pairs={{0,1},{1,2},{2,3},{4,5},{5,6},{6,7},{8,9},{9,10},{10,11},{12,13},{... | collective-permute-start | bytes 1179656 | tf_op jit(solution)/shard_map/ppermute | solution.py:646
  210.9 11.2 %collective-permute-start.13 = (bf16[128,1536]{1,0:T(8,128)(2,1)}, bf16[128,1536]{1,0:T(8,128)(2,1)S(1)}, u32[]{:S(2)}, u32[]{:S(2)}) collective-permute-start(bf16[128,1536]{1,0:T(8,128)(2,1)} %collective-permute-done.12), channel_id=1, source_target_pairs={{1,0},{2,1},{3,2},{5,4},{6,5},{7,6},{9,8},{10,9},{11,10},{13,12},{... | collective-permute-start | bytes 1179656 | tf_op jit(solution)/shard_map/ppermute | solution.py:646
  212.2 12.7 %collective-permute-start.15 = (bf16[128,1536]{1,0:T(8,128)(2,1)}, bf16[128,1536]{1,0:T(8,128)(2,1)S(1)}, u32[]{:S(2)}, u32[]{:S(2)}) collective-permute-start(bf16[128,1536]{1,0:T(8,128)(2,1)} %collective-permute-done.14), channel_id=1, source_target_pairs={{0,1},{1,2},{2,3},{4,5},{5,6},{6,7},{8,9},{9,10},{10,11},{12,13},{... | collective-permute-start | bytes 1179656 | tf_op jit(solution)/shard_map/ppermute | solution.py:646
  226.7 40.5 %collective-permute-start.16 = (bf16[4,2,128,1536]{3,2,1,0:T(8,128)(2,1)}, bf16[4,2,128,1536]{3,2,1,0:T(8,128)(2,1)}, u32[]{:S(2)}, u32[]{:S(2)}) collective-permute-start(bf16[4,2,128,1536]{3,2,1,0:T(8,128)(2,1)} %bitcast_dynamic-update-slice_fusion.16), channel_id=1, source_target_pairs={{0,4},{4,0},{1,5},{5,1},{2,6},{6,2},{3,7},{7,3},{8,12},{12,8},{9,1... | collective-permute-start | bytes 9437192 | tf_op jit(solution)/shard_map/ppermute | solution.py:725
  233.0 34.3 %collective-permute-start.24 = (f32[4,16,256]{1,2,0:T(8,128)S(1)}, f32[4,16,256]{1,2,0:T(8,128)S(1)}, u32[]{:S(2)}, u32[]{:S(2)}) collective-permute-start(f32[4,16,256]{1,2,0:T(8,128)S(1)} %constant_dynamic-update-slice_fusion.4), channel_id=1, source_target_pairs={{0,4},{4,0},{1,5},{5,1},{2,6},{6,2},{3,7},{7,3},{8,12},{12,8},{9,1... | collective-permute-start | bytes 196616 | tf_op jit(solution)/shard_map/ppermute | solution.py:725
  339.8 76.1 %all-to-all-start.1 = ((bf16[4,2,128,1536]{3,2,1,0:T(8,128)(2,1)}), bf16[4,2,128,1536]{3,2,1,0:T(8,128)(2,1)}, u32[]{:S(2)}, u32[]{:S(2)}) async-start(bf16[4,2,128,1536]{3,2,1,0:T(8,128)(2,1)} %bitcast.269), calls=%async_computation.1 | async-start | bytes 6291456 | tf_op jit(solution)/shard_map/all_to_all | solution.py:633
  344.5 353.8 %reduce-scatter.6.cloned.1.call-start = ((), (), s32[]{:S(2)}) async-start(), calls=%async_computation.9 | async-start | bytes 7962624 | tf_op jit(solution)/shard_map/reduce_scatter | solution.py:806
  422.2 43.1 %collective-permute-start.28 = (bf16[128,1536]{1,0:T(8,128)(2,1)}, bf16[128,1536]{1,0:T(8,128)(2,1)}, u32[]{:S(2)}, u32[]{:S(2)}) collective-permute-start(bf16[128,1536]{1,0:T(8,128)(2,1)} %get-tuple-element.352), channel_id=1, source_target_pairs={{0,1},{1,2},{2,3},{4,5},{5,6},{6,7},{8,9},{9,10},{10,11},{12,13},{... | collective-permute-start | bytes 1179656 | tf_op jit(solution)/shard_map/ppermute | solution.py:646
  424.3 26.9 %collective-permute-start.29 = (bf16[128,1536]{1,0:T(8,128)(2,1)}, bf16[128,1536]{1,0:T(8,128)(2,1)}, u32[]{:S(2)}, u32[]{:S(2)}) collective-permute-start(bf16[128,1536]{1,0:T(8,128)(2,1)} %get-tuple-element.352), channel_id=1, source_target_pairs={{1,0},{2,1},{3,2},{5,4},{6,5},{7,6},{9,8},{10,9},{11,10},{13,12},{... | collective-permute-start | bytes 1179656 | tf_op jit(solution)/shard_map/ppermute | solution.py:646
  425.6 16.0 %collective-permute-start.40 = (f32[2,128]{1,0:T(2,128)S(1)}, f32[2,128]{1,0:T(2,128)S(1)}, u32[]{:S(2)}, u32[]{:S(2)}) collective-permute-start(f32[2,128]{1,0:T(2,128)S(1)} %fusion.48), channel_id=1, source_target_pairs={{0,1},{1,2},{2,3},{4,5},{5,6},{6,7},{8,9},{9,10},{10,11},{12,13},{... | collective-permute-start | bytes 3080 | tf_op jit(solution)/shard_map/ppermute | solution.py:646
  430.1 10.1 %collective-permute-start.41 = (f32[2,128]{1,0:T(2,128)S(1)}, f32[2,128]{1,0:T(2,128)S(1)}, u32[]{:S(2)}, u32[]{:S(2)}) collective-permute-start(f32[2,128]{1,0:T(2,128)S(1)} %fusion.48), channel_id=1, source_target_pairs={{1,0},{2,1},{3,2},{5,4},{6,5},{7,6},{9,8},{10,9},{11,10},{13,12},{... | collective-permute-start | bytes 3080 | tf_op jit(solution)/shard_map/ppermute | solution.py:646
  434.1 37.2 %collective-permute-start.34 = (bf16[128,1536]{1,0:T(8,128)(2,1)}, bf16[128,1536]{1,0:T(8,128)(2,1)}, u32[]{:S(2)}, u32[]{:S(2)}) collective-permute-start(bf16[128,1536]{1,0:T(8,128)(2,1)} %get-tuple-element.351), channel_id=1, source_target_pairs={{0,1},{1,2},{2,3},{4,5},{5,6},{6,7},{8,9},{9,10},{10,11},{12,13},{... | collective-permute-start | bytes 1179656 | tf_op jit(solution)/shard_map/ppermute | solution.py:646
  448.5 21.5 %collective-permute-start.35 = (bf16[128,1536]{1,0:T(8,128)(2,1)}, bf16[128,1536]{1,0:T(8,128)(2,1)}, u32[]{:S(2)}, u32[]{:S(2)}) collective-permute-start(bf16[128,1536]{1,0:T(8,128)(2,1)} %get-tuple-element.351), channel_id=1, source_target_pairs={{1,0},{2,1},{3,2},{5,4},{6,5},{7,6},{9,8},{10,9},{11,10},{13,12},{... | collective-permute-start | bytes 1179656 | tf_op jit(solution)/shard_map/ppermute | solution.py:646
  449.8 13.0 %collective-permute-start.43 = (f32[2,128]{1,0:T(2,128)S(1)}, f32[2,128]{1,0:T(2,128)S(1)}, u32[]{:S(2)}, u32[]{:S(2)}) collective-permute-start(f32[2,128]{1,0:T(2,128)S(1)} %collective-permute-done.42), channel_id=1, source_target_pairs={{1,0},{2,1},{3,2},{5,4},{6,5},{7,6},{9,8},{10,9},{11,10},{13,12},{... | collective-permute-start | bytes 3080 | tf_op jit(solution)/shard_map/ppermute | solution.py:646
  451.2 25.5 %collective-permute-start.30 = (bf16[128,1536]{1,0:T(8,128)(2,1)}, bf16[128,1536]{1,0:T(8,128)(2,1)}, u32[]{:S(2)}, u32[]{:S(2)}) collective-permute-start(bf16[128,1536]{1,0:T(8,128)(2,1)} %collective-permute-done.29), channel_id=1, source_target_pairs={{1,0},{2,1},{3,2},{5,4},{6,5},{7,6},{9,8},{10,9},{11,10},{13,12},{... | collective-permute-start | bytes 1179656 | tf_op jit(solution)/shard_map/ppermute | solution.py:646
  462.8 15.1 %collective-permute-start.45 = (f32[2,128]{1,0:T(2,128)S(1)}, f32[2,128]{1,0:T(2,128)S(1)}, u32[]{:S(2)}, u32[]{:S(2)}) collective-permute-start(f32[2,128]{1,0:T(2,128)S(1)} %collective-permute-done.44), channel_id=1, source_target_pairs={{0,1},{1,2},{2,3},{4,5},{5,6},{6,7},{8,9},{9,10},{10,11},{12,13},{... | collective-permute-start | bytes 3080 | tf_op jit(solution)/shard_map/ppermute | solution.py:646
  465.4 19.0 %collective-permute-start.32 = (bf16[128,1536]{1,0:T(8,128)(2,1)}, bf16[128,1536]{1,0:T(8,128)(2,1)}, u32[]{:S(2)}, u32[]{:S(2)}) collective-permute-start(bf16[128,1536]{1,0:T(8,128)(2,1)} %collective-permute-done.28), channel_id=1, source_target_pairs={{0,1},{1,2},{2,3},{4,5},{5,6},{6,7},{8,9},{9,10},{10,11},{12,13},{... | collective-permute-start | bytes 1179656 | tf_op jit(solution)/shard_map/ppermute | solution.py:646
  470.0 18.9 %collective-permute-start.36 = (bf16[128,1536]{1,0:T(8,128)(2,1)}, bf16[128,1536]{1,0:T(8,128)(2,1)}, u32[]{:S(2)}, u32[]{:S(2)}) collective-permute-start(bf16[128,1536]{1,0:T(8,128)(2,1)} %collective-permute-done.35), channel_id=1, source_target_pairs={{1,0},{2,1},{3,2},{5,4},{6,5},{7,6},{9,8},{10,9},{11,10},{13,12},{... | collective-permute-start | bytes 1179656 | tf_op jit(solution)/shard_map/ppermute | solution.py:646
  471.3 18.9 %collective-permute-start.38 = (bf16[128,1536]{1,0:T(8,128)(2,1)}, bf16[128,1536]{1,0:T(8,128)(2,1)}, u32[]{:S(2)}, u32[]{:S(2)}) collective-permute-start(bf16[128,1536]{1,0:T(8,128)(2,1)} %collective-permute-done.34), channel_id=1, source_target_pairs={{0,1},{1,2},{2,3},{4,5},{5,6},{6,7},{8,9},{9,10},{10,11},{12,13},{... | collective-permute-start | bytes 1179656 | tf_op jit(solution)/shard_map/ppermute | solution.py:646
  476.7 18.2 %collective-permute-start.31 = (bf16[128,1536]{1,0:T(8,128)(2,1)}, bf16[128,1536]{1,0:T(8,128)(2,1)}, u32[]{:S(2)}, u32[]{:S(2)}) collective-permute-start(bf16[128,1536]{1,0:T(8,128)(2,1)} %collective-permute-done.30), channel_id=1, source_target_pairs={{1,0},{2,1},{3,2},{5,4},{6,5},{7,6},{9,8},{10,9},{11,10},{13,12},{... | collective-permute-start | bytes 1179656 | tf_op jit(solution)/shard_map/ppermute | solution.py:646
  484.4 14.2 %collective-permute-start.33 = (bf16[128,1536]{1,0:T(8,128)(2,1)}, bf16[128,1536]{1,0:T(8,128)(2,1)S(1)}, u32[]{:S(2)}, u32[]{:S(2)}) collective-permute-start(bf16[128,1536]{1,0:T(8,128)(2,1)} %collective-permute-done.32), channel_id=1, source_target_pairs={{0,1},{1,2},{2,3},{4,5},{5,6},{6,7},{8,9},{9,10},{10,11},{12,13},{... | collective-permute-start | bytes 1179656 | tf_op jit(solution)/shard_map/ppermute | solution.py:646
  488.9 12.2 %collective-permute-start.37 = (bf16[128,1536]{1,0:T(8,128)(2,1)}, bf16[128,1536]{1,0:T(8,128)(2,1)S(1)}, u32[]{:S(2)}, u32[]{:S(2)}) collective-permute-start(bf16[128,1536]{1,0:T(8,128)(2,1)} %collective-permute-done.36), channel_id=1, source_target_pairs={{1,0},{2,1},{3,2},{5,4},{6,5},{7,6},{9,8},{10,9},{11,10},{13,12},{... | collective-permute-start | bytes 1179656 | tf_op jit(solution)/shard_map/ppermute | solution.py:646
  490.2 13.6 %collective-permute-start.39 = (bf16[128,1536]{1,0:T(8,128)(2,1)}, bf16[128,1536]{1,0:T(8,128)(2,1)S(1)}, u32[]{:S(2)}, u32[]{:S(2)}) collective-permute-start(bf16[128,1536]{1,0:T(8,128)(2,1)} %collective-permute-done.38), channel_id=1, source_target_pairs={{0,1},{1,2},{2,3},{4,5},{5,6},{6,7},{8,9},{9,10},{10,11},{12,13},{... | collective-permute-start | bytes 1179656 | tf_op jit(solution)/shard_map/ppermute | solution.py:646
  537.4 67.0 %all-to-all-start.2 = ((bf16[4,2,128,1536]{3,2,1,0:T(8,128)(2,1)}), bf16[4,2,128,1536]{3,2,1,0:T(8,128)(2,1)}, u32[]{:S(2)}, u32[]{:S(2)}) async-start(bf16[4,2,128,1536]{3,2,1,0:T(8,128)(2,1)} %bitcast.266), calls=%async_computation.3 | async-start | bytes 6291456 | tf_op jit(solution)/shard_map/all_to_all | solution.py:633
  621.0 74.8 %all-to-all-start.3 = ((bf16[4,2,128,1536]{3,2,1,0:T(8,128)(2,1)}), bf16[4,2,128,1536]{3,2,1,0:T(8,128)(2,1)}, u32[]{:S(2)}, u32[]{:S(2)}) async-start(bf16[4,2,128,1536]{3,2,1,0:T(8,128)(2,1)} %get-tuple-element.333), calls=%async_computation.4 | async-start | bytes 6291456 | tf_op jit(solution)/shard_map/all_to_all | solution.py:633
  625.9 95.0 %reduce-scatter.8.cloned.1.call-start = ((), (), s32[]{:S(2)}) async-start(), calls=%async_computation.10 | async-start | bytes 4423680 | tf_op jit(solution)/shard_map/reduce_scatter | solution.py:806
  703.8 83.1 %collective-permute-start.48 = (bf16[128,1536]{1,0:T(8,128)(2,1)}, bf16[128,1536]{1,0:T(8,128)(2,1)}, u32[]{:S(2)}, u32[]{:S(2)}) collective-permute-start(bf16[128,1536]{1,0:T(8,128)(2,1)} %get-tuple-element.350), channel_id=1, source_target_pairs={{0,1},{1,2},{2,3},{4,5},{5,6},{6,7},{8,9},{9,10},{10,11},{12,13},{... | collective-permute-start | bytes 1179656 | tf_op jit(solution)/shard_map/ppermute | solution.py:646
  705.9 78.0 %collective-permute-start.49 = (bf16[128,1536]{1,0:T(8,128)(2,1)}, bf16[128,1536]{1,0:T(8,128)(2,1)}, u32[]{:S(2)}, u32[]{:S(2)}) collective-permute-start(bf16[128,1536]{1,0:T(8,128)(2,1)} %get-tuple-element.350), channel_id=1, source_target_pairs={{1,0},{2,1},{3,2},{5,4},{6,5},{7,6},{9,8},{10,9},{11,10},{13,12},{... | collective-permute-start | bytes 1179656 | tf_op jit(solution)/shard_map/ppermute | solution.py:646
  707.2 86.3 %collective-permute-start.54 = (bf16[128,1536]{1,0:T(8,128)(2,1)}, bf16[128,1536]{1,0:T(8,128)(2,1)}, u32[]{:S(2)}, u32[]{:S(2)}) collective-permute-start(bf16[128,1536]{1,0:T(8,128)(2,1)} %get-tuple-element.349), channel_id=1, source_target_pairs={{0,1},{1,2},{2,3},{4,5},{5,6},{6,7},{8,9},{9,10},{10,11},{12,13},{... | collective-permute-start | bytes 1179656 | tf_op jit(solution)/shard_map/ppermute | solution.py:646
  712.5 79.7 %collective-permute-start.55 = (bf16[128,1536]{1,0:T(8,128)(2,1)}, bf16[128,1536]{1,0:T(8,128)(2,1)S(1)}, u32[]{:S(2)}, u32[]{:S(2)}) collective-permute-start(bf16[128,1536]{1,0:T(8,128)(2,1)} %get-tuple-element.349), channel_id=1, source_target_pairs={{1,0},{2,1},{3,2},{5,4},{6,5},{7,6},{9,8},{10,9},{11,10},{13,12},{... | collective-permute-start | bytes 1179656 | tf_op jit(solution)/shard_map/ppermute | solution.py:646
  715.7 158.9 %all-to-all-start.4 = ((bf16[4,2,128,1536]{3,2,1,0:T(8,128)(2,1)}), bf16[4,2,128,1536]{3,2,1,0:T(8,128)(2,1)}, u32[]{:S(2)}, u32[]{:S(2)}) async-start(bf16[4,2,128,1536]{3,2,1,0:T(8,128)(2,1)} %broadcast_in_dim.178), calls=%async_computation.6 | async-start | bytes 6291456 | tf_op jit(solution)/shard_map/all_to_all | solution.py:639
  722.8 55.9 %collective-permute-start.60 = (f32[192,384]{1,0:T(8,128)S(1)}, f32[192,384]{1,0:T(8,128)S(1)}, u32[]{:S(2)}, u32[]{:S(2)}) collective-permute-start(f32[192,384]{1,0:T(8,128)S(1)} %pad_maximum_fusion.4), channel_id=1, source_target_pairs={{0,1},{1,0},{2,3},{3,2},{4,5},{5,4},{6,7},{7,6},{8,9},{9,8},{10,11... | collective-permute-start | bytes 884744 | tf_op jit(solution)/shard_map/ppermute | solution.py:694
  778.8 29.1 %collective-permute-start.61 = (f32[192,384]{1,0:T(8,128)S(1)}, f32[192,384]{1,0:T(8,128)S(1)}, u32[]{:S(2)}, u32[]{:S(2)}) collective-permute-start(f32[192,384]{1,0:T(8,128)S(1)} %fusion.57), channel_id=1, source_target_pairs={{0,2},{1,3},{2,0},{3,1},{4,6},{5,7},{6,4},{7,5},{8,10},{9,11},{10,... | collective-permute-start | bytes 884744 | tf_op jit(solution)/shard_map/ppermute | solution.py:694
  783.9 29.2 %collective-permute-start.50 = (bf16[128,1536]{1,0:T(8,128)(2,1)}, bf16[128,1536]{1,0:T(8,128)(2,1)}, u32[]{:S(2)}, u32[]{:S(2)}) collective-permute-start(bf16[128,1536]{1,0:T(8,128)(2,1)} %collective-permute-done.49), channel_id=1, source_target_pairs={{1,0},{2,1},{3,2},{5,4},{6,5},{7,6},{9,8},{10,9},{11,10},{13,12},{... | collective-permute-start | bytes 1179656 | tf_op jit(solution)/shard_map/ppermute | solution.py:646
  786.9 30.2 %collective-permute-start.52 = (bf16[128,1536]{1,0:T(8,128)(2,1)}, bf16[128,1536]{1,0:T(8,128)(2,1)}, u32[]{:S(2)}, u32[]{:S(2)}) collective-permute-start(bf16[128,1536]{1,0:T(8,128)(2,1)} %collective-permute-done.48), channel_id=1, source_target_pairs={{0,1},{1,2},{2,3},{4,5},{5,6},{6,7},{8,9},{9,10},{10,11},{12,13},{... | collective-permute-start | bytes 1179656 | tf_op jit(solution)/shard_map/ppermute | solution.py:646
  792.2 31.2 %collective-permute-start.56 = (bf16[128,1536]{1,0:T(8,128)(2,1)S(1)}, bf16[128,1536]{1,0:T(8,128)(2,1)}, u32[]{:S(2)}, u32[]{:S(2)}) collective-permute-start(bf16[128,1536]{1,0:T(8,128)(2,1)S(1)} %collective-permute-done.55), channel_id=1, source_target_pairs={{1,0},{2,1},{3,2},{5,4},{6,5},{7,6},{9,8},{10,9},{11,10},{13,12},{... | collective-permute-start | bytes 1179656 | tf_op jit(solution)/shard_map/ppermute | solution.py:646
  793.5 31.2 %collective-permute-start.58 = (bf16[128,1536]{1,0:T(8,128)(2,1)}, bf16[128,1536]{1,0:T(8,128)(2,1)}, u32[]{:S(2)}, u32[]{:S(2)}) collective-permute-start(bf16[128,1536]{1,0:T(8,128)(2,1)} %collective-permute-done.54), channel_id=1, source_target_pairs={{0,1},{1,2},{2,3},{4,5},{5,6},{6,7},{8,9},{9,10},{10,11},{12,13},{... | collective-permute-start | bytes 1179656 | tf_op jit(solution)/shard_map/ppermute | solution.py:646
  807.9 21.7 %collective-permute-start.62 = (f32[192,384]{1,0:T(8,128)S(1)}, f32[192,384]{1,0:T(8,128)S(1)}, u32[]{:S(2)}, u32[]{:S(2)}) collective-permute-start(f32[192,384]{1,0:T(8,128)S(1)} %add.310), channel_id=1, source_target_pairs={{0,4},{4,0},{1,5},{5,1},{2,6},{6,2},{3,7},{7,3},{8,12},{12,8},{9,1... | collective-permute-start | bytes 884744 | tf_op jit(solution)/shard_map/ppermute | solution.py:694
  813.1 17.9 %collective-permute-start.51 = (bf16[128,1536]{1,0:T(8,128)(2,1)}, bf16[128,1536]{1,0:T(8,128)(2,1)}, u32[]{:S(2)}, u32[]{:S(2)}) collective-permute-start(bf16[128,1536]{1,0:T(8,128)(2,1)} %collective-permute-done.50), channel_id=1, source_target_pairs={{1,0},{2,1},{3,2},{5,4},{6,5},{7,6},{9,8},{10,9},{11,10},{13,12},{... | collective-permute-start | bytes 1179656 | tf_op jit(solution)/shard_map/ppermute | solution.py:646
  817.1 16.2 %collective-permute-start.53 = (bf16[128,1536]{1,0:T(8,128)(2,1)}, bf16[128,1536]{1,0:T(8,128)(2,1)S(1)}, u32[]{:S(2)}, u32[]{:S(2)}) collective-permute-start(bf16[128,1536]{1,0:T(8,128)(2,1)} %collective-permute-done.52), channel_id=1, source_target_pairs={{0,1},{1,2},{2,3},{4,5},{5,6},{6,7},{8,9},{9,10},{10,11},{12,13},{... | collective-permute-start | bytes 1179656 | tf_op jit(solution)/shard_map/ppermute | solution.py:646
  823.4 17.9 %collective-permute-start.57 = (bf16[128,1536]{1,0:T(8,128)(2,1)}, bf16[128,1536]{1,0:T(8,128)(2,1)S(1)}, u32[]{:S(2)}, u32[]{:S(2)}) collective-permute-start(bf16[128,1536]{1,0:T(8,128)(2,1)} %collective-permute-done.56), channel_id=1, source_target_pairs={{1,0},{2,1},{3,2},{5,4},{6,5},{7,6},{9,8},{10,9},{11,10},{13,12},{... | collective-permute-start | bytes 1179656 | tf_op jit(solution)/shard_map/ppermute | solution.py:646
  824.7 17.8 %collective-permute-start.59 = (bf16[128,1536]{1,0:T(8,128)(2,1)}, bf16[128,1536]{1,0:T(8,128)(2,1)S(1)}, u32[]{:S(2)}, u32[]{:S(2)}) collective-permute-start(bf16[128,1536]{1,0:T(8,128)(2,1)} %collective-permute-done.58), channel_id=1, source_target_pairs={{0,1},{1,2},{2,3},{4,5},{5,6},{6,7},{8,9},{9,10},{10,11},{12,13},{... | collective-permute-start | bytes 1179656 | tf_op jit(solution)/shard_map/ppermute | solution.py:646
  829.6 10.6 %collective-permute-start.63 = (f32[384,384]{1,0:T(8,128)S(1)}, f32[384,384]{1,0:T(8,128)S(1)}, u32[]{:S(2)}, u32[]{:S(2)}) collective-permute-start(f32[384,384]{1,0:T(8,128)S(1)} %maximum_select_fusion.2), channel_id=1, source_target_pairs={{0,8},{8,0},{16,24},{24,16},{1,9},{9,1},{17,25},{25,17},{2,10},{10... | collective-permute-start | bytes 1769480 | tf_op jit(solution)/shard_map/ppermute | solution.py:694
  840.3 22.4 %collective-permute-start.64 = (f32[768,384]{1,0:T(8,128)S(1)}, f32[768,384]{1,0:T(8,128)S(1)}, u32[]{:S(2)}, u32[]{:S(2)}) collective-permute-start(f32[768,384]{1,0:T(8,128)S(1)} %maximum_select_fusion.1), channel_id=1, source_target_pairs={{0,16},{8,24},{16,0},{24,8},{1,17},{9,25},{17,1},{25,9},{2,18},{10... | collective-permute-start | bytes 3538952 | tf_op jit(solution)/shard_map/ppermute | solution.py:694
  (54 other events, 637.2 us)
Sparse Core Ops, SparseCore 0:
  328.2 95.0 reduce-scatter.3
  537.5 64.2 reduce-scatter.5
  656.7 51.3 reduce-scatter.7

commit v3 on v2

--- a/solution.py
+++ b/solution.py
@@ -133,12 +133,14 @@
     size = enter_ref.shape[0]
     mixed = joined(mixed_in).astype(f32)
     act = joined(act_in)
+    terms = joined(slope_in).astype(f32)
+    slope = terms[:, 0:1] + terms[:, 1:2]
     gate = joined(z)
     sigma = jax.nn.sigmoid(gate)
     silu = gate * sigma
     gated = mixed * silu
     low_grad = dot_nt(joined(push), w_out[...])
-    gated_grad = low_grad * gain[...] + 2.0 * gated * joined(slope_in)
+    gated_grad = low_grad * gain[...] + 2.0 * gated * slope
     dy = gated_grad * silu
     dy_ref[...] = dy.astype(bf16).reshape(dy_ref.shape)
     dz_ref[...] = (gated_grad * mixed * (sigma + silu * (1.0 - sigma))).astype(bf16).reshape(dz_ref.shape)
@@ -369,7 +371,7 @@
     )(y, act, z, decay, lead, entering, skip, gain, w_out)
 
 
-def gate_backward(push, w_out, mixed, z, act, decay, lead, slope, gain):
+def gate_backward(push, w_out, mixed, z, act, decay, lead, gain):
     shares, batch, share, inner = mixed.shape
     width, heads, model = act.shape[3], decay.shape[2], w_out.shape[1]
     size = (width - inner) // 2
@@ -385,7 +387,7 @@
             rows_of(share, width),
             in_order(heads),
             at_block(1, inner),
-            rows_of(share, 1),
+            pl.BlockSpec((BLOCK // share, None, share, 128), lambda b, k: (k, b, 0, model // 128)),
             only(1, inner),
         ],
         out_specs=[rows_of(share, inner), rows_of(share, inner), each(size, inner), only(8, inner)],
@@ -399,7 +401,7 @@
         cost_estimate=cost(
             2 * batch * tokens * inner * (model + size), batch * tokens * inner * 18, batch * tokens * inner
         ),
-    )(push, w_out, mixed, z, act, decay, lead, slope, gain)
+    )(push, w_out, mixed, z, act, decay, lead, push, gain)
 
 
 def scan_backward(cin, edge, taps, raw, bias, decay, decay_t, act, dy, start, lead, entering, leave_grad, skip):
@@ -450,8 +452,39 @@
     )(cin, cin, edge, taps, raw, bias, decay, decay_t, act, dy, start, lead, entering, leave_grad, skip)
 
 
-def weight_grads(groups, tile, extra=None):
-    depth = groups[0][0][0].shape[1]
+def end_rows(in_grad, last, following, taps):
+    shares, batch, share, width = in_grad.shape
+    columns = last.shape[2]
+
+    def kernel(rows, last_ref, next_ref, taps_ref, out_ref, buf):
+        for b in range(batch):
+            buf[0:8, :] = jnp.zeros((8, columns), f32)
+            buf[8:16, :] = next_ref[b]
+            added = sum(taps_ref[k : k + 1, :] * buf[3 - k : 11 - k, :] for k in range(4))
+            old = rows[b].astype(f32)
+            end = jnp.concatenate([last_ref[b] + added, old[8:, columns:]], axis=1)
+            out_ref[b] = jnp.concatenate([old[:8], end], axis=0).astype(bf16)
+
+    block = pl.BlockSpec((None, batch, 16, width), lambda i: (shares - 1, 0, share // 16 - 1, 0))
+
+    def whole(array):
+        zeros = (0,) * array.ndim
+        return pl.BlockSpec(array.shape, lambda i: zeros)
+
+    return pl.pallas_call(
+        kernel,
+        grid=(1,),
+        in_specs=[block, whole(last), whole(following), whole(taps)],
+        out_specs=block,
+        out_shape=made(*in_grad.shape),
+        input_output_aliases={0: 0},
+        scratch_shapes=[pltpu.VMEM((16, columns), f32)],
+        compiler_params=params(),
+        cost_estimate=cost(16 * width * batch, 200 * width * batch, 0),
+    )(in_grad, last, following, taps)
+
+
+def weight_grads(groups, depth, tile, extra=None):
     rows = groups[0][0][0].shape[0]
     tiles = [group[0][1].shape[1] // tile for group in groups]
     starts = [sum(tiles[:g]) for g in range(len(groups) + 1)]
@@ -507,83 +540,206 @@
     )(*flat)
 
 
-def expert_kernel(shared, x_ref, grad_ref, gates_ref, mine, w_gu, w_down, *refs):
-    if shared:
-        ws_gu, ws_down, out_ref, dx_ref, logit_ref, act_ref, gu_ref, s_act_ref, s_gu_ref = refs
-    else:
-        out_ref, dx_ref, logit_ref, act_ref, gu_ref = refs
-    x, grad, gates = x_ref[...], grad_ref[...], gates_ref[...]
-    wide = grad.astype(f32)
-
-    def back(gate, up, act_push):
-        sigma = jax.nn.sigmoid(gate)
-        silu = gate * sigma
-        slope = sigma + silu * (1.0 - sigma)
-        return silu, jnp.concatenate([act_push * up * slope, act_push * silu], axis=1).astype(bf16)
-
-    out = dx = 0.0
+def gates_of(gates_ref, mine):
+    terms = gates_ref[...].astype(f32)
+    every = mine.shape[1]
+    return terms[:, :every] + terms[:, every : 2 * every]
+
+
+def expert_forward_kernel(shared, x_ref, grad_ref, gates_ref, mine, w_gu, w_down, *refs):
+    out_ref, logit_ref, both_ref = refs[-3:]
+    x = x_ref[...]
+    gates = gates_of(gates_ref, mine)
+    wide = grad_ref[...].astype(f32)
+    out = own = total = 0.0
     width = w_down.shape[1]
-    own = total = 0.0
     for e in range(w_gu.shape[0]):
         weight = jnp.sum(gates * mine[e : e + 1, :], axis=1, keepdims=True)
         both = dot_nn(x, w_gu[e])
+        both_ref[:, 2 * e * width : 2 * (e + 1) * width] = both
         gate, up = both[:, :width], both[:, width:]
-        act_push = dot_nt((weight * wide).astype(bf16), w_down[e])
-        silu, gu_grad = back(gate, up, act_push)
-        act = (silu * up).astype(bf16)
-        act_ref[:, e * width : (e + 1) * width] = (weight * act.astype(f32)).astype(bf16)
-        gu_ref[:, 2 * e * width : 2 * (e + 1) * width] = gu_grad
+        act = (gate * jax.nn.sigmoid(gate) * up).astype(bf16)
         result = dot_nn(act, w_down[e]).astype(bf16).astype(f32)
         push = jnp.sum(wide * result, axis=1, keepdims=True)
         own = own + push * mine[e : e + 1, :]
         total = total + weight * push
         out = out + weight * result
+    if shared:
+        ws_gu, ws_down = refs[:2]
+        first, ff = 2 * w_gu.shape[0] * width, ws_down.shape[0]
+        gate, up = dot_nn(x, ws_gu[0]), dot_nn(x, ws_gu[1])
+        both_ref[:, first : first + ff] = gate
+        both_ref[:, first + ff :] = up
+        act = (gate * jax.nn.sigmoid(gate) * up).astype(bf16)
+        out = out + dot_nn(act, ws_down[...])
+    out_ref[...] = out.astype(bf16)
+    logit_ref[...] = gates * (own - total)
+
+
+def expert_backward_kernel(shared, grad_ref, gates_ref, both_ref, mine, w_gu, w_down, *refs):
+    grad = grad_ref[...]
+    gates = gates_of(gates_ref, mine)
+    wide = grad.astype(f32)
+    dx_ref, act_ref, gu_ref = refs[2:5] if shared else refs
+
+    def back(gate, up, act_push):
+        sigma = jax.nn.sigmoid(gate)
+        silu = gate * sigma
+        slope = sigma + silu * (1.0 - sigma)
+        gu_grad = jnp.concatenate([act_push * up * slope, act_push * silu], axis=1).astype(bf16)
+        return (silu * up).astype(bf16), gu_grad
+
+    dx = 0.0
+    width = w_down.shape[1]
+    for e in range(w_gu.shape[0]):
+        weight = jnp.sum(gates * mine[e : e + 1, :], axis=1, keepdims=True)
+        act_push = dot_nt((weight * wide).astype(bf16), w_down[e])
+        middle = (2 * e + 1) * width
+        gate, up = both_ref[:, middle - width : middle], both_ref[:, middle : middle + width]
+        act, gu_grad = back(gate, up, act_push)
+        act_ref[:, e * width : (e + 1) * width] = (weight * act.astype(f32)).astype(bf16)
+        gu_ref[:, middle - width : middle + width] = gu_grad
         dx = dx + dot_nt(gu_grad, w_gu[e]).astype(bf16).astype(f32)
     if shared:
-        width = ws_down.shape[0]
-        gate, up = dot_nn(x, ws_gu[0]), dot_nn(x, ws_gu[1])
-        silu, gu_grad = back(gate, up, dot_nt(grad, ws_down[...]))
-        act = (silu * up).astype(bf16)
+        ws_gu, ws_down = refs[:2]
+        s_act_ref, s_gu_ref = refs[5:]
+        first, ff = 2 * w_gu.shape[0] * width, ws_down.shape[0]
+        gate, up = both_ref[:, first : first + ff], both_ref[:, first + ff :]
+        act, gu_grad = back(gate, up, dot_nt(grad, ws_down[...]))
         s_act_ref[...] = act
         s_gu_ref[...] = gu_grad
-        out = out + dot_nn(act, ws_down[...])
-        dx = dx + dot_nt(gu_grad[:, :width], ws_gu[0]) + dot_nt(gu_grad[:, width:], ws_gu[1])
-    out_ref[...] = out.astype(bf16)
+        dx = dx + dot_nt(gu_grad[:, :ff], ws_gu[0]) + dot_nt(gu_grad[:, ff:], ws_gu[1])
     dx_ref[...] = dx.astype(bf16)
-    logit_ref[...] = gates * (own - total)
-
-
-def experts(x, grad, gates, mine, w_gu, w_down, shared=()):
-    rows, model = x.shape
-    count, _, double = w_gu.shape
-    width = double // 2
-    every = gates.shape[1]
-
-    def row(columns):
-        return pl.BlockSpec((ROWS, columns), lambda i: (i, 0))
-
-    def whole(array):
-        zeros = (0,) * array.ndim
-        return pl.BlockSpec(array.shape, lambda i: zeros, pipeline_mode=pl.Buffered(1))
-
-    widths = [model, model, every, count * width, count * double]
-    hidden = count * width
+
+
+def by_rows(columns, at=0):
+    return pl.BlockSpec((ROWS, columns), lambda i: (i, at))
+
+
+def kept(array):
+    zeros = (0,) * array.ndim
+    return pl.BlockSpec(array.shape, lambda i: zeros, pipeline_mode=pl.Buffered(1))
+
+
+def experts_forward(x, grad, mine, w_gu, w_down, shared=()):
+    rows = x.shape[0]
+    count, model, double = w_gu.shape
+    beside = x.shape[1] - model
+    every = mine.shape[1]
+    hidden = count * double + (2 * shared[1].shape[0] if shared else 0)
+    return pl.pallas_call(
+        lambda *refs: expert_forward_kernel(bool(shared), *refs),
+        grid=(rows // ROWS,),
+        in_specs=[by_rows(model), by_rows(model), by_rows(beside, model // beside)]
+        + [kept(w) for w in (mine, w_gu, w_down, *shared)],
+        out_specs=[by_rows(model), by_rows(every), by_rows(hidden)],
+        out_shape=[made(rows, model), made(rows, every, kind=f32), made(rows, hidden, kind=f32)],
+        compiler_params=params(),
+        cost_estimate=cost(3 * rows * hidden * model, 3 * hidden * model + rows * (6 * model + 4 * hidden), rows * hidden),
+    )(x, grad, x, mine, w_gu, w_down, *shared)
+
+
+def experts_backward(x, grad, both, mine, w_gu, w_down, shared=()):
+    rows = x.shape[0]
+    count, model, double = w_gu.shape
+    beside = x.shape[1] - model
+    hidden = both.shape[1]
+    widths = [model, count * double // 2, count * double]
     if shared:
-        ff = shared[1].shape[0]
-        hidden += ff
-        widths += [ff, 2 * ff]
+        widths += [shared[1].shape[0], 2 * shared[1].shape[0]]
     return pl.pallas_call(
-        lambda *refs: expert_kernel(bool(shared), *refs),
+        lambda *refs: expert_backward_kernel(bool(shared), *refs),
         grid=(rows // ROWS,),
-        in_specs=[row(model), row(model), row(every), whole(mine), whole(w_gu), whole(w_down)]
-        + [whole(w) for w in shared],
-        out_specs=[row(w) for w in widths],
-        out_shape=[made(rows, w, kind=f32 if i == 2 else bf16) for i, w in enumerate(widths)],
+        in_specs=[by_rows(model), by_rows(beside, model // beside), by_rows(hidden)]
+        + [kept(w) for w in (mine, w_gu, w_down, *shared)],
+        out_specs=[by_rows(w) for w in widths],
+        out_shape=[made(rows, w) for w in widths],
         compiler_params=params(),
-        cost_estimate=cost(
-            rows * hidden * model * 12, 6 * hidden * model + rows * (8 * model + 6 * hidden), rows * hidden
-        ),
-    )(x, grad, gates, mine, w_gu, w_down, *shared)
+        cost_estimate=cost(3 * rows * hidden * model, 3 * hidden * model + rows * (4 * model + 7 * hidden), rows * hidden),
+    )(grad, x, both, mine, w_gu, w_down, *shared)
+
+
+def summed(got):
+    return sum(got[i].astype(f32) for i in range(got.shape[0]))
+
+
+def two_terms(values, width):
+    high = values.astype(bf16)
+    low = (values - high.astype(f32)).astype(bf16)
+    terms, room = [high, low], width - 2 * values.shape[1]
+    if room:
+        terms.append(jnp.zeros((values.shape[0], room), bf16))
+    return jnp.concatenate(terms, axis=1)
+
+
+def after_mix_kernel(inner, got, x, squares, used, gain, router, packed_ref, hidden_ref, mix_ref, scale_ref):
+    model = x.shape[1]
+    mix = summed(got)
+    gate_scale = lax.rsqrt(squares[...] / inner + norm_eps)
+    hidden = x[...].astype(f32) + mix * gate_scale
+    scale = lax.rsqrt(jnp.mean(hidden * hidden, axis=1, keepdims=True) + norm_eps)
+    normed = (hidden * scale * gain[...]).astype(bf16)
+    mask = used[...] > 0.0
+    logits = jnp.where(mask, dot_nn(normed, router[...]), -1e30)
+    powers = jnp.where(mask, jnp.exp(logits - jnp.max(logits, axis=1, keepdims=True)), 0.0)
+    gates = powers / jnp.sum(powers, axis=1, keepdims=True)
+    packed_ref[:, :model] = normed
+    packed_ref[:, model:] = two_terms(gates, packed_ref.shape[1] - model)
+    hidden_ref[...] = hidden
+    mix_ref[...] = mix
+    lane = lax.broadcasted_iota(jnp.int32, scale_ref.shape, 1)
+    scale_ref[...] = jnp.where(lane == 0, gate_scale, scale)
+
+
+def after_ffn_kernel(inner, got, hidden_in, mix, scales, grad, gain, packed_ref, grad_ref, sum_ref):
+    model = grad.shape[1]
+    dx, hidden = summed(got), hidden_in[...]
+    gate_scale, scale = scales[:, 0:1], scales[:, 1:2]
+    gained = dx * gain[...]
+    mean = jnp.mean(gained * hidden, axis=1, keepdims=True)
+    hidden_grad = grad[...].astype(f32) + scale * (gained - hidden * (scale * scale * mean))
+    grad_ref[...] = hidden_grad
+    push = jnp.sum(hidden_grad * mix[...], axis=1, keepdims=True)
+    slope = (-0.5 / inner) * push * gate_scale * gate_scale * gate_scale
+    packed_ref[:, :model] = (hidden_grad * gate_scale).astype(bf16)
+    packed_ref[:, model:] = two_terms(slope, packed_ref.shape[1] - model)
+
+    @pl.when(pl.program_id(0) == 0)
+    def _():
+        sum_ref[...] = jnp.zeros_like(sum_ref)
+
+    sum_ref[0:1, :] += jnp.sum(dx * hidden * scale, axis=0, keepdims=True)
+
+
+def after_proj_kernel(got, x_in, hidden_grad, gain, out_ref):
+    dn, x = summed(got), x_in[...].astype(f32)
+    scale = lax.rsqrt(jnp.mean(x * x, axis=1, keepdims=True) + norm_eps)
+    gained = dn * gain[...]
+    mean = jnp.mean(gained * x, axis=1, keepdims=True)
+    out_ref[...] = (hidden_grad[...] + scale * (gained - x * (scale * scale * mean))).astype(bf16)
+
+
+def on_share(kernel, got, rows, wholes, outs, sums=()):
+    shares, batch, share, model = got.shape
+
+    def rows_at(width):
+        return pl.BlockSpec((None, share, width), lambda b: (b, 0, 0))
+
+    def kept_at(shape):
+        return pl.BlockSpec(shape, lambda b: (0, 0))
+
+    return pl.pallas_call(
+        kernel,
+        grid=(batch,),
+        in_specs=[pl.BlockSpec((shares, None, share, model), lambda b: (0, b, 0, 0))]
+        + [rows_at(r.shape[2]) for r in rows]
+        + [kept_at(w.shape) for w in wholes],
+        out_specs=[rows_at(width) for width, _ in outs] + [kept_at(shape) for shape in sums],
+        out_shape=[made(batch, share, width, kind=kind) for width, kind in outs]
+        + [made(*shape, kind=f32) for shape in sums],
+        compiler_params=params(),
+        cost_estimate=cost(40 * batch * share * model, 30 * batch * share * model, batch * share),
+    )(got, *rows, *wholes)
 
 
 def shifted(array, axis, by):
@@ -629,9 +785,8 @@
     return lax.fori_loop(0, count, lap, start)
 
 
-def sum_shares(part):
-    got = lax.all_to_all(part, "head", split_axis=0, concat_axis=0, tiled=True)
-    return jnp.sum(got.astype(f32), axis=0)
+def swap_shares(part):
+    return lax.all_to_all(part, "head", split_axis=0, concat_axis=0, tiled=True)
 
 
 def gather_shares(share):
@@ -639,50 +794,42 @@
     return lax.all_to_all(copies, "head", split_axis=0, concat_axis=0, tiled=True)
 
 
-def relay(parts):
+def relay(part):
     count, place = lax.axis_size("head"), lax.axis_index("head")
 
-    def passed(array, by):
-        return lax.ppermute(
-            array, "head", [(i, i + by) for i in range(count) if 0 <= i + by < count]
-        )
-
-    up, down = [[p] for p in parts], [[p] for p in parts]
+    def passed(array, by, start=0):
+        pairs = [(i, i + by) for i in range(count) if 0 <= i + by < count]
+        pairs = [(i, j) for i, j in pairs if 0 <= i - start * by < count]
+        return lax.ppermute(array, "head", pairs)
+
+    if count == 4:
+        up, down = passed(part, 1), passed(part, -1)
+        far = lax.ppermute(part, "head", [(0, 3), (3, 0)])
+        up_two, down_two = passed(up, 1, 1), passed(down, -1, 1)
+        return [
+            part,
+            jnp.where(place >= 1, up, far),
+            jnp.where(place >= 2, up_two, down_two),
+            jnp.where(place >= 3, far, down),
+        ]
+    up, down = [part], [part]
     for _ in range(count - 1):
-        for k in range(len(parts)):
-            up[k].append(passed(up[k][-1], 1))
-            down[k].append(passed(down[k][-1], -1))
-    return [
-        [p] + [jnp.where(place >= d, up[k][d], down[k][count - d]) for d in range(1, count)]
-        for k, p in enumerate(parts)
-    ]
-
-
-def laid(pieces, lists, shares_first=True):
+        up.append(passed(up[-1], 1))
+        down.append(passed(down[-1], -1))
+    return [part] + [jnp.where(place >= d, up[d], down[count - d]) for d in range(1, count)]
+
+
+def laid(pieces, axis=0):
     count, place = lax.axis_size("head"), lax.axis_index("head")
-    batch_size = len(lists)
-    lead = (count, batch_size) if shares_first else (batch_size, count)
-    out = jnp.zeros(lead + pieces.shape[1:], pieces.dtype)
-    for b, row in enumerate(lists):
-        for d, piece in enumerate(row):
-            slot = (place + count - d) % count
-            at = (slot, b) if shares_first else (b, slot)
-            out = lax.dynamic_update_slice(out, piece[None, None], at + (0,) * piece.ndim)
+    shape = pieces[0].shape[:axis] + (count,) + pieces[0].shape[axis:]
+    out = jnp.zeros(shape, pieces[0].dtype)
+    for d, piece in enumerate(pieces):
+        out = lax.dynamic_update_index_in_dim(out, piece, (place + count - d) % count, axis)
     return out
 
 
-def relay_shares(share, *extras, shares_first=True):
-    batch_size = share.shape[0]
-    lists = relay([share[b] for b in range(batch_size)] + list(extras))
-    whole = laid(share, lists[:batch_size], shares_first)
-    others = []
-    for row in lists[batch_size:]:
-        out = jnp.zeros((len(row),) + row[0].shape, row[0].dtype)
-        for d, piece in enumerate(row):
-            slot = (lax.axis_index("head") + len(row) - d) % len(row)
-            out = lax.dynamic_update_index_in_dim(out, piece, slot, 0)
-        others.append(out)
-    return (whole, *others) if extras else whole
+def relay_shares(share, axis=0):
+    return laid(relay(share), axis)
 
 
 def bits_of(axis):
@@ -781,7 +928,6 @@
     share_rows = tokens // head_count
     rows_all = batch_size * tokens
     conv_width = inner_dev + 2 * state_size
-    edge = conv_taps - 1
 
     def by_share(array):
         array = array.reshape((batch_size, head_count, share_rows) + array.shape[2:])
@@ -816,8 +962,7 @@
     conv_in = times(normed_one, w_conv).astype(bf16)
     step_raw = times(normed_one, w_step)[..., :heads_dev]
     gate_z = times(normed_one, w_in_zx[0])
-    edge_rows = shifted(conv_in[head_count - 1, :, share_rows - edge :], "seq", 1).astype(f32)
-    edge_rows = jnp.pad(edge_rows, ((0, 0), (8 - edge, 0), (0, 0)))
+    edge_rows = shifted(conv_in[head_count - 1, :, share_rows - 8 :].astype(f32), "seq", 1)
     taps = jnp.concatenate([conv_x, conv_bc], axis=1)
     bias = jnp.concatenate([conv_x_bias, conv_bc_bias])
     taps_bias = jnp.concatenate([taps, bias[None], jnp.zeros((7 - conv_taps, conv_width), f32)])
@@ -844,66 +989,78 @@
         scanned, conv_act, gate_z, log_decay, lead, entering, skip, gate_gain, w_out
     )
 
-    mix_out = sum_shares(partial_out)
+    got_mix, *grads_in = tie(swap_shares(partial_out), *grads_in)
     squares = own_share(add_over(squares[..., 0], "head"))
-    gate_scale = lax.rsqrt(squares / inner_all + norm_eps)[..., None]
-    hidden = own_share(x_rows).astype(f32) + mix_out * gate_scale
-    scale_two = lax.rsqrt(jnp.mean(hidden * hidden, axis=-1, keepdims=True) + norm_eps)
-    normed_share = (hidden * scale_two * norm2_gain).astype(bf16)
-
     expert_ids = jnp.arange(experts_all, dtype=jnp.int32)
-    used = jnp.any(own_share(by_share(routes))[..., None] == expert_ids, axis=2)
-    logits = times(normed_share, router)
-    top = jnp.max(jnp.where(used, logits, -jnp.inf), axis=-1, keepdims=True)
-    powers = jnp.where(used, jnp.exp(jnp.where(used, logits - top, 0.0)), 0.0)
-    gates = powers / jnp.sum(powers, axis=-1, keepdims=True)
-    normed_two, gates = relay_shares(normed_share, flat(gates).T)
+    used = jnp.any(own_share(by_share(routes))[..., None] == expert_ids, axis=2).astype(f32)
+    x_share, grad_share = own_share(x_rows), own_share(grad_rows)
+    beside = -(-2 * experts_all // 128) * 128
+    normed_share, hidden, mix_out, scales = on_share(
+        lambda *refs: after_mix_kernel(inner_all, *refs),
+        got_mix,
+        [x_share, squares[..., None], used],
+        [norm2_gain[None], router],
+        [(model_width + beside, bf16), (model_width, f32), (model_width, f32), (128, f32)],
+    )
+    pieces = relay(normed_share)
+    rows_in = [flat(laid([around(piece, k) for piece in pieces])) for k in range(seq_count)]
 
     first = (seq_rank * head_count + head_rank) * experts_dev
     mine = (jnp.arange(8)[:, None] + first == expert_ids) & (jnp.arange(8)[:, None] < experts_dev)
     mine = mine.astype(f32)
-    ffn_out, ffn_dx, logit_grad = [], [], []
+    turns = [*range(1, seq_count), 0]
+    ffn_out, ffn_dx, logit_grad, before_act = [], [], [], []
+    for k in turns:
+        shared = (w_shared_gu, w_shared_down) if k == 0 else ()
+        out, logit, both = experts_forward(rows_in[k], grads_in[k], mine, w_expert_gu, w_expert_down, shared)
+        ffn_out.append(around(out, -k))
+        logit_grad.append(around(logit, -k))
+        before_act.append(both)
+    ffn_low = sum(f.astype(f32) for f in ffn_out).astype(bf16)
+    ffn_low = ffn_low.reshape(head_count, batch_size, share_rows, model_width)
+    ffn_low, before_act[-1] = tie(ffn_low, before_act[-1])
+    got_out = swap_shares(ffn_low)
     up_terms, down_terms = [], []
-    for k in [*range(1, seq_count), 0]:
-        rows = flat(around(normed_two, k))
-        weights = flat(jnp.swapaxes(around(gates, k), 1, 2))
+    for k, both in zip(turns, before_act):
         shared = (w_shared_gu, w_shared_down) if k == 0 else ()
-        pieces = experts(rows, grads_in[k], weights, mine, w_expert_gu, w_expert_down, shared)
-        ffn_out.append(around(pieces[0], -k))
-        ffn_dx.append(around(pieces[1], -k))
-        logit_grad.append(around(pieces[2], -k))
-        down_terms.append((grads_in[k], pieces[3]))
-        up_terms.append((rows, pieces[4]))
-    shared_terms = [[(rows, pieces[6])], [(grads_in[0], pieces[5])]]
+        made_k = experts_backward(rows_in[k], grads_in[k], both, mine, w_expert_gu, w_expert_down, shared)
+        ffn_dx.append(around(made_k[0], -k))
+        down_terms.append((grads_in[k], made_k[1]))
+        up_terms.append((rows_in[k], made_k[2]))
+    shared_terms = [[(rows_in[0], made_k[4])], [(grads_in[0], made_k[3])]]
+    logit_grad = sum(logit_grad).astype(bf16)
+    ffn_dx = sum(d.astype(f32) for d in ffn_dx) + times_t(logit_grad, router)
+    ffn_dx = ffn_dx.astype(bf16).reshape(ffn_low.shape)
+    ffn_dx, *gu_grads = tie(ffn_dx, *[term[1] for term in up_terms])
+    up_terms = [(term[0], gu_grad) for term, gu_grad in zip(up_terms, gu_grads)]
+    ffn_dx, got_out = tie(ffn_dx, got_out)
+    got_dx = swap_shares(ffn_dx)
     expert_grads = [
-        weight_grads([up_terms[k : k + 2], down_terms[k : k + 2]], 512) for k in range(0, seq_count, 2)
+        weight_grads([up_terms[k : k + 2], down_terms[k : k + 2]], model_width, 512)
+        for k in range(0, seq_count, 2)
     ]
     if len(expert_grads) > 1:
         expert_grads = [sum(g.astype(f32) for g in expert_grads).astype(bf16)]
-    logit_grad = sum(logit_grad).astype(bf16)
-    ffn_dx = sum(d.astype(f32) for d in ffn_dx) + times_t(logit_grad, router)
-    ffn_dx = ffn_dx.astype(bf16).reshape(normed_two.shape)
-    expert_sum = scattered(expert_grads[0], "dp")
-    dx_share, _, logit_grad = tie(sum_shares(ffn_dx), expert_grads[0], logit_grad)
+    got_dx, expert_grads, logit_grad = tie(got_dx, expert_grads[0], logit_grad)
+    expert_sum = scattered(expert_grads, "dp")
     grad_router = lax.dot_general(
-        logit_grad, flat(normed_two), (((0,), (0,)), ((), ())), preferred_element_type=f32
+        logit_grad, rows_in[0], (((0,), (0,)), ((), ())), preferred_element_type=f32
+    )[:, :model_width]
+    push_share, hidden_grad, norm_two_sums = on_share(
+        lambda *refs: after_ffn_kernel(inner_all, *refs),
+        got_dx,
+        [hidden, mix_out, scales, grad_share],
+        [norm2_gain[None]],
+        [(model_width + 128, bf16), (model_width, f32)],
+        [(8, model_width)],
     )
-    gained_two = dx_share * norm2_gain
-    hidden_grad = own_share(grad_rows).astype(f32) + scale_two * (
-        gained_two
-        - hidden * scale_two * scale_two * jnp.mean(gained_two * hidden, axis=-1, keepdims=True)
-    )
-    grad_norm_two = jnp.sum(dx_share * hidden * scale_two, axis=(0, 1))
-    scale_push = jnp.sum(hidden_grad * mix_out, axis=-1)
-    squares_grad = -0.5 * scale_push * gate_scale[..., 0] ** 3 / inner_all
-    out_push, squares_grad = relay_shares((hidden_grad * gate_scale).astype(bf16), squares_grad)
-    out_push, expert_sum = tie(out_push, expert_sum)
-    ffn_low = sum(f.astype(f32) for f in ffn_out).astype(bf16).reshape(normed_two.shape)
-    ffn_low, out_push = tie(ffn_low, out_push)
-    ffn_share = sum_shares(ffn_low)
+    out_push = relay_shares(push_share)
+
+    layer_share, out_push = tie((hidden + summed(got_out)).astype(bf16), out_push)
+    layer_out = gather_shares(layer_share)
 
     mixed_grad, z_grad, entering_grad, channel_sums = gate_backward(
-        out_push, w_out, mixed, gate_z, conv_act, log_decay, lead, squares_grad[..., None], gate_gain
+        out_push, w_out, mixed, gate_z, conv_act, log_decay, lead, gate_gain
     )
     if seq_count == 2:
         leaving_grad = shifted(entering_grad.astype(bf16), "seq", -1).astype(f32)
@@ -926,24 +1083,19 @@
         skip,
     )
     early_dx = times_t(z_grad, w_in_zx[0])
-    in_grad, ffn_share = tie(in_grad, ffn_share)
-    next_rows = shifted(first_rows[:, :edge], "seq", -1)
-    late = [
-        sum(taps[edge - k] * next_rows[:, k + i - edge] for k in range(conv_taps) if k + i >= edge)
-        for i in range(edge)
-    ]
-    late = last_rows.at[:, 8 - edge :].add(jnp.stack(late, axis=1)).astype(bf16)
-    in_grad = in_grad.at[head_count - 1, :, share_rows - 8 :, :conv_width].set(late)
+    in_grad, layer_out, early_dx, expert_sum = tie(in_grad, layer_out, early_dx, expert_sum)
+    in_grad = end_rows(in_grad, last_rows, shifted(first_rows, "seq", -1), taps_bias)
     normed_one_grad = early_dx + times_t(in_grad, w_late)
     grad_norm_one = jnp.sum(normed_one_grad * input_wide * scale_one, axis=(0, 1, 2))
     normed_one_grad = normed_one_grad.astype(bf16)
-    dn_share = sum_shares(normed_one_grad)
+    normed_one_grad, in_grad = tie(normed_one_grad, in_grad)
+    got_dn = swap_shares(normed_one_grad)
 
     def whole(array):
         return spread_last(array, head_rank, head_count).reshape(-1)
 
     small = [
-        grad_norm_two,
+        norm_two_sums[0],
         grad_router.reshape(-1),
         whole(tap_sums[:conv_taps, :inner_dev]),
         whole(tap_sums[conv_taps, :inner_dev]),
@@ -957,29 +1109,27 @@
     sizes = [a.shape[0] for a in small]
     small = jnp.concatenate(small + [jnp.zeros((128 * model_width - sum(sizes),), f32)])
     small = small.reshape(128, model_width).T.astype(bf16)
-    grad_late = weight_grads([[(flat(normed_one), flat(in_grad))]], 128, small)
+    grad_late = weight_grads([[(flat(normed_one), flat(in_grad))]], model_width, 128, small)
     early_terms = [[(flat(out_push), flat(gated_low))], [(flat(normed_one), flat(z_grad))]]
-    grad_early = weight_grads(early_terms + shared_terms, 256)
+    grad_early = weight_grads(early_terms + shared_terms, model_width, 256)
     late_sum = scattered(grad_late, ("dp", "seq")).astype(f32)
+    late_sum, got_dn = tie(late_sum, got_dn)
+    input_grad = on_share(
+        after_proj_kernel, got_dn, [x_share, hidden_grad], [norm1_gain[None]], [(model_width, bf16)]
+    )[0]
     merged = jnp.concatenate([late_sum[:, inner_dev:conv_width], late_sum[:, conv_width + 128 :]], axis=1)
-    merged = add_over(merged, "head")
-    merged = join_over(merged, 0, "seq", "dp")
-    early_sum = scattered(grad_early, ("dp", "seq"))
-
-    layer_share, dn_share, early_sum = tie((hidden + ffn_share).astype(bf16), dn_share, early_sum)
-    early_sum = early_sum.astype(f32)
-    layer_out = by_position(gather_shares(layer_share))
-    gained_one = dn_share * norm1_gain
-    input_share, scale_share = own_share(input_wide), own_share(scale_one)
-    input_grad = hidden_grad + scale_share * (
-        gained_one
-        - input_share
-        * scale_share
-        * scale_share
-        * jnp.mean(gained_one * input_share, axis=-1, keepdims=True)
-    )
-    d_input = relay_shares(input_grad.astype(bf16), shares_first=False)
-    d_input = d_input.reshape(batch_size, tokens, model_width)
+    for bit in bits_of("head"):
+        merged = merged.astype(bf16)
+        merged = merged.astype(f32) + across(merged, "head", bit).astype(f32)
+    merged = merged.astype(bf16)
+    input_grad, merged = tie(input_grad, merged)
+    merged = join_over(merged[None], 0, "dp", "seq")
+    merged = jnp.swapaxes(merged.reshape((seq_count, -1) + merged.shape[1:]), 0, 1)
+    merged = merged.reshape(model_width, -1).astype(f32)
+    layer_out = by_position(layer_out)
+    late_sum, grad_early = tie(late_sum, grad_early)
+    early_sum = scattered(grad_early, ("dp", "seq")).astype(f32)
+    d_input = relay_shares(input_grad, 1).reshape(batch_size, tokens, model_width)
 
     grad_bc = merged[:, : 2 * state_size]
     small = merged[:, 2 * state_size :].T.reshape(-1)

time: 898 us -> 796 us (0.89)
  starting transfers between devices: 187 us -> 71.3 us
  Pallas kernels: 191 us -> 228 us
  other arithmetic: 77.5 us -> 43.6 us
  waiting for transfers between devices: 284 us -> 316 us
  local copies, waits for them, and re-layouts: 100 us -> 76.5 us
    ppermute x48 -> x15, starting transfers between devices: 136 us -> 27.8 us  [the longest x12 16.7 us: passed(): return lax.ppermute(array, 'head', pairs)]
    ppermute x48 -> x15, waiting for transfers between devices: 25.3 us -> 132 us  [the longest x12 118 us: passed(): return lax.ppermute(array, 'head', pairs)]
    ppermute x7, waiting for transfers between devices: 143 us -> 69.3 us  [across(): lax.ppermute(array, axis, [(i, i ^ bit) for i in range(lax.axis_size(axis...]
    pallas_call x2 -> x8, Pallas kernels: 61.1 us -> 97.8 us  [the longest x2 42.4 us: experts_backward(): pl.pallas_call(lambda *refs: expert_backward_kernel(bool(shared), *refs),...]
    reduce_scatter x3, waiting for transfers between devices: 0.03 us -> 26.5 us  [scattered(): return lax.psum_scatter(array, axes, scatter_dimension=0, tiled=True)]
    all_to_all x4, waiting for transfers between devices: 104 us -> 78.9 us  [swap_shares(): return lax.all_to_all(part, 'head', split_axis=0, concat_axis=0, tiled=True)]
    reduce_sum x8 -> x1, other arithmetic: 17.9 us -> 2.42 us  [local(): jnp.sum(normed_one_grad * input_wide * scale_one, axis=(0, 1, 2))]
    dynamic_update_slice x18 -> x9, other arithmetic: 23.7 us -> 10.4 us  [laid(): lax.dynamic_update_index_in_dim(out, piece, (place + count - d) % count,...]
  transfers between devices with their start and end apart: 73 -> 42, of which waited for: 17 -> 22; matrix products, arithmetic and copies ran while one was open for 21% -> 15% of each run, Pallas kernels for 8% -> 21%
where the time goes in v3:
time: 796 us; the launch traced here: 786 us
  waiting for transfers between devices  316 us (40%)
  Pallas kernels  228 us (29%)
  local copies, waits for them, and re-layouts  76.5 us (10%)
  starting transfers between devices  71.3 us (9%)
  other arithmetic  43.6 us (5%)
  matrix products  35.2 us (4%)
  between operations  15.1 us (2%)
    ppermute x12, waiting for transfers between devices, passed(): return lax.ppermute(array, 'head', pairs)  118 us
    all_to_all x4, waiting for transfers between devices, swap_shares(): return lax.all_to_all(part, 'head', split_axis=0, concat_axis=0, tiled=True)  78.9 us
    ppermute x7, waiting for transfers between devices, across(): lax.ppermute(array, axis, [(i, i ^ bit) for i in range(lax.axis_size(axis...  69.3 us
    pallas_call x3, Pallas kernels, weight_grads(): pl.pallas_call(kernel, grid=(steps,), in_specs=specs, out_specs=pl.BlockS...  66.6 us
    pallas_call x2, Pallas kernels, experts_backward(): pl.pallas_call(lambda *refs: expert_backward_kernel(bool(shared), *refs),...  42.4 us
    pallas_call x2, Pallas kernels, experts_forward(): pl.pallas_call(lambda *refs: expert_forward_kernel(bool(shared), *refs),...  39.7 us
    reduce_scatter x3, waiting for transfers between devices, scattered(): return lax.psum_scatter(array, axes, scatter_dimension=0, tiled=True)  26.5 us
    pallas_call x1, Pallas kernels, scan_backward(): pl.pallas_call(scan_back_kernel, grid=(batch, blocks), in_specs=[rows_of(...  25.7 us
  transfers between devices with their start and end apart: 42, of which 22 were waited for; matrix products, arithmetic and copies ran while one was open for 15% of the time, Pallas kernels for 21%

profile of v3, /device:TPU:0, one launch (start us, length us, event | category | flops | bytes accessed | tf_op | source)
XLA Modules:
  0.0 785.6 jit_solution(7488072262205476619)
XLA Ops:
  7.2 2.6 fusion
  14.1 3.7 fusion.19.cin.cin_before
  19.2 3.0 collective-permute-start
  24.1 3.7 fusion.21.raw
  31.0 14.4 %shard_map.365 = (bf16[4,2,128,1024]{3,2,1,0:T(8,128)(2,1)}, f32[4,2,128,768]{3,2,1,0:T(8,128)}, f32[2,2,128,768]{3,2,1,0:T(8,128)}, f32[2,128,768]{2,1,0:T(8,128)}) custom-call(bf16[4,2,128,1024]{3,2,1,0:T(8,128)(2,1)} %copy-done.5, f32[2,8,1024]{2,1,0:T(8,128)} %collective-permute-done.edge, f32[8,1024]{1,0:T(8,128)} %maximum_maximum_fusion.taps.taps_ref, ...), custom_call_target="tpu_custom_call" | custom-call | flops 1207959552 | bytes 7864320 | tf_op jit(solution)/shard_map/pallas_call | solution.py:310
  45.4 2.2 collective-permute-start.1
  49.5 6.9 fusion.15.z
  56.4 12.2 %shard_map.366 = (bf16[4,2,128,768]{3,2,1,0:T(8,128)(2,1)}, bf16[4,2,128,768]{3,2,1,0:T(8,128)(2,1)}, f32[4,2,128,128]{3,2,1,0:T(8,128)}, bf16[4,2,128,1536]{3,2,1,0:T(8,128)(2,1)}) custom-call(f32[4,2,128,768]{3,2,1,0:T(8,128)} %get-tuple-element.85.y, bf16[4,2,128,1024]{3,2,1,0:T(8,128)(2,1)} %get-tuple-element.84.act_in, f32[4,2,128,768]{3,2,1,0:T(8,128)} %fusion.15.z, ...), custom_call_target="tpu_custom_call" | custom-call | flops 2617245696 | bytes 14155776 | tf_op jit(solution)/shard_map/pallas_call | solution.py:346
  68.6 5.9 all-to-all-start
  74.6 3.8 copy.286
  82.7 40.7 %collective-permute-done.3 = f32[4,2,128]{2,1,0:T(2,128)S(1)} collective-permute-done((f32[4,2,128]{2,1,0:T(2,128)S(1)}, f32[4,2,128]{2,1,0:T(2,128)S(1)}, u32[]{:S(2)}, u32[]{:S(2)}) %collective-permute-start.3) | collective-permute-done | bytes 4128 | tf_op jit(solution)/shard_map/ppermute | solution.py:841
  123.5 4.7 collective-permute-start.4
  130.4 13.0 %collective-permute-done.4 = f32[4,2,128]{2,1,0:T(2,128)S(1)} collective-permute-done((f32[4,2,128]{2,1,0:T(2,128)S(1)}, f32[4,2,128]{2,1,0:T(2,128)S(1)}, u32[]{:S(2)}, u32[]{:S(2)}) %collective-permute-start.4) | collective-permute-done | bytes 4128 | tf_op jit(solution)/shard_map/ppermute | solution.py:841
  144.3 4.2 shard_map.367
  148.5 2.2 collective-permute-start.6
  150.7 2.4 collective-permute-start.7
  155.8 13.7 %collective-permute-done.6 = bf16[2,128,1664]{2,1,0:T(8,128)(2,1)} collective-permute-done((bf16[2,128,1664]{2,1,0:T(8,128)(2,1)}, bf16[2,128,1664]{2,1,0:T(8,128)(2,1)}, u32[]{:S(2)}, u32[]{:S(2)}) %collective-permute-start.6) | collective-permute-done | bytes 852000 | tf_op jit(solution)/shard_map/ppermute | solution.py:803
  170.2 22.7 %collective-permute-done.10 = bf16[2,128,1664]{2,1,0:T(8,128)(2,1)} collective-permute-done((bf16[2,128,1664]{2,1,0:T(8,128)(2,1)}, bf16[2,128,1664]{2,1,0:T(8,128)(2,1)}, u32[]{:S(2)}, u32[]{:S(2)}) %collective-permute-start.10) | collective-permute-done | bytes 852000 | tf_op jit(solution)/shard_map/ppermute | solution.py:803
  198.8 17.1 %collective-permute-done.11 = bf16[2,128,1664]{2,1,0:T(8,128)(2,1)S(1)} collective-permute-done((bf16[2,128,1664]{2,1,0:T(8,128)(2,1)}, bf16[2,128,1664]{2,1,0:T(8,128)(2,1)S(1)}, u32[]{:S(2)}, u32[]{:S(2)}) %collective-permute-start.11) | collective-permute-done | bytes 852000 | tf_op jit(solution)/shard_map/ppermute | solution.py:803
  221.7 18.3 %shard_map.368 = (bf16[1024,1536]{1,0:T(8,128)(2,1)}, f32[1024,16]{1,0:T(8,128)}, f32[1024,2048]{1,0:T(8,128)}) custom-call(bf16[1024,1664]{1,0:T(8,128)(2,1)} %bitcast.24.refs_0_.refs_2_.refs_1_, bf16[1024,1536]{1,0:T(8,128)(2,1)} %bitcast.16.refs_1_.refs_0_.refs_4_, bf16[1024,1664]{1,0:T(8,128)(2,1)} %bitcast.24.refs_0_.refs_2_.refs_1_, ...), custom_call_target="tpu_custom_call" | custom-call | flops 9663676416 | bytes 27262976 | tf_op jit(solution)/shard_map/pallas_call | solution.py:630
  240.1 21.3 %shard_map.370 = (bf16[1024,1536]{1,0:T(8,128)(2,1)}, f32[1024,16]{1,0:T(8,128)}, f32[1024,2560]{1,0:T(8,128)}) custom-call(bf16[1024,1664]{1,0:T(8,128)(2,1)} %bitcast.184, bf16[1024,1536]{1,0:T(8,128)(2,1)} %bitcast.15.refs_1_.refs_0_.refs_6_, bf16[1024,1664]{1,0:T(8,128)(2,1)} %bitcast.185, f32[8,16]{1,0:T(8,128)} %fusion.27.refs_3_, ...), custom_call_target="tpu_custom_call" | custom-call | flops 12079595520 | bytes 31719424 | tf_op jit(solution)/shard_map/pallas_call | solution.py:630
  261.4 4.4 add_convert_fusion.1
  265.8 5.1 all-to-all-start.1
  270.9 18.1 %shard_map.369 = (bf16[1024,1536]{1,0:T(8,128)(2,1)}, bf16[1024,1024]{1,0:T(8,128)(2,1)}, bf16[1024,2048]{1,0:T(8,128)(2,1)}) custom-call(bf16[1024,1536]{1,0:T(8,128)(2,1)} %bitcast.16.refs_1_.refs_0_.refs_4_, bf16[1024,1664]{1,0:T(8,128)(2,1)} %bitcast.24.refs_0_.refs_2_.refs_1_, f32[1024,2048]{1,0:T(8,128)} %get-tuple-element.93.refs_2_, ...), custom_call_target="tpu_custom_call" | custom-call | flops 9663676416 | bytes 30408704 | tf_op jit(solution)/shard_map/pallas_call | solution.py:650
  289.5 5.9 collective-permute-done.16
  295.4 24.3 %shard_map.371 = (bf16[1024,1536]{1,0:T(8,128)(2,1)}, bf16[1024,1024]{1,0:T(8,128)(2,1)}, bf16[1024,2048]{1,0:T(8,128)(2,1)}, bf16[1024,256]{1,0:T(8,128)(2,1)}, bf16[1024,512]{1,0:T(8,128)(2,1)}) custom-call(bf16[1024,1536]{1,0:T(8,128)(2,1)} %bitcast.15.refs_1_.refs_0_.refs_6_, bf16[1024,1664]{1,0:T(8,128)(2,1)} %bitcast.186, ...), custom_call_target="tpu_custom_call" | custom-call | flops 12079595520 | bytes 36438016 | tf_op jit(solution)/shard_map/pallas_call | solution.py:650
  319.7 4.6 add_convert_fusion
  324.3 18.2 %all-to-all-done.1 = bf16[4,2,128,1536]{3,2,1,0:T(8,128)(2,1)} async-done(((bf16[4,2,128,1536]{3,2,1,0:T(8,128)(2,1)}), bf16[4,2,128,1536]{3,2,1,0:T(8,128)(2,1)}, u32[]{:S(2)}, u32[]{:S(2)}) %all-to-all-start.1) | async-done | bytes 3145760 | tf_op jit(solution)/shard_map/all_to_all | solution.py:789
  342.5 4.7 all-to-all-start.2
  347.4 32.3 %shard_map.372 = bf16[1536,3072]{1,0:T(8,128)(2,1)} custom-call(bf16[1024,1664]{1,0:T(8,128)(2,1)} %bitcast.24.refs_0_.refs_2_.refs_1_, bf16[1024,2048]{1,0:T(8,128)(2,1)} %get-tuple-element.109.refs_1_, bf16[1024,1664]{1,0:T(8,128)(2,1)} %bitcast.187, bf16[1024,2048]{1,0:T(8,128)(2,1)} %get-tuple-element.110.refs_3_, ...), custom_call_target="tpu_custom_call" | custom-call | flops 19327352832 | bytes 34603008 | tf_op jit(solution)/shard_map/pallas_call | solution.py:531
  379.7 38.3 %all-to-all-done.2.refs_0_ = bf16[4,2,128,1536]{3,2,1,0:T(8,128)(2,1)} async-done(((bf16[4,2,128,1536]{3,2,1,0:T(8,128)(2,1)}), bf16[4,2,128,1536]{3,2,1,0:T(8,128)(2,1)}, u32[]{:S(2)}, u32[]{:S(2)}) %all-to-all-start.2) | async-done | bytes 3145760 | tf_op jit(solution)/shard_map/all_to_all | solution.py:789
  420.2 5.0 shard_map.373
  427.9 6.6 collective-permute-start.18
  434.6 2.3 fusion.20
  436.9 9.4 %collective-permute-done.17 = bf16[2,128,1664]{2,1,0:T(8,128)(2,1)S(1)} collective-permute-done((bf16[2,128,1664]{2,1,0:T(8,128)(2,1)}, bf16[2,128,1664]{2,1,0:T(8,128)(2,1)S(1)}, u32[]{:S(2)}, u32[]{:S(2)}) %collective-permute-start.17) | collective-permute-done | bytes 852000 | tf_op jit(solution)/shard_map/ppermute | solution.py:803
  447.0 2.7 collective-permute-done.20
  453.9 14.6 %collective-permute-done.18 = bf16[2,128,1664]{2,1,0:T(8,128)(2,1)S(1)} collective-permute-done((bf16[2,128,1664]{2,1,0:T(8,128)(2,1)}, bf16[2,128,1664]{2,1,0:T(8,128)(2,1)S(1)}, u32[]{:S(2)}, u32[]{:S(2)}) %collective-permute-start.18) | collective-permute-done | bytes 852000 | tf_op jit(solution)/shard_map/ppermute | solution.py:807
  469.7 16.3 %collective-permute-done.21 = bf16[2,128,1664]{2,1,0:T(8,128)(2,1)S(1)} collective-permute-done((bf16[2,128,1664]{2,1,0:T(8,128)(2,1)S(1)}, bf16[2,128,1664]{2,1,0:T(8,128)(2,1)S(1)}, u32[]{:S(2)}, u32[]{:S(2)}) %collective-permute-start.21) | collective-permute-done | bytes 852000 | tf_op jit(solution)/shard_map/ppermute | solution.py:803
  490.3 4.7 all-to-all-start.3
  495.3 2.6 fusion.36
  499.5 11.7 %shard_map.374 = (bf16[4,2,128,768]{3,2,1,0:T(8,128)(2,1)}, bf16[4,2,128,768]{3,2,1,0:T(8,128)(2,1)}, f32[2,128,768]{2,1,0:T(8,128)}, f32[8,768]{1,0:T(8,128)}) custom-call(bf16[4,2,128,1664]{3,2,1,0:T(8,128)(2,1)} %bitcast_dynamic-update-slice_fusion.push.slope_in, bf16[768,1536]{1,0:T(8,128)(2,1)} %w_out.3, ...), custom_call_target="tpu_custom_call" | custom-call | flops 2617245696 | bytes 14155776 | tf_op jit(solution)/shard_map/pallas_call | solution.py:379
  518.6 7.4 fusion.13
  528.0 25.7 %shard_map.375 = (bf16[4,2,128,1152]{3,2,1,0:T(8,128)(2,1)}, f32[2,8,1024]{2,1,0:T(8,128)}, f32[2,8,1024]{2,1,0:T(8,128)}, f32[8,1024]{1,0:T(8,128)}) custom-call(bf16[4,2,128,1024]{3,2,1,0:T(8,128)(2,1)} %copy-done.5, bf16[4,2,128,1024]{3,2,1,0:T(8,128)(2,1)} %copy-done.5, f32[2,8,1024]{2,1,0:T(8,128)} %collective-permute-done.edge, ...), custom_call_target="tpu_custom_call" | custom-call | flops 2617245696 | bytes 11796480 | tf_op jit(solution)/shard_map/pallas_call | solution.py:413
  562.9 2.5 all-to-all-done.3
  567.2 6.2 fusion.5
  573.6 2.4 fusion.4
  576.1 3.4 concatenate.47
  580.8 13.4 %shard_map.377 = bf16[1536,1280]{1,0:T(8,128)(2,1)} custom-call(bf16[1024,1536]{1,0:T(8,128)(2,1)} %bitcast.192, bf16[1024,1152]{1,0:T(8,128)(2,1)} %bitcast.202, bf16[1536,128]{1,0:T(8,128)(2,1)} %bitcast.205), custom_call_target="tpu_custom_call" | custom-call | flops 4026531840 | bytes 10223616 | tf_op jit(solution)/shard_map/pallas_call | solution.py:531
  594.3 3.7 all-to-all-start.4
  598.2 20.9 %shard_map.379 = bf16[1536,2304]{1,0:T(8,128)(2,1)} custom-call(bf16[1024,1664]{1,0:T(8,128)(2,1)} %bitcast.59.refs_0_, bf16[1024,768]{1,0:T(8,128)(2,1)} %bitcast.215, bf16[1024,1536]{1,0:T(8,128)(2,1)} %bitcast.193, bf16[1024,768]{1,0:T(8,128)(2,1)} %bitcast.216, bf16[1024,1664]{1,0:T(8,128)(2,1)} %bitcast.189, ...), custom_call_target="tpu_custom_call" | custom-call | flops 7247757312 | bytes 32243712 | tf_op jit(solution)/shard_map/pallas_call | solution.py:531
  619.1 26.5 %reduce-scatter.6.cloned.1.call-done = bf16[192,1280]{1,0:T(8,128)(2,1)} async-done(((bf16[1536,1280]{1,0:T(8,128)(2,1)}), bf16[192,1280]{1,0:T(8,128)(2,1)}) %reduce-scatter.6.cloned.1.call-update) | async-done | bytes 491536 | tf_op jit(solution)/shard_map/reduce_scatter | solution.py:952
  647.6 22.3 %all-to-all-done.4.got = bf16[4,2,128,1536]{3,2,1,0:T(8,128)(2,1)S(1)} async-done(((bf16[4,2,128,1536]{3,2,1,0:T(8,128)(2,1)}), bf16[4,2,128,1536]{3,2,1,0:T(8,128)(2,1)S(1)}, u32[]{:S(2)}, u32[]{:S(2)}) %all-to-all-start.4) | async-done | bytes 3145760 | tf_op jit(solution)/shard_map/all_to_all | solution.py:789
  672.2 2.3 convert_element_type.157
  675.0 5.6 collective-permute-done.24
  681.1 4.8 shard_map.378
  685.9 3.9 collective-permute-done.25
  693.8 3.7 collective-permute-done.31
  698.8 3.8 copy.255
  711.2 2.4 collective-permute-done.32
  715.4 8.7 %collective-permute-done.26 = bf16[2,128,1536]{2,1,0:T(8,128)(2,1)} collective-permute-done((bf16[2,128,1536]{2,1,0:T(8,128)(2,1)S(1)}, bf16[2,128,1536]{2,1,0:T(8,128)(2,1)}, u32[]{:S(2)}, u32[]{:S(2)}) %collective-permute-start.26) | collective-permute-done | bytes 786464 | tf_op jit(solution)/shard_map/ppermute | solution.py:803
  725.7 20.1 %collective-permute-done.29 = bf16[2,128,1536]{2,1,0:T(8,128)(2,1)} collective-permute-done((bf16[2,128,1536]{2,1,0:T(8,128)(2,1)S(1)}, bf16[2,128,1536]{2,1,0:T(8,128)(2,1)}, u32[]{:S(2)}, u32[]{:S(2)}) %collective-permute-start.29) | collective-permute-done | bytes 786464 | tf_op jit(solution)/shard_map/ppermute | solution.py:803
  760.2 7.2 collective-permute-done.30
  767.4 2.2 bitcast_dynamic-update-slice_fusion.13
  769.6 2.3 copy.257
  (283 shorter events, 118.7 us)
Async XLA Ops:
  14.1 3.8 copy-start.4
  17.8 10.5 %copy-start.29 = (f32[4,768]{1,0:T(4,128)S(1)}, f32[4,768]{1,0:T(4,128)}, u32[]{:S(2)}) copy-start(f32[4,768]{1,0:T(4,128)} %param.31) | copy-start | bytes 36868
  19.2 11.8 %collective-permute-start = (f32[2,8,1024]{2,1,0:T(8,128)}, f32[2,8,1024]{2,1,0:T(8,128)}, u32[]{:S(2)}, u32[]{:S(2)}) collective-permute-start(f32[2,8,1024]{2,1,0:T(8,128)} %fusion.24), channel_id=1, source_target_pairs={{0,4},{1,5},{2,6},{3,7},{8,12},{9,13},{10,14},{11,15},{16,20},{17,... | collective-permute-start | bytes 196616 | tf_op jit(solution)/shard_map/ppermute | solution.py:748
  24.1 4.2 copy-start.33
  24.1 4.3 copy-start.35
  24.1 4.3 copy-start.34
  30.1 18.0 %copy-start.36 = (f32[12]{0:T(128)S(1)}, f32[12]{0:T(128)}, u32[]{:S(2)}) copy-start(f32[12]{0:T(128)} %param.35) | copy-start | bytes 148
  30.1 18.8 %copy-start.32 = (f32[768]{0:T(1024)S(1)}, f32[768]{0:T(1024)}, u32[]{:S(2)}) copy-start(f32[768]{0:T(1024)} %param.36) | copy-start | bytes 9220
  45.4 11.0 %collective-permute-start.1 = (f32[2,128,768]{2,1,0:T(8,128)}, f32[2,128,768]{2,1,0:T(8,128)}, u32[]{:S(2)}, u32[]{:S(2)}) collective-permute-start(f32[2,128,768]{2,1,0:T(8,128)} %get-tuple-element.86), channel_id=1, source_target_pairs={{0,4},{1,5},{2,6},{3,7},{8,12},{9,13},{10,14},{11,15},{16,20},{17,... | collective-permute-start | bytes 2359304 | tf_op jit(solution)/shard_map/ppermute | solution.py:748
  68.6 75.6 %all-to-all-start = ((bf16[4,2,128,1536]{3,2,1,0:T(8,128)(2,1)}), bf16[4,2,128,1536]{3,2,1,0:T(8,128)(2,1)}, u32[]{:S(2)}, u32[]{:S(2)}) async-start(bf16[4,2,128,1536]{3,2,1,0:T(8,128)(2,1)} %get-tuple-element.87), calls=%async_computation | async-start | bytes 6291456 | tf_op jit(solution)/shard_map/all_to_all | solution.py:789
  74.6 3.8 copy-start.27
  74.6 54.3 %copy-start.31 = (f32[1536]{0:T(1024)S(1)}, f32[1536]{0:T(1024)}, u32[]{:S(2)}) copy-start(f32[1536]{0:T(1024)} %param.38) | copy-start | bytes 18436
  74.6 54.9 %copy-start.20 = (bf16[1536,16]{0,1:T(8,128)(2,1)S(1)}, bf16[1536,16]{0,1:T(8,128)(2,1)}, u32[]{:S(2)}) copy-start(bf16[1536,16]{0,1:T(8,128)(2,1)} %param.39) | copy-start | bytes 147460
  78.4 65.9 %collective-permute-start.2 = (bf16[4,2,128,1536]{3,2,1,0:T(8,128)(2,1)}, bf16[4,2,128,1536]{3,2,1,0:T(8,128)(2,1)}, u32[]{:S(2)}, u32[]{:S(2)}) collective-permute-start(bf16[4,2,128,1536]{3,2,1,0:T(8,128)(2,1)} %bitcast.180), channel_id=1, source_target_pairs={{0,4},{4,0},{1,5},{5,1},{2,6},{6,2},{3,7},{7,3},{8,12},{12,8},{9,1... | collective-permute-start | bytes 9437192 | tf_op jit(solution)/shard_map/ppermute | solution.py:872
  80.6 42.8 %collective-permute-start.3 = (f32[4,2,128]{2,1,0:T(2,128)S(1)}, f32[4,2,128]{2,1,0:T(2,128)S(1)}, u32[]{:S(2)}, u32[]{:S(2)}) collective-permute-start(f32[4,2,128]{2,1,0:T(2,128)S(1)} %slice_reduce_fusion.2), channel_id=1, source_target_pairs={{0,1},{1,0},{2,3},{3,2},{4,5},{5,4},{6,7},{7,6},{8,9},{9,8},{10,11... | collective-permute-start | bytes 12296 | tf_op jit(solution)/shard_map/ppermute | solution.py:841
  123.5 20.0 %collective-permute-start.4 = (f32[4,2,128]{2,1,0:T(2,128)S(1)}, f32[4,2,128]{2,1,0:T(2,128)S(1)}, u32[]{:S(2)}, u32[]{:S(2)}) collective-permute-start(f32[4,2,128]{2,1,0:T(2,128)S(1)} %add.179), channel_id=1, source_target_pairs={{0,2},{1,3},{2,0},{3,1},{4,6},{5,7},{6,4},{7,5},{8,10},{9,11},{10,... | collective-permute-start | bytes 12296 | tf_op jit(solution)/shard_map/ppermute | solution.py:841
  148.5 21.0 %collective-permute-start.6 = (bf16[2,128,1664]{2,1,0:T(8,128)(2,1)}, bf16[2,128,1664]{2,1,0:T(8,128)(2,1)}, u32[]{:S(2)}, u32[]{:S(2)}) collective-permute-start(bf16[2,128,1664]{2,1,0:T(8,128)(2,1)} %get-tuple-element.92), channel_id=1, source_target_pairs={{0,1},{1,2},{2,3},{4,5},{5,6},{6,7},{8,9},{9,10},{10,11},{12,13},{... | collective-permute-start | bytes 2555912 | tf_op jit(solution)/shard_map/ppermute | solution.py:803
  150.7 43.5 %collective-permute-start.7 = (bf16[2,128,1664]{2,1,0:T(8,128)(2,1)}, bf16[2,128,1664]{2,1,0:T(8,128)(2,1)}, u32[]{:S(2)}, u32[]{:S(2)}) collective-permute-start(bf16[2,128,1664]{2,1,0:T(8,128)(2,1)} %get-tuple-element.92), channel_id=1, source_target_pairs={{0,3},{3,0},{4,7},{7,4},{8,11},{11,8},{12,15},{15,12},{16,19},{19,... | collective-permute-start | bytes 2555912 | tf_op jit(solution)/shard_map/ppermute | solution.py:807
  153.2 39.8 %collective-permute-start.10 = (bf16[2,128,1664]{2,1,0:T(8,128)(2,1)}, bf16[2,128,1664]{2,1,0:T(8,128)(2,1)}, u32[]{:S(2)}, u32[]{:S(2)}) collective-permute-start(bf16[2,128,1664]{2,1,0:T(8,128)(2,1)} %get-tuple-element.92), channel_id=1, source_target_pairs={{1,0},{2,1},{3,2},{5,4},{6,5},{7,6},{9,8},{10,9},{11,10},{13,12},{... | collective-permute-start | bytes 2555912 | tf_op jit(solution)/shard_map/ppermute | solution.py:803
  155.2 40.5 %collective-permute-start.5 = (bf16[2,128,1664]{2,1,0:T(8,128)(2,1)}, bf16[2,128,1664]{2,1,0:T(8,128)(2,1)S(1)}, u32[]{:S(2)}, u32[]{:S(2)}) collective-permute-start(bf16[2,128,1664]{2,1,0:T(8,128)(2,1)} %get-tuple-element.92), channel_id=1, source_target_pairs={{0,4},{4,0},{1,5},{5,1},{2,6},{6,2},{3,7},{7,3},{8,12},{12,8},{9,1... | collective-permute-start | bytes 2555912 | tf_op jit(solution)/shard_map/ppermute | solution.py:872
  169.5 29.3 %collective-permute-start.9 = (bf16[2,128,1664]{2,1,0:T(8,128)(2,1)}, bf16[2,128,1664]{2,1,0:T(8,128)(2,1)S(1)}, u32[]{:S(2)}, u32[]{:S(2)}) collective-permute-start(bf16[2,128,1664]{2,1,0:T(8,128)(2,1)} %collective-permute-done.6), channel_id=1, source_target_pairs={{1,2},{2,3},{5,6},{6,7},{9,10},{10,11},{13,14},{14,15},{17,18},{18... | collective-permute-start | bytes 2555912 | tf_op jit(solution)/shard_map/ppermute | solution.py:803
  192.9 23.0 %collective-permute-start.11 = (bf16[2,128,1664]{2,1,0:T(8,128)(2,1)}, bf16[2,128,1664]{2,1,0:T(8,128)(2,1)S(1)}, u32[]{:S(2)}, u32[]{:S(2)}) collective-permute-start(bf16[2,128,1664]{2,1,0:T(8,128)(2,1)} %collective-permute-done.10), channel_id=1, source_target_pairs={{1,0},{2,1},{5,4},{6,5},{9,8},{10,9},{13,12},{14,13},{17,16},{18,1... | collective-permute-start | bytes 2555912 | tf_op jit(solution)/shard_map/ppermute | solution.py:803
  195.7 22.6 %collective-permute-start.8 = (bf16[2,128,1664]{2,1,0:T(8,128)(2,1)S(1)}, bf16[2,128,1664]{2,1,0:T(8,128)(2,1)S(1)}, u32[]{:S(2)}, u32[]{:S(2)}) collective-permute-start(bf16[2,128,1664]{2,1,0:T(8,128)(2,1)S(1)} %get-tuple-element.317), channel_id=1, source_target_pairs={{0,4},{4,0},{1,5},{5,1},{2,6},{6,2},{3,7},{7,3},{8,12},{12,8},{9,1... | collective-permute-start | bytes 2555912 | tf_op jit(solution)/shard_map/ppermute | solution.py:872
  216.2 3.5 collective-permute-start.12
  217.7 22.4 %copy-start.1 = (bf16[4,2,128,1664]{3,2,1,0:T(8,128)(2,1)}, bf16[4,2,128,1664]{3,2,1,0:T(8,128)(2,1)S(1)}, u32[]{:S(2)}) copy-start(bf16[4,2,128,1664]{3,2,1,0:T(8,128)(2,1)S(1)} %get-tuple-element.312) | copy-start | bytes 10223620
  217.7 3.0 collective-permute-start.13
  240.1 21.3 %collective-permute-start.15 = (bf16[1024,1536]{1,0:T(8,128)(2,1)}, bf16[1024,1536]{1,0:T(8,128)(2,1)S(1)}, u32[]{:S(2)}, u32[]{:S(2)}) collective-permute-start(bf16[1024,1536]{1,0:T(8,128)(2,1)} %get-tuple-element.96), channel_id=1, source_target_pairs={{0,4},{4,0},{1,5},{5,1},{2,6},{6,2},{3,7},{7,3},{8,12},{12,8},{9,1... | collective-permute-start | bytes 9437192 | tf_op jit(solution)/shard_map/ppermute | solution.py:872
  265.8 76.7 %all-to-all-start.1 = ((bf16[4,2,128,1536]{3,2,1,0:T(8,128)(2,1)}), bf16[4,2,128,1536]{3,2,1,0:T(8,128)(2,1)}, u32[]{:S(2)}, u32[]{:S(2)}) async-start(bf16[4,2,128,1536]{3,2,1,0:T(8,128)(2,1)} %bitcast.190), calls=%async_computation.1 | async-start | bytes 6291456 | tf_op jit(solution)/shard_map/all_to_all | solution.py:789
  270.9 18.6 %copy-start.41 = (f32[1024,16]{1,0:T(8,128)S(1)}, f32[1024,16]{1,0:T(8,128)}, u32[]{:S(2)}) copy-start(f32[1024,16]{1,0:T(8,128)} %get-tuple-element.101) | copy-start | bytes 196612
  270.9 24.5 %copy-start.17 = (f32[1024,16]{1,0:T(8,128)S(1)}, f32[1024,16]{1,0:T(8,128)}, u32[]{:S(2)}) copy-start(f32[1024,16]{1,0:T(8,128)} %get-tuple-element.102) | copy-start | bytes 196612
  288.9 30.8 %collective-permute-start.14 = (bf16[1024,1536]{1,0:T(8,128)(2,1)}, bf16[1024,1536]{1,0:T(8,128)(2,1)S(1)}, u32[]{:S(2)}, u32[]{:S(2)}) collective-permute-start(bf16[1024,1536]{1,0:T(8,128)(2,1)} %get-tuple-element.94), channel_id=1, source_target_pairs={{0,4},{4,0},{1,5},{5,1},{2,6},{6,2},{3,7},{7,3},{8,12},{12,8},{9,1... | collective-permute-start | bytes 9437192 | tf_op jit(solution)/shard_map/ppermute | solution.py:872
  289.4 5.9 collective-permute-start.16
  342.5 75.6 %all-to-all-start.2 = ((bf16[4,2,128,1536]{3,2,1,0:T(8,128)(2,1)}), bf16[4,2,128,1536]{3,2,1,0:T(8,128)(2,1)}, u32[]{:S(2)}, u32[]{:S(2)}) async-start(bf16[4,2,128,1536]{3,2,1,0:T(8,128)(2,1)} %bitcast.191), calls=%async_computation.2 | async-start | bytes 6291456 | tf_op jit(solution)/shard_map/all_to_all | solution.py:789
  347.2 218.2 %reduce-scatter.4.cloned.1.call-start = ((), (), s32[]{:S(2)}) async-start(), calls=%async_computation.8 | async-start | bytes 11796480 | tf_op jit(solution)/shard_map/reduce_scatter | solution.py:952
  420.2 14.4 %copy-start.7 = (f32[2,128,1536]{2,1,0:T(8,128)S(1)}, f32[2,128,1536]{2,1,0:T(8,128)}, u32[]{:S(2)}) copy-start(f32[2,128,1536]{2,1,0:T(8,128)} %get-tuple-element.90.refs_1_) | copy-start | bytes 4718596
  425.1 27.8 %copy-start.16 = (bf16[2,128,1664]{2,1,0:T(8,128)(2,1)S(1)}, bf16[2,128,1664]{2,1,0:T(8,128)(2,1)}, u32[]{:S(2)}) copy-start(bf16[2,128,1664]{2,1,0:T(8,128)(2,1)} %get-tuple-element.116) | copy-start | bytes 2555908
  425.1 21.1 %collective-permute-start.17 = (bf16[2,128,1664]{2,1,0:T(8,128)(2,1)}, bf16[2,128,1664]{2,1,0:T(8,128)(2,1)S(1)}, u32[]{:S(2)}, u32[]{:S(2)}) collective-permute-start(bf16[2,128,1664]{2,1,0:T(8,128)(2,1)} %get-tuple-element.116), channel_id=1, source_target_pairs={{0,1},{1,2},{2,3},{4,5},{5,6},{6,7},{8,9},{9,10},{10,11},{12,13},{... | collective-permute-start | bytes 2555912 | tf_op jit(solution)/shard_map/ppermute | solution.py:803
  426.6 23.1 %collective-permute-start.20 = (bf16[2,128,1664]{2,1,0:T(8,128)(2,1)}, bf16[2,128,1664]{2,1,0:T(8,128)(2,1)S(1)}, u32[]{:S(2)}, u32[]{:S(2)}) collective-permute-start(bf16[2,128,1664]{2,1,0:T(8,128)(2,1)} %get-tuple-element.116), channel_id=1, source_target_pairs={{1,0},{2,1},{3,2},{5,4},{6,5},{7,6},{9,8},{10,9},{11,10},{13,12},{... | collective-permute-start | bytes 2555912 | tf_op jit(solution)/shard_map/ppermute | solution.py:803
  427.9 40.6 %collective-permute-start.18 = (bf16[2,128,1664]{2,1,0:T(8,128)(2,1)}, bf16[2,128,1664]{2,1,0:T(8,128)(2,1)S(1)}, u32[]{:S(2)}, u32[]{:S(2)}) collective-permute-start(bf16[2,128,1664]{2,1,0:T(8,128)(2,1)} %get-tuple-element.116), channel_id=1, source_target_pairs={{0,3},{3,0},{4,7},{7,4},{8,11},{11,8},{12,15},{15,12},{16,19},{19,... | collective-permute-start | bytes 2555912 | tf_op jit(solution)/shard_map/ppermute | solution.py:807
  446.3 23.4 %collective-permute-start.19 = (bf16[2,128,1664]{2,1,0:T(8,128)(2,1)S(1)}, bf16[2,128,1664]{2,1,0:T(8,128)(2,1)S(1)}, u32[]{:S(2)}, u32[]{:S(2)}) collective-permute-start(bf16[2,128,1664]{2,1,0:T(8,128)(2,1)S(1)} %collective-permute-done.17), channel_id=1, source_target_pairs={{1,2},{2,3},{5,6},{6,7},{9,10},{10,11},{13,14},{14,15},{17,18},{18... | collective-permute-start | bytes 2555912 | tf_op jit(solution)/shard_map/ppermute | solution.py:803
  449.7 36.3 %collective-permute-start.21 = (bf16[2,128,1664]{2,1,0:T(8,128)(2,1)S(1)}, bf16[2,128,1664]{2,1,0:T(8,128)(2,1)S(1)}, u32[]{:S(2)}, u32[]{:S(2)}) collective-permute-start(bf16[2,128,1664]{2,1,0:T(8,128)(2,1)S(1)} %collective-permute-done.20), channel_id=1, source_target_pairs={{1,0},{2,1},{5,4},{6,5},{9,8},{10,9},{13,12},{14,13},{17,16},{18,1... | collective-permute-start | bytes 2555912 | tf_op jit(solution)/shard_map/ppermute | solution.py:803
  490.3 75.1 %all-to-all-start.3 = ((bf16[4,2,128,1536]{3,2,1,0:T(8,128)(2,1)}), bf16[4,2,128,1536]{3,2,1,0:T(8,128)(2,1)}, u32[]{:S(2)}, u32[]{:S(2)}) async-start(bf16[4,2,128,1536]{3,2,1,0:T(8,128)(2,1)} %broadcast_in_dim.127), calls=%async_computation.3 | async-start | bytes 6291456 | tf_op jit(solution)/shard_map/all_to_all | solution.py:794
  495.0 150.6 %reduce-scatter.6.cloned.1.call-start = ((), (), s32[]{:S(2)}) async-start(), calls=%async_computation.9 | async-start | bytes 4423680 | tf_op jit(solution)/shard_map/reduce_scatter | solution.py:952
  512.3 13.7 %collective-permute-start.22 = (bf16[2,128,768]{2,1,0:T(8,128)(2,1)S(1)}, bf16[2,128,768]{2,1,0:T(8,128)(2,1)}, u32[]{:S(2)}, u32[]{:S(2)}) collective-permute-start(bf16[2,128,768]{2,1,0:T(8,128)(2,1)S(1)} %convert_element_type.140), channel_id=1, source_target_pairs={{4,0},{5,1},{6,2},{7,3},{12,8},{13,9},{14,10},{15,11},{20,16},{21,... | collective-permute-start | bytes 1179656 | tf_op jit(solution)/shard_map/ppermute | solution.py:748
  518.6 7.4 copy-start.25
  553.7 13.5 %copy-start.19 = (bf16[1536,128]{1,0:T(8,128)(2,1)S(1)}, bf16[1536,128]{1,0:T(8,128)(2,1)}, u32[]{:S(2)}) copy-start(bf16[1536,128]{1,0:T(8,128)(2,1)} %get-tuple-element.335) | copy-start | bytes 1179652
  553.7 11.8 %collective-permute-start.23 = (f32[2,8,1024]{2,1,0:T(8,128)}, f32[2,8,1024]{2,1,0:T(8,128)}, u32[]{:S(2)}, u32[]{:S(2)}) collective-permute-start(f32[2,8,1024]{2,1,0:T(8,128)} %get-tuple-element.130), channel_id=1, source_target_pairs={{4,0},{5,1},{6,2},{7,3},{12,8},{13,9},{14,10},{15,11},{20,16},{21,... | collective-permute-start | bytes 196616 | tf_op jit(solution)/shard_map/ppermute | solution.py:748
  555.9 5.0 copy-start.28
  565.4 8.0 %slice-start.1 = ((s8[6291456]{0:T(1024)(128)(4,1)}), s8[2097152]{0:T(1024)(128)(4,1)S(1)}, s32[]{:S(2)}) async-start(s8[6291456]{0:T(1024)(128)(4,1)} %bitcast.196), calls=%async_computation.12 | async-start | bytes 4194304
  567.2 6.3 slice-start.2
  594.3 75.7 %all-to-all-start.4 = ((bf16[4,2,128,1536]{3,2,1,0:T(8,128)(2,1)}), bf16[4,2,128,1536]{3,2,1,0:T(8,128)(2,1)S(1)}, u32[]{:S(2)}, u32[]{:S(2)}) async-start(bf16[4,2,128,1536]{3,2,1,0:T(8,128)(2,1)} %get-tuple-element.136), calls=%async_computation.6 | async-start | bytes 6291456 | tf_op jit(solution)/shard_map/all_to_all | solution.py:789
  598.0 175.3 %reduce-scatter.8.cloned.1.call-start = ((), (), s32[]{:S(2)}) async-start(), calls=%async_computation.10 | async-start | bytes 7962624 | tf_op jit(solution)/shard_map/reduce_scatter | solution.py:952
  647.6 24.0 %copy-start.24 = (f32[1536]{0:T(1024)S(1)}, f32[1536]{0:T(1024)}, u32[]{:S(2)}) copy-start(f32[1536]{0:T(1024)} %param.26) | copy-start | bytes 18436
  674.6 5.9 collective-permute-start.24
  680.6 9.2 %collective-permute-start.25 = (bf16[192,384]{1,0:T(8,128)(2,1)S(1)}, bf16[192,384]{1,0:T(8,128)(2,1)S(1)}, u32[]{:S(2)}, u32[]{:S(2)}) collective-permute-start(bf16[192,384]{1,0:T(8,128)(2,1)S(1)} %add_convert_fusion.5), channel_id=1, source_target_pairs={{0,2},{1,3},{2,0},{3,1},{4,6},{5,7},{6,4},{7,5},{8,10},{9,11},{10,... | collective-permute-start | bytes 442376 | tf_op jit(solution)/shard_map/ppermute | solution.py:841
  689.8 7.7 collective-permute-start.31
  698.3 15.3 %collective-permute-start.32 = (bf16[2,192,384]{2,1,0:T(8,128)(2,1)}, bf16[2,192,384]{2,1,0:T(8,128)(2,1)}, u32[]{:S(2)}, u32[]{:S(2)}) collective-permute-start(bf16[2,192,384]{2,1,0:T(8,128)(2,1)} %maximum_select_fusion.2), channel_id=1, source_target_pairs={{0,16},{8,24},{16,0},{24,8},{1,17},{9,25},{17,1},{25,9},{2,18},{10... | collective-permute-start | bytes 884744 | tf_op jit(solution)/shard_map/ppermute | solution.py:841
  704.9 19.3 %collective-permute-start.26 = (bf16[2,128,1536]{2,1,0:T(8,128)(2,1)S(1)}, bf16[2,128,1536]{2,1,0:T(8,128)(2,1)}, u32[]{:S(2)}, u32[]{:S(2)}) collective-permute-start(bf16[2,128,1536]{2,1,0:T(8,128)(2,1)S(1)} %copy-done.8), channel_id=1, source_target_pairs={{0,1},{1,2},{2,3},{4,5},{5,6},{6,7},{8,9},{9,10},{10,11},{12,13},{... | collective-permute-start | bytes 2359304 | tf_op jit(solution)/shard_map/ppermute | solution.py:803
  707.1 40.2 %collective-permute-start.27 = (bf16[2,128,1536]{2,1,0:T(8,128)(2,1)S(1)}, bf16[2,128,1536]{2,1,0:T(8,128)(2,1)S(1)}, u32[]{:S(2)}, u32[]{:S(2)}) collective-permute-start(bf16[2,128,1536]{2,1,0:T(8,128)(2,1)S(1)} %copy-done.8), channel_id=1, source_target_pairs={{0,3},{3,0},{4,7},{7,4},{8,11},{11,8},{12,15},{15,12},{16,19},{19,... | collective-permute-start | bytes 2359304 | tf_op jit(solution)/shard_map/ppermute | solution.py:807
  709.1 36.7 %collective-permute-start.29 = (bf16[2,128,1536]{2,1,0:T(8,128)(2,1)S(1)}, bf16[2,128,1536]{2,1,0:T(8,128)(2,1)}, u32[]{:S(2)}, u32[]{:S(2)}) collective-permute-start(bf16[2,128,1536]{2,1,0:T(8,128)(2,1)S(1)} %copy-done.8), channel_id=1, source_target_pairs={{1,0},{2,1},{3,2},{5,4},{6,5},{7,6},{9,8},{10,9},{11,10},{13,12},{... | collective-permute-start | bytes 2359304 | tf_op jit(solution)/shard_map/ppermute | solution.py:803
  715.0 32.5 %collective-permute-start.33 = (bf16[4,192,384]{2,1,0:T(8,128)(2,1)S(1)}, bf16[4,192,384]{2,1,0:T(8,128)(2,1)S(1)}, u32[]{:S(2)}, u32[]{:S(2)}) collective-permute-start(bf16[4,192,384]{2,1,0:T(8,128)(2,1)S(1)} %maximum_select_fusion.1), channel_id=1, source_target_pairs={{0,4},{4,0},{1,5},{5,1},{2,6},{6,2},{3,7},{7,3},{8,12},{12,8},{9,1... | collective-permute-start | bytes 1769480 | tf_op jit(solution)/shard_map/ppermute | solution.py:841
  724.1 36.0 %collective-permute-start.28 = (bf16[2,128,1536]{2,1,0:T(8,128)(2,1)}, bf16[2,128,1536]{2,1,0:T(8,128)(2,1)}, u32[]{:S(2)}, u32[]{:S(2)}) collective-permute-start(bf16[2,128,1536]{2,1,0:T(8,128)(2,1)} %collective-permute-done.26), channel_id=1, source_target_pairs={{1,2},{2,3},{5,6},{6,7},{9,10},{10,11},{13,14},{14,15},{17,18},{18... | collective-permute-start | bytes 2359304 | tf_op jit(solution)/shard_map/ppermute | solution.py:803
  745.7 21.7 %collective-permute-start.30 = (bf16[2,128,1536]{2,1,0:T(8,128)(2,1)}, bf16[2,128,1536]{2,1,0:T(8,128)(2,1)}, u32[]{:S(2)}, u32[]{:S(2)}) collective-permute-start(bf16[2,128,1536]{2,1,0:T(8,128)(2,1)} %collective-permute-done.29), channel_id=1, source_target_pairs={{1,0},{2,1},{5,4},{6,5},{9,8},{10,9},{13,12},{14,13},{17,16},{18,1... | collective-permute-start | bytes 2359304 | tf_op jit(solution)/shard_map/ppermute | solution.py:803
  773.3 4.8 copy-start.9
  (23 other events, 50.9 us)
Sparse Core Ops, SparseCore 0:
  418.2 94.2 reduce-scatter.3
  594.4 51.1 reduce-scatter.5
  670.1 70.9 reduce-scatter.7

commit v4 on v3

--- a/solution.py
+++ b/solution.py
@@ -512,9 +512,11 @@
 
         if extra is not None:
 
-            @pl.when(j >= starts[-1])
+            @pl.when(j == starts[-1] - 1)
             def _():
-                out[...] = refs[count][...]
+                added = refs[count]
+                room = tile - added.shape[1]
+                out[:, room:] = (out[:, room:].astype(f32) + added[...].astype(f32)).astype(bf16)
 
     specs = []
     for g, group in enumerate(groups):
@@ -526,8 +528,7 @@
     steps = starts[-1]
     if extra is not None:
         flat = flat + [extra]
-        specs.append(pl.BlockSpec((depth, tile), lambda j, a=steps: (0, jnp.maximum(j - a, 0))))
-        steps += extra.shape[1] // tile
+        specs.append(pl.BlockSpec(extra.shape, lambda j: (0, 0)))
     return pl.pallas_call(
         kernel,
         grid=(steps,),
@@ -794,7 +795,7 @@
     return lax.all_to_all(copies, "head", split_axis=0, concat_axis=0, tiled=True)
 
 
-def relay(part):
+def relay(part, *beside):
     count, place = lax.axis_size("head"), lax.axis_index("head")
 
     def passed(array, by, start=0):
@@ -806,17 +807,21 @@
         up, down = passed(part, 1), passed(part, -1)
         far = lax.ppermute(part, "head", [(0, 3), (3, 0)])
         up_two, down_two = passed(up, 1, 1), passed(down, -1, 1)
-        return [
+        if beside:
+            far, *beside = tie(far, *beside)
+        pieces = [
             part,
             jnp.where(place >= 1, up, far),
             jnp.where(place >= 2, up_two, down_two),
             jnp.where(place >= 3, far, down),
         ]
+        return (pieces, *beside) if beside else pieces
     up, down = [part], [part]
     for _ in range(count - 1):
         up.append(passed(up[-1], 1))
         down.append(passed(down[-1], -1))
-    return [part] + [jnp.where(place >= d, up[d], down[count - d]) for d in range(1, count)]
+    pieces = [part] + [jnp.where(place >= d, up[d], down[count - d]) for d in range(1, count)]
+    return (pieces, *beside) if beside else pieces
 
 
 def laid(pieces, axis=0):
@@ -963,6 +968,7 @@
     step_raw = times(normed_one, w_step)[..., :heads_dev]
     gate_z = times(normed_one, w_in_zx[0])
     edge_rows = shifted(conv_in[head_count - 1, :, share_rows - 8 :].astype(f32), "seq", 1)
+    edge_rows, gate_z = tie(edge_rows, gate_z)
     taps = jnp.concatenate([conv_x, conv_bc], axis=1)
     bias = jnp.concatenate([conv_x_bias, conv_bc_bias])
     taps_bias = jnp.concatenate([taps, bias[None], jnp.zeros((7 - conv_taps, conv_width), f32)])
@@ -1107,32 +1113,38 @@
         whole(jnp.sum(channel_sums[1].reshape(heads_dev, head_size), axis=-1)),
     ]
     sizes = [a.shape[0] for a in small]
-    small = jnp.concatenate(small + [jnp.zeros((128 * model_width - sum(sizes),), f32)])
+    skipped = 16 * model_width
+    small = [jnp.zeros((skipped,), f32)] + small
+    small = jnp.concatenate(small + [jnp.zeros((128 * model_width - skipped - sum(sizes),), f32)])
     small = small.reshape(128, model_width).T.astype(bf16)
-    grad_late = weight_grads([[(flat(normed_one), flat(in_grad))]], model_width, 128, small)
+    grad_late = weight_grads([[(flat(normed_one), flat(in_grad))]], model_width, 384, small)
     early_terms = [[(flat(out_push), flat(gated_low))], [(flat(normed_one), flat(z_grad))]]
     grad_early = weight_grads(early_terms + shared_terms, model_width, 256)
-    late_sum = scattered(grad_late, ("dp", "seq")).astype(f32)
+    late_sum = scattered(grad_late, ("dp", "seq"))
     late_sum, got_dn = tie(late_sum, got_dn)
     input_grad = on_share(
         after_proj_kernel, got_dn, [x_share, hidden_grad], [norm1_gain[None]], [(model_width, bf16)]
     )[0]
-    merged = jnp.concatenate([late_sum[:, inner_dev:conv_width], late_sum[:, conv_width + 128 :]], axis=1)
+    merged = late_sum[:, inner_dev:]
     for bit in bits_of("head"):
         merged = merged.astype(bf16)
         merged = merged.astype(f32) + across(merged, "head", bit).astype(f32)
     merged = merged.astype(bf16)
     input_grad, merged = tie(input_grad, merged)
+    late_sum, grad_early = tie(late_sum, grad_early)
+    early_sum = scattered(grad_early, ("dp", "seq")).astype(f32)
+    pieces, merged, layer_out, late_sum, expert_sum = relay(
+        input_grad, merged, layer_out, late_sum, expert_sum
+    )
+    late_sum = late_sum.astype(f32)
     merged = join_over(merged[None], 0, "dp", "seq")
     merged = jnp.swapaxes(merged.reshape((seq_count, -1) + merged.shape[1:]), 0, 1)
     merged = merged.reshape(model_width, -1).astype(f32)
     layer_out = by_position(layer_out)
-    late_sum, grad_early = tie(late_sum, grad_early)
-    early_sum = scattered(grad_early, ("dp", "seq")).astype(f32)
-    d_input = relay_shares(input_grad, 1).reshape(batch_size, tokens, model_width)
+    d_input = laid(pieces, 1).reshape(batch_size, tokens, model_width)
 
     grad_bc = merged[:, : 2 * state_size]
-    small = merged[:, 2 * state_size :].T.reshape(-1)
+    small = merged[:, 2 * state_size + 16 :].T.reshape(-1)
     ends = [sum(sizes[:k]) for k in range(len(sizes) + 1)]
     small = [small[ends[k] : ends[k + 1]] for k in range(len(sizes))]
     expert_sum = expert_sum.astype(f32)

time: 796 us -> 785 us (0.986)
  waiting for transfers between devices: 316 us -> 306 us
    all_to_all x4, waiting for transfers between devices: 78.9 us -> 107 us  [swap_shares(): return lax.all_to_all(part, 'head', split_axis=0, concat_axis=0, tiled=True)]
    reduce_scatter x3, waiting for transfers between devices: 26.5 us -> 0.01 us  [scattered(): return lax.psum_scatter(array, axes, scatter_dimension=0, tiled=True)]
    ppermute x12, waiting for transfers between devices: 118 us -> 94.5 us  [passed(): return lax.ppermute(array, 'head', pairs)]
    ppermute x3, waiting for transfers between devices: 14.6 us -> 31 us  [relay(): far = lax.ppermute(part, 'head', [(0, 3), (3, 0)])]
  transfers between devices with their start and end apart: 42 -> 42, of which waited for: 22 -> 20; matrix products, arithmetic and copies ran while one was open for 15% -> 15% of each run, Pallas kernels for 21% -> 21%
where the time goes in v4:
time: 785 us; the launch traced here: 774 us
  waiting for transfers between devices  306 us (39%)
  Pallas kernels  225 us (29%)
  local copies, waits for them, and re-layouts  79.5 us (10%)
  starting transfers between devices  74.1 us (9%)
  other arithmetic  43 us (5%)
  matrix products  32.5 us (4%)
  between operations  15 us (2%)
    all_to_all x4, waiting for transfers between devices, swap_shares(): return lax.all_to_all(part, 'head', split_axis=0, concat_axis=0, tiled=True)  107 us
    ppermute x12, waiting for transfers between devices, passed(): return lax.ppermute(array, 'head', pairs)  94.5 us
    ppermute x7, waiting for transfers between devices, across(): lax.ppermute(array, axis, [(i, i ^ bit) for i in range(lax.axis_size(axis...  64.2 us
    pallas_call x3, Pallas kernels, weight_grads(): pl.pallas_call(kernel, grid=(steps,), in_specs=specs, out_specs=pl.BlockS...  62.8 us
    pallas_call x2, Pallas kernels, experts_backward(): pl.pallas_call(lambda *refs: expert_backward_kernel(bool(shared), *refs),...  42.4 us
    pallas_call x2, Pallas kernels, experts_forward(): pl.pallas_call(lambda *refs: expert_forward_kernel(bool(shared), *refs),...  39.7 us
    ppermute x3, waiting for transfers between devices, relay(): far = lax.ppermute(part, 'head', [(0, 3), (3, 0)])  31 us
    pallas_call x1, Pallas kernels, scan_backward(): pl.pallas_call(scan_back_kernel, grid=(batch, blocks), in_specs=[rows_of(...  25.7 us
  transfers between devices with their start and end apart: 42, of which 20 were waited for; matrix products, arithmetic and copies ran while one was open for 15% of the time, Pallas kernels for 21%

profile of v4, /device:TPU:0, one launch (start us, length us, event | category | flops | bytes accessed | tf_op | source)
XLA Modules:
  0.0 774.3 jit_solution(17540142276195277497)
XLA Ops:
  7.2 2.6 fusion
  14.1 3.7 fusion.19.cin.cin_before
  19.8 3.0 collective-permute-start
  22.8 4.3 fusion.15.z
  29.0 3.7 fusion.21.raw
  35.1 14.4 %shard_map.365 = (bf16[4,2,128,1024]{3,2,1,0:T(8,128)(2,1)}, f32[4,2,128,768]{3,2,1,0:T(8,128)}, f32[2,2,128,768]{3,2,1,0:T(8,128)}, f32[2,128,768]{2,1,0:T(8,128)}) custom-call(bf16[4,2,128,1024]{3,2,1,0:T(8,128)(2,1)} %copy-done.4, f32[2,8,1024]{2,1,0:T(8,128)} %collective-permute-done.edge, f32[8,1024]{1,0:T(8,128)} %maximum_maximum_fusion.taps.taps_ref, ...), custom_call_target="tpu_custom_call" | custom-call | flops 1207959552 | bytes 7864320 | tf_op jit(solution)/shard_map/pallas_call | solution.py:310
  49.5 2.2 collective-permute-start.1
  54.4 12.2 %shard_map.366 = (bf16[4,2,128,768]{3,2,1,0:T(8,128)(2,1)}, bf16[4,2,128,768]{3,2,1,0:T(8,128)(2,1)}, f32[4,2,128,128]{3,2,1,0:T(8,128)}, bf16[4,2,128,1536]{3,2,1,0:T(8,128)(2,1)}) custom-call(f32[4,2,128,768]{3,2,1,0:T(8,128)} %get-tuple-element.93.y, bf16[4,2,128,1024]{3,2,1,0:T(8,128)(2,1)} %get-tuple-element.92.act_in, f32[4,2,128,768]{3,2,1,0:T(8,128)} %fusion.15.z, ...), custom_call_target="tpu_custom_call" | custom-call | flops 2617245696 | bytes 14155776 | tf_op jit(solution)/shard_map/pallas_call | solution.py:346
  66.7 5.9 all-to-all-start
  72.6 3.8 copy.286
  78.7 2.1 collective-permute-start.3
  80.8 41.9 %collective-permute-done.3 = f32[4,2,128]{2,1,0:T(2,128)S(1)} collective-permute-done((f32[4,2,128]{2,1,0:T(2,128)S(1)}, f32[4,2,128]{2,1,0:T(2,128)S(1)}, u32[]{:S(2)}, u32[]{:S(2)}) %collective-permute-start.3) | collective-permute-done | bytes 4128 | tf_op jit(solution)/shard_map/ppermute | solution.py:846
  122.7 4.7 collective-permute-start.4
  129.6 13.0 %collective-permute-done.4 = f32[4,2,128]{2,1,0:T(2,128)S(1)} collective-permute-done((f32[4,2,128]{2,1,0:T(2,128)S(1)}, f32[4,2,128]{2,1,0:T(2,128)S(1)}, u32[]{:S(2)}, u32[]{:S(2)}) %collective-permute-start.4) | collective-permute-done | bytes 4128 | tf_op jit(solution)/shard_map/ppermute | solution.py:846
  143.5 4.2 shard_map.367
  147.7 2.2 collective-permute-start.6
  149.9 2.5 collective-permute-start.7
  155.0 13.7 %collective-permute-done.6 = bf16[2,128,1664]{2,1,0:T(8,128)(2,1)} collective-permute-done((bf16[2,128,1664]{2,1,0:T(8,128)(2,1)}, bf16[2,128,1664]{2,1,0:T(8,128)(2,1)}, u32[]{:S(2)}, u32[]{:S(2)}) %collective-permute-start.6) | collective-permute-done | bytes 852000 | tf_op jit(solution)/shard_map/ppermute | solution.py:804
  169.4 22.7 %collective-permute-done.10 = bf16[2,128,1664]{2,1,0:T(8,128)(2,1)} collective-permute-done((bf16[2,128,1664]{2,1,0:T(8,128)(2,1)}, bf16[2,128,1664]{2,1,0:T(8,128)(2,1)}, u32[]{:S(2)}, u32[]{:S(2)}) %collective-permute-start.10) | collective-permute-done | bytes 852000 | tf_op jit(solution)/shard_map/ppermute | solution.py:804
  198.0 17.1 %collective-permute-done.11 = bf16[2,128,1664]{2,1,0:T(8,128)(2,1)S(1)} collective-permute-done((bf16[2,128,1664]{2,1,0:T(8,128)(2,1)}, bf16[2,128,1664]{2,1,0:T(8,128)(2,1)S(1)}, u32[]{:S(2)}, u32[]{:S(2)}) %collective-permute-start.11) | collective-permute-done | bytes 852000 | tf_op jit(solution)/shard_map/ppermute | solution.py:804
  220.9 18.4 %shard_map.368 = (bf16[1024,1536]{1,0:T(8,128)(2,1)}, f32[1024,16]{1,0:T(8,128)}, f32[1024,2048]{1,0:T(8,128)}) custom-call(bf16[1024,1664]{1,0:T(8,128)(2,1)} %bitcast.25.refs_0_.refs_2_.refs_1_, bf16[1024,1536]{1,0:T(8,128)(2,1)} %bitcast.17.refs_1_.refs_0_.refs_4_, bf16[1024,1664]{1,0:T(8,128)(2,1)} %bitcast.25.refs_0_.refs_2_.refs_1_, ...), custom_call_target="tpu_custom_call" | custom-call | flops 9663676416 | bytes 27262976 | tf_op jit(solution)/shard_map/pallas_call | solution.py:631
  239.3 21.4 %shard_map.370 = (bf16[1024,1536]{1,0:T(8,128)(2,1)}, f32[1024,16]{1,0:T(8,128)}, f32[1024,2560]{1,0:T(8,128)}) custom-call(bf16[1024,1664]{1,0:T(8,128)(2,1)} %bitcast.184, bf16[1024,1536]{1,0:T(8,128)(2,1)} %bitcast.16.refs_1_.refs_0_.refs_6_, bf16[1024,1664]{1,0:T(8,128)(2,1)} %bitcast.185, f32[8,16]{1,0:T(8,128)} %fusion.27.refs_3_, ...), custom_call_target="tpu_custom_call" | custom-call | flops 12079595520 | bytes 31719424 | tf_op jit(solution)/shard_map/pallas_call | solution.py:631
  260.7 4.4 add_convert_fusion.1
  265.0 5.1 all-to-all-start.1
  270.1 18.0 %shard_map.369 = (bf16[1024,1536]{1,0:T(8,128)(2,1)}, bf16[1024,1024]{1,0:T(8,128)(2,1)}, bf16[1024,2048]{1,0:T(8,128)(2,1)}) custom-call(bf16[1024,1536]{1,0:T(8,128)(2,1)} %bitcast.17.refs_1_.refs_0_.refs_4_, bf16[1024,1664]{1,0:T(8,128)(2,1)} %bitcast.25.refs_0_.refs_2_.refs_1_, f32[1024,2048]{1,0:T(8,128)} %get-tuple-element.102.refs_2_, ...), custom_call_target="tpu_custom_call" | custom-call | flops 9663676416 | bytes 30408704 | tf_op jit(solution)/shard_map/pallas_call | solution.py:651
  288.7 5.9 collective-permute-done.16
  294.6 24.3 %shard_map.371 = (bf16[1024,1536]{1,0:T(8,128)(2,1)}, bf16[1024,1024]{1,0:T(8,128)(2,1)}, bf16[1024,2048]{1,0:T(8,128)(2,1)}, bf16[1024,256]{1,0:T(8,128)(2,1)}, bf16[1024,512]{1,0:T(8,128)(2,1)}) custom-call(bf16[1024,1536]{1,0:T(8,128)(2,1)} %bitcast.16.refs_1_.refs_0_.refs_6_, bf16[1024,1664]{1,0:T(8,128)(2,1)} %bitcast.186, ...), custom_call_target="tpu_custom_call" | custom-call | flops 12079595520 | bytes 36438016 | tf_op jit(solution)/shard_map/pallas_call | solution.py:651
  319.0 4.6 add_convert_fusion
  323.5 18.2 %all-to-all-done.1 = bf16[4,2,128,1536]{3,2,1,0:T(8,128)(2,1)} async-done(((bf16[4,2,128,1536]{3,2,1,0:T(8,128)(2,1)}), bf16[4,2,128,1536]{3,2,1,0:T(8,128)(2,1)}, u32[]{:S(2)}, u32[]{:S(2)}) %all-to-all-start.1) | async-done | bytes 3145760 | tf_op jit(solution)/shard_map/all_to_all | solution.py:790
  341.7 4.7 all-to-all-start.2
  346.6 32.2 %shard_map.372 = bf16[1536,3072]{1,0:T(8,128)(2,1)} custom-call(bf16[1024,1664]{1,0:T(8,128)(2,1)} %bitcast.25.refs_0_.refs_2_.refs_1_, bf16[1024,2048]{1,0:T(8,128)(2,1)} %get-tuple-element.118.refs_1_, bf16[1024,1664]{1,0:T(8,128)(2,1)} %bitcast.187, bf16[1024,2048]{1,0:T(8,128)(2,1)} %get-tuple-element.119.refs_3_, ...), custom_call_target="tpu_custom_call" | custom-call | flops 19327352832 | bytes 34603008 | tf_op jit(solution)/shard_map/pallas_call | solution.py:532
  378.8 38.4 %all-to-all-done.2.refs_0_ = bf16[4,2,128,1536]{3,2,1,0:T(8,128)(2,1)} async-done(((bf16[4,2,128,1536]{3,2,1,0:T(8,128)(2,1)}), bf16[4,2,128,1536]{3,2,1,0:T(8,128)(2,1)}, u32[]{:S(2)}, u32[]{:S(2)}) %all-to-all-start.2) | async-done | bytes 3145760 | tf_op jit(solution)/shard_map/all_to_all | solution.py:790
  417.3 2.1 dynamic-slice_bitcast_fusion.refs_4_
  419.4 5.0 shard_map.373
  427.1 6.6 collective-permute-start.18
  433.7 2.3 fusion.20
  436.1 9.4 %collective-permute-done.17 = bf16[2,128,1664]{2,1,0:T(8,128)(2,1)S(1)} collective-permute-done((bf16[2,128,1664]{2,1,0:T(8,128)(2,1)}, bf16[2,128,1664]{2,1,0:T(8,128)(2,1)S(1)}, u32[]{:S(2)}, u32[]{:S(2)}) %collective-permute-start.17) | collective-permute-done | bytes 852000 | tf_op jit(solution)/shard_map/ppermute | solution.py:804
  446.2 2.8 collective-permute-done.20
  453.1 14.5 %collective-permute-done.18 = bf16[2,128,1664]{2,1,0:T(8,128)(2,1)S(1)} collective-permute-done((bf16[2,128,1664]{2,1,0:T(8,128)(2,1)}, bf16[2,128,1664]{2,1,0:T(8,128)(2,1)S(1)}, u32[]{:S(2)}, u32[]{:S(2)}) %collective-permute-start.18) | collective-permute-done | bytes 852000 | tf_op jit(solution)/shard_map/ppermute | solution.py:808
  468.8 16.3 %collective-permute-done.21 = bf16[2,128,1664]{2,1,0:T(8,128)(2,1)S(1)} collective-permute-done((bf16[2,128,1664]{2,1,0:T(8,128)(2,1)S(1)}, bf16[2,128,1664]{2,1,0:T(8,128)(2,1)S(1)}, u32[]{:S(2)}, u32[]{:S(2)}) %collective-permute-start.21) | collective-permute-done | bytes 852000 | tf_op jit(solution)/shard_map/ppermute | solution.py:804
  489.5 4.6 all-to-all-start.3
  494.4 2.6 fusion.36
  498.6 11.7 %shard_map.374 = (bf16[4,2,128,768]{3,2,1,0:T(8,128)(2,1)}, bf16[4,2,128,768]{3,2,1,0:T(8,128)(2,1)}, f32[2,128,768]{2,1,0:T(8,128)}, f32[8,768]{1,0:T(8,128)}) custom-call(bf16[4,2,128,1664]{3,2,1,0:T(8,128)(2,1)} %bitcast_dynamic-update-slice_fusion.push.slope_in, bf16[768,1536]{1,0:T(8,128)(2,1)} %w_out.3, ...), custom_call_target="tpu_custom_call" | custom-call | flops 2617245696 | bytes 14155776 | tf_op jit(solution)/shard_map/pallas_call | solution.py:379
  517.7 7.4 fusion.13
  527.1 25.7 %shard_map.375 = (bf16[4,2,128,1152]{3,2,1,0:T(8,128)(2,1)}, f32[2,8,1024]{2,1,0:T(8,128)}, f32[2,8,1024]{2,1,0:T(8,128)}, f32[8,1024]{1,0:T(8,128)}) custom-call(bf16[4,2,128,1024]{3,2,1,0:T(8,128)(2,1)} %copy-done.4, bf16[4,2,128,1024]{3,2,1,0:T(8,128)(2,1)} %copy-done.4, f32[2,8,1024]{2,1,0:T(8,128)} %collective-permute-done.edge, ...), custom_call_target="tpu_custom_call" | custom-call | flops 2617245696 | bytes 11796480 | tf_op jit(solution)/shard_map/pallas_call | solution.py:413
  562.1 2.5 all-to-all-done.3
  566.3 6.2 fusion.5
  572.7 2.4 fusion.4
  575.2 3.2 concatenate.43
  579.8 9.8 %shard_map.377 = bf16[1536,1152]{1,0:T(8,128)(2,1)} custom-call(bf16[1024,1536]{1,0:T(8,128)(2,1)} %bitcast.192, bf16[1024,1152]{1,0:T(8,128)(2,1)} %bitcast.202, bf16[1536,128]{1,0:T(8,128)(2,1)} %bitcast.207), custom_call_target="tpu_custom_call" | custom-call | flops 3623878656 | bytes 9830400 | tf_op jit(solution)/shard_map/pallas_call | solution.py:532
  589.6 3.7 all-to-all-start.4
  593.6 20.9 %shard_map.379 = bf16[1536,2304]{1,0:T(8,128)(2,1)} custom-call(bf16[1024,1664]{1,0:T(8,128)(2,1)} %bitcast.46.refs_0_, bf16[1024,768]{1,0:T(8,128)(2,1)} %bitcast.217, bf16[1024,1536]{1,0:T(8,128)(2,1)} %bitcast.193, bf16[1024,768]{1,0:T(8,128)(2,1)} %bitcast.218, bf16[1024,1664]{1,0:T(8,128)(2,1)} %bitcast.189, ...), custom_call_target="tpu_custom_call" | custom-call | flops 7247757312 | bytes 32243712 | tf_op jit(solution)/shard_map/pallas_call | solution.py:532
  614.4 50.8 %all-to-all-done.4.got = bf16[4,2,128,1536]{3,2,1,0:T(8,128)(2,1)S(1)} async-done(((bf16[4,2,128,1536]{3,2,1,0:T(8,128)(2,1)}), bf16[4,2,128,1536]{3,2,1,0:T(8,128)(2,1)S(1)}, u32[]{:S(2)}, u32[]{:S(2)}) %all-to-all-start.4) | async-done | bytes 3145760 | tf_op jit(solution)/shard_map/all_to_all | solution.py:790
  668.0 5.9 collective-permute-done.24
  675.7 4.8 shard_map.378
  680.5 3.4 collective-permute-done.25
  684.0 3.3 collective-permute-start.26
  687.4 2.2 collective-permute-start.27
  692.0 16.5 %collective-permute-done.26 = bf16[2,128,1536]{2,1,0:T(8,128)(2,1)} collective-permute-done((bf16[2,128,1536]{2,1,0:T(8,128)(2,1)}, bf16[2,128,1536]{2,1,0:T(8,128)(2,1)}, u32[]{:S(2)}, u32[]{:S(2)}) %collective-permute-start.26) | collective-permute-done | bytes 786464 | tf_op jit(solution)/shard_map/ppermute | solution.py:808
  710.3 2.2 convert_element_type.156
  712.6 9.0 %collective-permute-done.27 = bf16[2,128,1536]{2,1,0:T(8,128)(2,1)} collective-permute-done((bf16[2,128,1536]{2,1,0:T(8,128)(2,1)}, bf16[2,128,1536]{2,1,0:T(8,128)(2,1)}, u32[]{:S(2)}, u32[]{:S(2)}) %collective-permute-start.27) | collective-permute-done | bytes 786464 | tf_op jit(solution)/shard_map/ppermute | solution.py:804
  734.0 3.8 copy.256
  738.4 3.0 copy.267
  744.6 2.4 collective-permute-done.30
  (283 shorter events, 117.1 us)
Async XLA Ops:
  12.4 10.4 %slice-start.2 = ((s8[4718592]{0:T(1024)(128)(4,1)}), s8[4194304]{0:T(1024)(128)(4,1)S(1)}, s32[]{:S(2)}) async-start(s8[4718592]{0:T(1024)(128)(4,1)} %bitcast.203), calls=%async_computation.13 | async-start | bytes 8388608
  14.1 8.7 %copy-start.3 = (bf16[4,2,128,1536]{3,2,1,0:T(8,128)(2,1)}, bf16[4,2,128,1536]{3,2,1,0:T(8,128)(2,1)S(1)}, u32[]{:S(2)}) copy-start(bf16[4,2,128,1536]{3,2,1,0:T(8,128)(2,1)S(1)} %fusion.2) | copy-start | bytes 9437188
  14.1 8.7 %slice-start.3 = ((s8[4718592]{0:T(1024)(128)(4,1)}), s8[524288]{0:T(1024)(128)(4,1)S(1)}, s32[]{:S(2)}) async-start(s8[4718592]{0:T(1024)(128)(4,1)} %bitcast.203), calls=%async_computation.14 | async-start | bytes 1048576
  19.8 15.3 %collective-permute-start = (f32[2,8,1024]{2,1,0:T(8,128)}, f32[2,8,1024]{2,1,0:T(8,128)}, u32[]{:S(2)}, u32[]{:S(2)}) collective-permute-start(f32[2,8,1024]{2,1,0:T(8,128)} %fusion.24), channel_id=1, source_target_pairs={{0,4},{1,5},{2,6},{3,7},{8,12},{9,13},{10,14},{11,15},{16,20},{17,... | collective-permute-start | bytes 196616 | tf_op jit(solution)/shard_map/ppermute | solution.py:749
  27.1 5.7 copy-start.28
  28.1 4.6 copy-start.32
  28.1 4.6 copy-start.33
  35.1 18.0 %copy-start.35 = (f32[12]{0:T(128)S(1)}, f32[12]{0:T(128)}, u32[]{:S(2)}) copy-start(f32[12]{0:T(128)} %param.35) | copy-start | bytes 148
  35.1 18.7 %copy-start.31 = (f32[768]{0:T(1024)S(1)}, f32[768]{0:T(1024)}, u32[]{:S(2)}) copy-start(f32[768]{0:T(1024)} %param.36) | copy-start | bytes 9220
  49.5 4.9 collective-permute-start.1
  66.7 76.8 %all-to-all-start = ((bf16[4,2,128,1536]{3,2,1,0:T(8,128)(2,1)}), bf16[4,2,128,1536]{3,2,1,0:T(8,128)(2,1)}, u32[]{:S(2)}, u32[]{:S(2)}) async-start(bf16[4,2,128,1536]{3,2,1,0:T(8,128)(2,1)} %get-tuple-element.96), calls=%async_computation | async-start | bytes 6291456 | tf_op jit(solution)/shard_map/all_to_all | solution.py:790
  72.6 55.5 %copy-start.30 = (f32[1536]{0:T(1024)S(1)}, f32[1536]{0:T(1024)}, u32[]{:S(2)}) copy-start(f32[1536]{0:T(1024)} %param.38) | copy-start | bytes 18436
  72.6 56.1 %copy-start.19 = (bf16[1536,16]{0,1:T(8,128)(2,1)S(1)}, bf16[1536,16]{0,1:T(8,128)(2,1)}, u32[]{:S(2)}) copy-start(bf16[1536,16]{0,1:T(8,128)(2,1)} %param.39) | copy-start | bytes 147460
  76.4 67.1 %collective-permute-start.2 = (bf16[4,2,128,1536]{3,2,1,0:T(8,128)(2,1)}, bf16[4,2,128,1536]{3,2,1,0:T(8,128)(2,1)}, u32[]{:S(2)}, u32[]{:S(2)}) collective-permute-start(bf16[4,2,128,1536]{3,2,1,0:T(8,128)(2,1)} %bitcast.180), channel_id=1, source_target_pairs={{0,4},{4,0},{1,5},{5,1},{2,6},{6,2},{3,7},{7,3},{8,12},{12,8},{9,1... | collective-permute-start | bytes 9437192 | tf_op jit(solution)/shard_map/ppermute | solution.py:877
  78.7 44.0 %collective-permute-start.3 = (f32[4,2,128]{2,1,0:T(2,128)S(1)}, f32[4,2,128]{2,1,0:T(2,128)S(1)}, u32[]{:S(2)}, u32[]{:S(2)}) collective-permute-start(f32[4,2,128]{2,1,0:T(2,128)S(1)} %slice_reduce_fusion.2), channel_id=1, source_target_pairs={{0,1},{1,0},{2,3},{3,2},{4,5},{5,4},{6,7},{7,6},{8,9},{9,8},{10,11... | collective-permute-start | bytes 12296 | tf_op jit(solution)/shard_map/ppermute | solution.py:846
  122.7 20.0 %collective-permute-start.4 = (f32[4,2,128]{2,1,0:T(2,128)S(1)}, f32[4,2,128]{2,1,0:T(2,128)S(1)}, u32[]{:S(2)}, u32[]{:S(2)}) collective-permute-start(f32[4,2,128]{2,1,0:T(2,128)S(1)} %add.179), channel_id=1, source_target_pairs={{0,2},{1,3},{2,0},{3,1},{4,6},{5,7},{6,4},{7,5},{8,10},{9,11},{10,... | collective-permute-start | bytes 12296 | tf_op jit(solution)/shard_map/ppermute | solution.py:846
  147.7 21.0 %collective-permute-start.6 = (bf16[2,128,1664]{2,1,0:T(8,128)(2,1)}, bf16[2,128,1664]{2,1,0:T(8,128)(2,1)}, u32[]{:S(2)}, u32[]{:S(2)}) collective-permute-start(bf16[2,128,1664]{2,1,0:T(8,128)(2,1)} %get-tuple-element.101), channel_id=1, source_target_pairs={{0,1},{1,2},{2,3},{4,5},{5,6},{6,7},{8,9},{9,10},{10,11},{12,13},{... | collective-permute-start | bytes 2555912 | tf_op jit(solution)/shard_map/ppermute | solution.py:804
  149.9 43.5 %collective-permute-start.7 = (bf16[2,128,1664]{2,1,0:T(8,128)(2,1)}, bf16[2,128,1664]{2,1,0:T(8,128)(2,1)}, u32[]{:S(2)}, u32[]{:S(2)}) collective-permute-start(bf16[2,128,1664]{2,1,0:T(8,128)(2,1)} %get-tuple-element.101), channel_id=1, source_target_pairs={{0,3},{3,0},{4,7},{7,4},{8,11},{11,8},{12,15},{15,12},{16,19},{19,... | collective-permute-start | bytes 2555912 | tf_op jit(solution)/shard_map/ppermute | solution.py:808
  152.4 39.8 %collective-permute-start.10 = (bf16[2,128,1664]{2,1,0:T(8,128)(2,1)}, bf16[2,128,1664]{2,1,0:T(8,128)(2,1)}, u32[]{:S(2)}, u32[]{:S(2)}) collective-permute-start(bf16[2,128,1664]{2,1,0:T(8,128)(2,1)} %get-tuple-element.101), channel_id=1, source_target_pairs={{1,0},{2,1},{3,2},{5,4},{6,5},{7,6},{9,8},{10,9},{11,10},{13,12},{... | collective-permute-start | bytes 2555912 | tf_op jit(solution)/shard_map/ppermute | solution.py:804
  154.4 40.5 %collective-permute-start.5 = (bf16[2,128,1664]{2,1,0:T(8,128)(2,1)}, bf16[2,128,1664]{2,1,0:T(8,128)(2,1)S(1)}, u32[]{:S(2)}, u32[]{:S(2)}) collective-permute-start(bf16[2,128,1664]{2,1,0:T(8,128)(2,1)} %get-tuple-element.101), channel_id=1, source_target_pairs={{0,4},{4,0},{1,5},{5,1},{2,6},{6,2},{3,7},{7,3},{8,12},{12,8},{9,1... | collective-permute-start | bytes 2555912 | tf_op jit(solution)/shard_map/ppermute | solution.py:877
  168.7 29.3 %collective-permute-start.9 = (bf16[2,128,1664]{2,1,0:T(8,128)(2,1)}, bf16[2,128,1664]{2,1,0:T(8,128)(2,1)S(1)}, u32[]{:S(2)}, u32[]{:S(2)}) collective-permute-start(bf16[2,128,1664]{2,1,0:T(8,128)(2,1)} %collective-permute-done.6), channel_id=1, source_target_pairs={{1,2},{2,3},{5,6},{6,7},{9,10},{10,11},{13,14},{14,15},{17,18},{18... | collective-permute-start | bytes 2555912 | tf_op jit(solution)/shard_map/ppermute | solution.py:804
  192.1 23.0 %collective-permute-start.11 = (bf16[2,128,1664]{2,1,0:T(8,128)(2,1)}, bf16[2,128,1664]{2,1,0:T(8,128)(2,1)S(1)}, u32[]{:S(2)}, u32[]{:S(2)}) collective-permute-start(bf16[2,128,1664]{2,1,0:T(8,128)(2,1)} %collective-permute-done.10), channel_id=1, source_target_pairs={{1,0},{2,1},{5,4},{6,5},{9,8},{10,9},{13,12},{14,13},{17,16},{18,1... | collective-permute-start | bytes 2555912 | tf_op jit(solution)/shard_map/ppermute | solution.py:804
  194.9 22.6 %collective-permute-start.8 = (bf16[2,128,1664]{2,1,0:T(8,128)(2,1)S(1)}, bf16[2,128,1664]{2,1,0:T(8,128)(2,1)S(1)}, u32[]{:S(2)}, u32[]{:S(2)}) collective-permute-start(bf16[2,128,1664]{2,1,0:T(8,128)(2,1)S(1)} %get-tuple-element.331), channel_id=1, source_target_pairs={{0,4},{4,0},{1,5},{5,1},{2,6},{6,2},{3,7},{7,3},{8,12},{12,8},{9,1... | collective-permute-start | bytes 2555912 | tf_op jit(solution)/shard_map/ppermute | solution.py:877
  215.4 3.5 collective-permute-start.12
  216.9 22.4 %copy-start.1 = (bf16[4,2,128,1664]{3,2,1,0:T(8,128)(2,1)}, bf16[4,2,128,1664]{3,2,1,0:T(8,128)(2,1)S(1)}, u32[]{:S(2)}) copy-start(bf16[4,2,128,1664]{3,2,1,0:T(8,128)(2,1)S(1)} %get-tuple-element.326) | copy-start | bytes 10223620
  216.9 3.0 collective-permute-start.13
  239.3 21.4 %collective-permute-start.15 = (bf16[1024,1536]{1,0:T(8,128)(2,1)}, bf16[1024,1536]{1,0:T(8,128)(2,1)S(1)}, u32[]{:S(2)}, u32[]{:S(2)}) collective-permute-start(bf16[1024,1536]{1,0:T(8,128)(2,1)} %get-tuple-element.105), channel_id=1, source_target_pairs={{0,4},{4,0},{1,5},{5,1},{2,6},{6,2},{3,7},{7,3},{8,12},{12,8},{9,1... | collective-permute-start | bytes 9437192 | tf_op jit(solution)/shard_map/ppermute | solution.py:877
  265.0 76.7 %all-to-all-start.1 = ((bf16[4,2,128,1536]{3,2,1,0:T(8,128)(2,1)}), bf16[4,2,128,1536]{3,2,1,0:T(8,128)(2,1)}, u32[]{:S(2)}, u32[]{:S(2)}) async-start(bf16[4,2,128,1536]{3,2,1,0:T(8,128)(2,1)} %bitcast.190), calls=%async_computation.1 | async-start | bytes 6291456 | tf_op jit(solution)/shard_map/all_to_all | solution.py:790
  270.1 18.5 %copy-start.40 = (f32[1024,16]{1,0:T(8,128)S(1)}, f32[1024,16]{1,0:T(8,128)}, u32[]{:S(2)}) copy-start(f32[1024,16]{1,0:T(8,128)} %get-tuple-element.110) | copy-start | bytes 196612
  270.1 24.5 %copy-start.16 = (f32[1024,16]{1,0:T(8,128)S(1)}, f32[1024,16]{1,0:T(8,128)}, u32[]{:S(2)}) copy-start(f32[1024,16]{1,0:T(8,128)} %get-tuple-element.111) | copy-start | bytes 196612
  288.2 30.8 %collective-permute-start.14 = (bf16[1024,1536]{1,0:T(8,128)(2,1)}, bf16[1024,1536]{1,0:T(8,128)(2,1)S(1)}, u32[]{:S(2)}, u32[]{:S(2)}) collective-permute-start(bf16[1024,1536]{1,0:T(8,128)(2,1)} %get-tuple-element.103), channel_id=1, source_target_pairs={{0,4},{4,0},{1,5},{5,1},{2,6},{6,2},{3,7},{7,3},{8,12},{12,8},{9,1... | collective-permute-start | bytes 9437192 | tf_op jit(solution)/shard_map/ppermute | solution.py:877
  288.6 6.0 collective-permute-start.16
  341.7 75.5 %all-to-all-start.2 = ((bf16[4,2,128,1536]{3,2,1,0:T(8,128)(2,1)}), bf16[4,2,128,1536]{3,2,1,0:T(8,128)(2,1)}, u32[]{:S(2)}, u32[]{:S(2)}) async-start(bf16[4,2,128,1536]{3,2,1,0:T(8,128)(2,1)} %bitcast.191), calls=%async_computation.2 | async-start | bytes 6291456 | tf_op jit(solution)/shard_map/all_to_all | solution.py:790
  346.4 218.1 %reduce-scatter.4.cloned.1.call-start = ((), (), s32[]{:S(2)}) async-start(), calls=%async_computation.8 | async-start | bytes 11796480 | tf_op jit(solution)/shard_map/reduce_scatter | solution.py:957
  419.4 14.4 %copy-start.5 = (f32[2,128,1536]{2,1,0:T(8,128)S(1)}, f32[2,128,1536]{2,1,0:T(8,128)}, u32[]{:S(2)}) copy-start(f32[2,128,1536]{2,1,0:T(8,128)} %get-tuple-element.99.refs_1_) | copy-start | bytes 4718596
  424.3 27.9 %copy-start.13 = (bf16[2,128,1664]{2,1,0:T(8,128)(2,1)S(1)}, bf16[2,128,1664]{2,1,0:T(8,128)(2,1)}, u32[]{:S(2)}) copy-start(bf16[2,128,1664]{2,1,0:T(8,128)(2,1)} %get-tuple-element.125) | copy-start | bytes 2555908
  424.3 21.1 %collective-permute-start.17 = (bf16[2,128,1664]{2,1,0:T(8,128)(2,1)}, bf16[2,128,1664]{2,1,0:T(8,128)(2,1)S(1)}, u32[]{:S(2)}, u32[]{:S(2)}) collective-permute-start(bf16[2,128,1664]{2,1,0:T(8,128)(2,1)} %get-tuple-element.125), channel_id=1, source_target_pairs={{0,1},{1,2},{2,3},{4,5},{5,6},{6,7},{8,9},{9,10},{10,11},{12,13},{... | collective-permute-start | bytes 2555912 | tf_op jit(solution)/shard_map/ppermute | solution.py:804
  425.8 23.1 %collective-permute-start.20 = (bf16[2,128,1664]{2,1,0:T(8,128)(2,1)}, bf16[2,128,1664]{2,1,0:T(8,128)(2,1)S(1)}, u32[]{:S(2)}, u32[]{:S(2)}) collective-permute-start(bf16[2,128,1664]{2,1,0:T(8,128)(2,1)} %get-tuple-element.125), channel_id=1, source_target_pairs={{1,0},{2,1},{3,2},{5,4},{6,5},{7,6},{9,8},{10,9},{11,10},{13,12},{... | collective-permute-start | bytes 2555912 | tf_op jit(solution)/shard_map/ppermute | solution.py:804
  427.1 40.6 %collective-permute-start.18 = (bf16[2,128,1664]{2,1,0:T(8,128)(2,1)}, bf16[2,128,1664]{2,1,0:T(8,128)(2,1)S(1)}, u32[]{:S(2)}, u32[]{:S(2)}) collective-permute-start(bf16[2,128,1664]{2,1,0:T(8,128)(2,1)} %get-tuple-element.125), channel_id=1, source_target_pairs={{0,3},{3,0},{4,7},{7,4},{8,11},{11,8},{12,15},{15,12},{16,19},{19,... | collective-permute-start | bytes 2555912 | tf_op jit(solution)/shard_map/ppermute | solution.py:808
  445.4 23.4 %collective-permute-start.19 = (bf16[2,128,1664]{2,1,0:T(8,128)(2,1)S(1)}, bf16[2,128,1664]{2,1,0:T(8,128)(2,1)S(1)}, u32[]{:S(2)}, u32[]{:S(2)}) collective-permute-start(bf16[2,128,1664]{2,1,0:T(8,128)(2,1)S(1)} %collective-permute-done.17), channel_id=1, source_target_pairs={{1,2},{2,3},{5,6},{6,7},{9,10},{10,11},{13,14},{14,15},{17,18},{18... | collective-permute-start | bytes 2555912 | tf_op jit(solution)/shard_map/ppermute | solution.py:804
  448.9 36.2 %collective-permute-start.21 = (bf16[2,128,1664]{2,1,0:T(8,128)(2,1)S(1)}, bf16[2,128,1664]{2,1,0:T(8,128)(2,1)S(1)}, u32[]{:S(2)}, u32[]{:S(2)}) collective-permute-start(bf16[2,128,1664]{2,1,0:T(8,128)(2,1)S(1)} %collective-permute-done.20), channel_id=1, source_target_pairs={{1,0},{2,1},{5,4},{6,5},{9,8},{10,9},{13,12},{14,13},{17,16},{18,1... | collective-permute-start | bytes 2555912 | tf_op jit(solution)/shard_map/ppermute | solution.py:804
  489.5 75.1 %all-to-all-start.3 = ((bf16[4,2,128,1536]{3,2,1,0:T(8,128)(2,1)}), bf16[4,2,128,1536]{3,2,1,0:T(8,128)(2,1)}, u32[]{:S(2)}, u32[]{:S(2)}) async-start(bf16[4,2,128,1536]{3,2,1,0:T(8,128)(2,1)} %broadcast_in_dim.130), calls=%async_computation.3 | async-start | bytes 6291456 | tf_op jit(solution)/shard_map/all_to_all | solution.py:795
  494.1 171.2 %reduce-scatter.6.cloned.1.call-start = ((), (), s32[]{:S(2)}) async-start(), calls=%async_computation.9 | async-start | bytes 3981312 | tf_op jit(solution)/shard_map/reduce_scatter | solution.py:957
  511.4 13.7 %collective-permute-start.22 = (bf16[2,128,768]{2,1,0:T(8,128)(2,1)S(1)}, bf16[2,128,768]{2,1,0:T(8,128)(2,1)}, u32[]{:S(2)}, u32[]{:S(2)}) collective-permute-start(bf16[2,128,768]{2,1,0:T(8,128)(2,1)S(1)} %convert_element_type.139), channel_id=1, source_target_pairs={{4,0},{5,1},{6,2},{7,3},{12,8},{13,9},{14,10},{15,11},{20,16},{21,... | collective-permute-start | bytes 1179656 | tf_op jit(solution)/shard_map/ppermute | solution.py:749
  517.7 7.4 copy-start.24
  552.8 13.5 %copy-start.18 = (bf16[1536,128]{1,0:T(8,128)(2,1)S(1)}, bf16[1536,128]{1,0:T(8,128)(2,1)}, u32[]{:S(2)}) copy-start(bf16[1536,128]{1,0:T(8,128)(2,1)} %get-tuple-element.349) | copy-start | bytes 1179652
  552.8 11.7 %collective-permute-start.23 = (f32[2,8,1024]{2,1,0:T(8,128)}, f32[2,8,1024]{2,1,0:T(8,128)}, u32[]{:S(2)}, u32[]{:S(2)}) collective-permute-start(f32[2,8,1024]{2,1,0:T(8,128)} %get-tuple-element.138), channel_id=1, source_target_pairs={{4,0},{5,1},{6,2},{7,3},{12,8},{13,9},{14,10},{15,11},{20,16},{21,... | collective-permute-start | bytes 196616 | tf_op jit(solution)/shard_map/ppermute | solution.py:749
  555.0 5.0 copy-start.27
  564.6 8.0 %slice-start = ((s8[6291456]{0:T(1024)(128)(4,1)}), s8[2097152]{0:T(1024)(128)(4,1)S(1)}, s32[]{:S(2)}) async-start(s8[6291456]{0:T(1024)(128)(4,1)} %bitcast.196), calls=%async_computation.11 | async-start | bytes 4194304
  566.3 6.3 slice-start.1
  589.6 75.7 %all-to-all-start.4 = ((bf16[4,2,128,1536]{3,2,1,0:T(8,128)(2,1)}), bf16[4,2,128,1536]{3,2,1,0:T(8,128)(2,1)S(1)}, u32[]{:S(2)}, u32[]{:S(2)}) async-start(bf16[4,2,128,1536]{3,2,1,0:T(8,128)(2,1)} %get-tuple-element.144), calls=%async_computation.6 | async-start | bytes 6291456 | tf_op jit(solution)/shard_map/all_to_all | solution.py:790
  593.3 169.5 %reduce-scatter.8.cloned.1.call-start = ((), (), s32[]{:S(2)}) async-start(), calls=%async_computation.10 | async-start | bytes 7962624 | tf_op jit(solution)/shard_map/reduce_scatter | solution.py:957
  614.4 60.7 %copy-start.23 = (f32[1536]{0:T(1024)S(1)}, f32[1536]{0:T(1024)}, u32[]{:S(2)}) copy-start(f32[1536]{0:T(1024)} %param.26) | copy-start | bytes 18436
  667.9 5.9 collective-permute-start.24
  674.8 9.2 %collective-permute-start.25 = (bf16[192,384]{1,0:T(8,128)(2,1)S(1)}, bf16[192,384]{1,0:T(8,128)(2,1)S(1)}, u32[]{:S(2)}, u32[]{:S(2)}) collective-permute-start(bf16[192,384]{1,0:T(8,128)(2,1)S(1)} %add_convert_fusion.5), channel_id=1, source_target_pairs={{0,2},{1,3},{2,0},{3,1},{4,6},{5,7},{6,4},{7,5},{8,10},{9,11},{10,... | collective-permute-start | bytes 442376 | tf_op jit(solution)/shard_map/ppermute | solution.py:846
  684.0 28.5 %copy-start.14 = (bf16[192,384]{1,0:T(8,128)(2,1)}, bf16[192,384]{1,0:T(8,128)(2,1)S(1)}, u32[]{:S(2)}) copy-start(bf16[192,384]{1,0:T(8,128)(2,1)S(1)} %add_convert_fusion.4) | copy-start | bytes 442372
  684.0 24.5 %collective-permute-start.26 = (bf16[2,128,1536]{2,1,0:T(8,128)(2,1)}, bf16[2,128,1536]{2,1,0:T(8,128)(2,1)}, u32[]{:S(2)}, u32[]{:S(2)}) collective-permute-start(bf16[2,128,1536]{2,1,0:T(8,128)(2,1)} %shard_map.378), channel_id=1, source_target_pairs={{0,3},{3,0},{4,7},{7,4},{8,11},{11,8},{12,15},{15,12},{16,19},{19,... | collective-permute-start | bytes 2359304 | tf_op jit(solution)/shard_map/ppermute | solution.py:808
  687.4 34.2 %collective-permute-start.27 = (bf16[2,128,1536]{2,1,0:T(8,128)(2,1)}, bf16[2,128,1536]{2,1,0:T(8,128)(2,1)}, u32[]{:S(2)}, u32[]{:S(2)}) collective-permute-start(bf16[2,128,1536]{2,1,0:T(8,128)(2,1)} %shard_map.378), channel_id=1, source_target_pairs={{0,1},{1,2},{2,3},{4,5},{5,6},{6,7},{8,9},{9,10},{10,11},{12,13},{... | collective-permute-start | bytes 2359304 | tf_op jit(solution)/shard_map/ppermute | solution.py:804
  689.5 34.8 %collective-permute-start.29 = (bf16[2,128,1536]{2,1,0:T(8,128)(2,1)}, bf16[2,128,1536]{2,1,0:T(8,128)(2,1)}, u32[]{:S(2)}, u32[]{:S(2)}) collective-permute-start(bf16[2,128,1536]{2,1,0:T(8,128)(2,1)} %shard_map.378), channel_id=1, source_target_pairs={{1,0},{2,1},{3,2},{5,4},{6,5},{7,6},{9,8},{10,9},{11,10},{13,12},{... | collective-permute-start | bytes 2359304 | tf_op jit(solution)/shard_map/ppermute | solution.py:804
  708.5 21.2 %collective-permute-start.31 = (bf16[1,192,384]{2,1,0:T(8,128)(2,1)S(1)}, bf16[1,192,384]{2,1,0:T(8,128)(2,1)S(1)}, u32[]{:S(2)}, u32[]{:S(2)}) collective-permute-start(bf16[1,192,384]{2,1,0:T(8,128)(2,1)S(1)} %bitcast.205), channel_id=1, source_target_pairs={{0,8},{8,0},{16,24},{24,16},{1,9},{9,1},{17,25},{25,17},{2,10},{10... | collective-permute-start | bytes 442376 | tf_op jit(solution)/shard_map/ppermute | solution.py:846
  721.5 23.0 %collective-permute-start.28 = (bf16[2,128,1536]{2,1,0:T(8,128)(2,1)}, bf16[2,128,1536]{2,1,0:T(8,128)(2,1)}, u32[]{:S(2)}, u32[]{:S(2)}) collective-permute-start(bf16[2,128,1536]{2,1,0:T(8,128)(2,1)} %collective-permute-done.27), channel_id=1, source_target_pairs={{1,2},{2,3},{5,6},{6,7},{9,10},{10,11},{13,14},{14,15},{17,18},{18... | collective-permute-start | bytes 2359304 | tf_op jit(solution)/shard_map/ppermute | solution.py:804
  724.4 22.6 %collective-permute-start.30 = (bf16[2,128,1536]{2,1,0:T(8,128)(2,1)}, bf16[2,128,1536]{2,1,0:T(8,128)(2,1)}, u32[]{:S(2)}, u32[]{:S(2)}) collective-permute-start(bf16[2,128,1536]{2,1,0:T(8,128)(2,1)} %collective-permute-done.29), channel_id=1, source_target_pairs={{1,0},{2,1},{5,4},{6,5},{9,8},{10,9},{13,12},{14,13},{17,16},{18,1... | collective-permute-start | bytes 2359304 | tf_op jit(solution)/shard_map/ppermute | solution.py:804
  729.7 13.6 %collective-permute-start.32 = (bf16[2,192,384]{2,1,0:T(8,128)(2,1)S(1)}, bf16[2,192,384]{2,1,0:T(8,128)(2,1)}, u32[]{:S(2)}, u32[]{:S(2)}) collective-permute-start(bf16[2,192,384]{2,1,0:T(8,128)(2,1)S(1)} %maximum_select_fusion.2), channel_id=1, source_target_pairs={{0,16},{8,24},{16,0},{24,8},{1,17},{9,25},{17,1},{25,9},{2,18},{10... | collective-permute-start | bytes 884744 | tf_op jit(solution)/shard_map/ppermute | solution.py:846
  744.5 5.5 collective-permute-start.33
  (23 other events, 57.6 us)
Sparse Core Ops, SparseCore 0:
  417.4 94.2 reduce-scatter.3
  589.7 49.1 reduce-scatter.5
  665.4 66.9 reduce-scatter.7

commit v5 on v4

--- a/solution.py
+++ b/solution.py
@@ -1089,12 +1089,12 @@
         skip,
     )
     early_dx = times_t(z_grad, w_in_zx[0])
-    in_grad, layer_out, early_dx, expert_sum = tie(in_grad, layer_out, early_dx, expert_sum)
+    in_grad, early_dx, expert_sum = tie(in_grad, early_dx, expert_sum)
     in_grad = end_rows(in_grad, last_rows, shifted(first_rows, "seq", -1), taps_bias)
     normed_one_grad = early_dx + times_t(in_grad, w_late)
     grad_norm_one = jnp.sum(normed_one_grad * input_wide * scale_one, axis=(0, 1, 2))
     normed_one_grad = normed_one_grad.astype(bf16)
-    normed_one_grad, in_grad = tie(normed_one_grad, in_grad)
+    normed_one_grad, in_grad, layer_out = tie(normed_one_grad, in_grad, layer_out)
     got_dn = swap_shares(normed_one_grad)
 
     def whole(array):

time: 785 us -> 784 us (level)
  transfers between devices with their start and end apart: 42 -> 42, of which waited for: 20 -> 19; matrix products, arithmetic and copies ran while one was open for 15% -> 16% of each run, Pallas kernels for 21% -> 21%
where the time goes in v5:
time: 784 us; the launch traced here: 774 us
  waiting for transfers between devices  304 us (39%)
  Pallas kernels  224 us (29%)
  local copies, waits for them, and re-layouts  79.5 us (10%)
  starting transfers between devices  74.9 us (10%)
  other arithmetic  43.1 us (5%)
  matrix products  32.5 us (4%)
  between operations  15 us (2%)
    all_to_all x4, waiting for transfers between devices, swap_shares(): return lax.all_to_all(part, 'head', split_axis=0, concat_axis=0, tiled=True)  107 us
    ppermute x12, waiting for transfers between devices, passed(): return lax.ppermute(array, 'head', pairs)  95.1 us
    ppermute x7, waiting for transfers between devices, across(): lax.ppermute(array, axis, [(i, i ^ bit) for i in range(lax.axis_size(axis...  65.4 us
    pallas_call x3, Pallas kernels, weight_grads(): pl.pallas_call(kernel, grid=(steps,), in_specs=specs, out_specs=pl.BlockS...  62.5 us
    pallas_call x2, Pallas kernels, experts_backward(): pl.pallas_call(lambda *refs: expert_backward_kernel(bool(shared), *refs),...  42.4 us
    pallas_call x2, Pallas kernels, experts_forward(): pl.pallas_call(lambda *refs: expert_forward_kernel(bool(shared), *refs),...  39.7 us
    ppermute x3, waiting for transfers between devices, relay(): far = lax.ppermute(part, 'head', [(0, 3), (3, 0)])  30.7 us
    pallas_call x1, Pallas kernels, scan_backward(): pl.pallas_call(scan_back_kernel, grid=(batch, blocks), in_specs=[rows_of(...  25.7 us
  transfers between devices with their start and end apart: 42, of which 19 were waited for; matrix products, arithmetic and copies ran while one was open for 16% of the time, Pallas kernels for 21%

profile of v5, /device:TPU:0, one launch (start us, length us, event | category | flops | bytes accessed | tf_op | source)
XLA Modules:
  0.0 773.6 jit_solution(12593163152394489439)
XLA Ops:
  7.2 2.6 fusion
  14.1 3.7 fusion.19.cin.cin_before
  19.8 3.0 collective-permute-start
  22.8 4.3 fusion.15.z
  29.0 3.7 fusion.21.raw
  35.1 14.4 %shard_map.365 = (bf16[4,2,128,1024]{3,2,1,0:T(8,128)(2,1)}, f32[4,2,128,768]{3,2,1,0:T(8,128)}, f32[2,2,128,768]{3,2,1,0:T(8,128)}, f32[2,128,768]{2,1,0:T(8,128)}) custom-call(bf16[4,2,128,1024]{3,2,1,0:T(8,128)(2,1)} %copy-done.4, f32[2,8,1024]{2,1,0:T(8,128)} %collective-permute-done.edge, f32[8,1024]{1,0:T(8,128)} %maximum_maximum_fusion.taps.taps_ref, ...), custom_call_target="tpu_custom_call" | custom-call | flops 1207959552 | bytes 7864320 | tf_op jit(solution)/shard_map/pallas_call | solution.py:310
  49.5 2.2 collective-permute-start.1
  54.4 12.2 %shard_map.366 = (bf16[4,2,128,768]{3,2,1,0:T(8,128)(2,1)}, bf16[4,2,128,768]{3,2,1,0:T(8,128)(2,1)}, f32[4,2,128,128]{3,2,1,0:T(8,128)}, bf16[4,2,128,1536]{3,2,1,0:T(8,128)(2,1)}) custom-call(f32[4,2,128,768]{3,2,1,0:T(8,128)} %get-tuple-element.93.y, bf16[4,2,128,1024]{3,2,1,0:T(8,128)(2,1)} %get-tuple-element.92.act_in, f32[4,2,128,768]{3,2,1,0:T(8,128)} %fusion.15.z, ...), custom_call_target="tpu_custom_call" | custom-call | flops 2617245696 | bytes 14155776 | tf_op jit(solution)/shard_map/pallas_call | solution.py:346
  66.7 5.9 all-to-all-start
  72.6 3.8 copy.286
  78.7 2.1 collective-permute-start.3
  80.8 41.9 %collective-permute-done.3 = f32[4,2,128]{2,1,0:T(2,128)S(1)} collective-permute-done((f32[4,2,128]{2,1,0:T(2,128)S(1)}, f32[4,2,128]{2,1,0:T(2,128)S(1)}, u32[]{:S(2)}, u32[]{:S(2)}) %collective-permute-start.3) | collective-permute-done | bytes 4128 | tf_op jit(solution)/shard_map/ppermute | solution.py:846
  122.7 4.7 collective-permute-start.4
  129.6 13.0 %collective-permute-done.4 = f32[4,2,128]{2,1,0:T(2,128)S(1)} collective-permute-done((f32[4,2,128]{2,1,0:T(2,128)S(1)}, f32[4,2,128]{2,1,0:T(2,128)S(1)}, u32[]{:S(2)}, u32[]{:S(2)}) %collective-permute-start.4) | collective-permute-done | bytes 4128 | tf_op jit(solution)/shard_map/ppermute | solution.py:846
  143.5 4.2 shard_map.367
  147.7 2.2 collective-permute-start.6
  149.9 2.5 collective-permute-start.7
  155.0 13.7 %collective-permute-done.6 = bf16[2,128,1664]{2,1,0:T(8,128)(2,1)} collective-permute-done((bf16[2,128,1664]{2,1,0:T(8,128)(2,1)}, bf16[2,128,1664]{2,1,0:T(8,128)(2,1)}, u32[]{:S(2)}, u32[]{:S(2)}) %collective-permute-start.6) | collective-permute-done | bytes 852000 | tf_op jit(solution)/shard_map/ppermute | solution.py:804
  169.4 22.7 %collective-permute-done.10 = bf16[2,128,1664]{2,1,0:T(8,128)(2,1)} collective-permute-done((bf16[2,128,1664]{2,1,0:T(8,128)(2,1)}, bf16[2,128,1664]{2,1,0:T(8,128)(2,1)}, u32[]{:S(2)}, u32[]{:S(2)}) %collective-permute-start.10) | collective-permute-done | bytes 852000 | tf_op jit(solution)/shard_map/ppermute | solution.py:804
  195.0 2.1 broadcast.52.clone.1
  198.0 17.1 %collective-permute-done.11 = bf16[2,128,1664]{2,1,0:T(8,128)(2,1)S(1)} collective-permute-done((bf16[2,128,1664]{2,1,0:T(8,128)(2,1)}, bf16[2,128,1664]{2,1,0:T(8,128)(2,1)S(1)}, u32[]{:S(2)}, u32[]{:S(2)}) %collective-permute-start.11) | collective-permute-done | bytes 852000 | tf_op jit(solution)/shard_map/ppermute | solution.py:804
  220.9 18.4 %shard_map.368 = (bf16[1024,1536]{1,0:T(8,128)(2,1)}, f32[1024,16]{1,0:T(8,128)}, f32[1024,2048]{1,0:T(8,128)}) custom-call(bf16[1024,1664]{1,0:T(8,128)(2,1)} %bitcast.25.refs_0_.refs_2_.refs_1_, bf16[1024,1536]{1,0:T(8,128)(2,1)} %bitcast.17.refs_1_.refs_0_.refs_4_, bf16[1024,1664]{1,0:T(8,128)(2,1)} %bitcast.25.refs_0_.refs_2_.refs_1_, ...), custom_call_target="tpu_custom_call" | custom-call | flops 9663676416 | bytes 27262976 | tf_op jit(solution)/shard_map/pallas_call | solution.py:631
  239.3 21.4 %shard_map.370 = (bf16[1024,1536]{1,0:T(8,128)(2,1)}, f32[1024,16]{1,0:T(8,128)}, f32[1024,2560]{1,0:T(8,128)}) custom-call(bf16[1024,1664]{1,0:T(8,128)(2,1)} %bitcast.184, bf16[1024,1536]{1,0:T(8,128)(2,1)} %bitcast.16.refs_1_.refs_0_.refs_6_, bf16[1024,1664]{1,0:T(8,128)(2,1)} %bitcast.185, f32[8,16]{1,0:T(8,128)} %fusion.27.refs_3_, ...), custom_call_target="tpu_custom_call" | custom-call | flops 12079595520 | bytes 31719424 | tf_op jit(solution)/shard_map/pallas_call | solution.py:631
  260.7 4.4 add_convert_fusion.1
  265.0 5.1 all-to-all-start.1
  270.1 18.0 %shard_map.369 = (bf16[1024,1536]{1,0:T(8,128)(2,1)}, bf16[1024,1024]{1,0:T(8,128)(2,1)}, bf16[1024,2048]{1,0:T(8,128)(2,1)}) custom-call(bf16[1024,1536]{1,0:T(8,128)(2,1)} %bitcast.17.refs_1_.refs_0_.refs_4_, bf16[1024,1664]{1,0:T(8,128)(2,1)} %bitcast.25.refs_0_.refs_2_.refs_1_, f32[1024,2048]{1,0:T(8,128)} %get-tuple-element.102.refs_2_, ...), custom_call_target="tpu_custom_call" | custom-call | flops 9663676416 | bytes 30408704 | tf_op jit(solution)/shard_map/pallas_call | solution.py:651
  288.7 5.9 collective-permute-done.16
  294.6 24.3 %shard_map.371 = (bf16[1024,1536]{1,0:T(8,128)(2,1)}, bf16[1024,1024]{1,0:T(8,128)(2,1)}, bf16[1024,2048]{1,0:T(8,128)(2,1)}, bf16[1024,256]{1,0:T(8,128)(2,1)}, bf16[1024,512]{1,0:T(8,128)(2,1)}) custom-call(bf16[1024,1536]{1,0:T(8,128)(2,1)} %bitcast.16.refs_1_.refs_0_.refs_6_, bf16[1024,1664]{1,0:T(8,128)(2,1)} %bitcast.186, ...), custom_call_target="tpu_custom_call" | custom-call | flops 12079595520 | bytes 36438016 | tf_op jit(solution)/shard_map/pallas_call | solution.py:651
  319.0 4.6 add_convert_fusion
  323.5 18.2 %all-to-all-done.1 = bf16[4,2,128,1536]{3,2,1,0:T(8,128)(2,1)} async-done(((bf16[4,2,128,1536]{3,2,1,0:T(8,128)(2,1)}), bf16[4,2,128,1536]{3,2,1,0:T(8,128)(2,1)}, u32[]{:S(2)}, u32[]{:S(2)}) %all-to-all-start.1) | async-done | bytes 3145760 | tf_op jit(solution)/shard_map/all_to_all | solution.py:790
  341.7 4.7 all-to-all-start.2
  346.6 32.2 %shard_map.372 = bf16[1536,3072]{1,0:T(8,128)(2,1)} custom-call(bf16[1024,1664]{1,0:T(8,128)(2,1)} %bitcast.25.refs_0_.refs_2_.refs_1_, bf16[1024,2048]{1,0:T(8,128)(2,1)} %get-tuple-element.118.refs_1_, bf16[1024,1664]{1,0:T(8,128)(2,1)} %bitcast.187, bf16[1024,2048]{1,0:T(8,128)(2,1)} %get-tuple-element.119.refs_3_, ...), custom_call_target="tpu_custom_call" | custom-call | flops 19327352832 | bytes 34603008 | tf_op jit(solution)/shard_map/pallas_call | solution.py:532
  378.8 38.4 %all-to-all-done.2.refs_0_ = bf16[4,2,128,1536]{3,2,1,0:T(8,128)(2,1)} async-done(((bf16[4,2,128,1536]{3,2,1,0:T(8,128)(2,1)}), bf16[4,2,128,1536]{3,2,1,0:T(8,128)(2,1)}, u32[]{:S(2)}, u32[]{:S(2)}) %all-to-all-start.2) | async-done | bytes 3145760 | tf_op jit(solution)/shard_map/all_to_all | solution.py:790
  417.3 2.1 dynamic-slice_bitcast_fusion.refs_4_
  419.4 5.0 shard_map.373
  427.1 6.6 collective-permute-start.18
  433.7 2.3 fusion.20
  436.1 9.4 %collective-permute-done.17 = bf16[2,128,1664]{2,1,0:T(8,128)(2,1)S(1)} collective-permute-done((bf16[2,128,1664]{2,1,0:T(8,128)(2,1)}, bf16[2,128,1664]{2,1,0:T(8,128)(2,1)S(1)}, u32[]{:S(2)}, u32[]{:S(2)}) %collective-permute-start.17) | collective-permute-done | bytes 852000 | tf_op jit(solution)/shard_map/ppermute | solution.py:804
  446.2 2.8 collective-permute-done.20
  453.1 14.5 %collective-permute-done.18 = bf16[2,128,1664]{2,1,0:T(8,128)(2,1)S(1)} collective-permute-done((bf16[2,128,1664]{2,1,0:T(8,128)(2,1)}, bf16[2,128,1664]{2,1,0:T(8,128)(2,1)S(1)}, u32[]{:S(2)}, u32[]{:S(2)}) %collective-permute-start.18) | collective-permute-done | bytes 852000 | tf_op jit(solution)/shard_map/ppermute | solution.py:808
  468.8 16.3 %collective-permute-done.21 = bf16[2,128,1664]{2,1,0:T(8,128)(2,1)S(1)} collective-permute-done((bf16[2,128,1664]{2,1,0:T(8,128)(2,1)S(1)}, bf16[2,128,1664]{2,1,0:T(8,128)(2,1)S(1)}, u32[]{:S(2)}, u32[]{:S(2)}) %collective-permute-start.21) | collective-permute-done | bytes 852000 | tf_op jit(solution)/shard_map/ppermute | solution.py:804
  489.5 4.6 all-to-all-start.3
  494.4 2.6 fusion.36
  498.6 11.7 %shard_map.374 = (bf16[4,2,128,768]{3,2,1,0:T(8,128)(2,1)}, bf16[4,2,128,768]{3,2,1,0:T(8,128)(2,1)}, f32[2,128,768]{2,1,0:T(8,128)}, f32[8,768]{1,0:T(8,128)}) custom-call(bf16[4,2,128,1664]{3,2,1,0:T(8,128)(2,1)} %bitcast_dynamic-update-slice_fusion.push.slope_in, bf16[768,1536]{1,0:T(8,128)(2,1)} %w_out.3, ...), custom_call_target="tpu_custom_call" | custom-call | flops 2617245696 | bytes 14155776 | tf_op jit(solution)/shard_map/pallas_call | solution.py:379
  517.7 7.4 fusion.13
  527.1 25.7 %shard_map.375 = (bf16[4,2,128,1152]{3,2,1,0:T(8,128)(2,1)}, f32[2,8,1024]{2,1,0:T(8,128)}, f32[2,8,1024]{2,1,0:T(8,128)}, f32[8,1024]{1,0:T(8,128)}) custom-call(bf16[4,2,128,1024]{3,2,1,0:T(8,128)(2,1)} %copy-done.4, bf16[4,2,128,1024]{3,2,1,0:T(8,128)(2,1)} %copy-done.4, f32[2,8,1024]{2,1,0:T(8,128)} %collective-permute-done.edge, ...), custom_call_target="tpu_custom_call" | custom-call | flops 2617245696 | bytes 11796480 | tf_op jit(solution)/shard_map/pallas_call | solution.py:413
  563.9 6.2 fusion.5
  570.2 2.4 fusion.4
  572.7 3.2 concatenate.43
  577.3 9.8 %shard_map.377 = bf16[1536,1152]{1,0:T(8,128)(2,1)} custom-call(bf16[1024,1536]{1,0:T(8,128)(2,1)} %bitcast.192, bf16[1024,1152]{1,0:T(8,128)(2,1)} %bitcast.202, bf16[1536,128]{1,0:T(8,128)(2,1)} %bitcast.207), custom_call_target="tpu_custom_call" | custom-call | flops 3623878656 | bytes 9830400 | tf_op jit(solution)/shard_map/pallas_call | solution.py:532
  587.1 5.0 all-to-all-start.4
  592.4 20.5 %shard_map.379 = bf16[1536,2304]{1,0:T(8,128)(2,1)} custom-call(bf16[1024,1664]{1,0:T(8,128)(2,1)} %bitcast.46.refs_0_, bf16[1024,768]{1,0:T(8,128)(2,1)} %bitcast.217, bf16[1024,1536]{1,0:T(8,128)(2,1)} %bitcast.193, bf16[1024,768]{1,0:T(8,128)(2,1)} %bitcast.218, bf16[1024,1664]{1,0:T(8,128)(2,1)} %bitcast.189, ...), custom_call_target="tpu_custom_call" | custom-call | flops 7247757312 | bytes 32243712 | tf_op jit(solution)/shard_map/pallas_call | solution.py:532
  612.9 50.4 %all-to-all-done.4.got = bf16[4,2,128,1536]{3,2,1,0:T(8,128)(2,1)S(1)} async-done(((bf16[4,2,128,1536]{3,2,1,0:T(8,128)(2,1)}), bf16[4,2,128,1536]{3,2,1,0:T(8,128)(2,1)S(1)}, u32[]{:S(2)}, u32[]{:S(2)}) %all-to-all-start.4) | async-done | bytes 3145760 | tf_op jit(solution)/shard_map/all_to_all | solution.py:790
  665.9 6.6 collective-permute-done.24
  674.2 4.8 shard_map.378
  679.0 3.9 collective-permute-done.25
  682.9 3.6 collective-permute-start.26
  686.5 2.2 collective-permute-start.27
  691.2 16.2 %collective-permute-done.26 = bf16[2,128,1536]{2,1,0:T(8,128)(2,1)} collective-permute-done((bf16[2,128,1536]{2,1,0:T(8,128)(2,1)}, bf16[2,128,1536]{2,1,0:T(8,128)(2,1)}, u32[]{:S(2)}, u32[]{:S(2)}) %collective-permute-start.26) | collective-permute-done | bytes 786464 | tf_op jit(solution)/shard_map/ppermute | solution.py:808
  709.0 2.3 convert_element_type.156
  711.4 9.3 %collective-permute-done.27 = bf16[2,128,1536]{2,1,0:T(8,128)(2,1)} collective-permute-done((bf16[2,128,1536]{2,1,0:T(8,128)(2,1)}, bf16[2,128,1536]{2,1,0:T(8,128)(2,1)}, u32[]{:S(2)}, u32[]{:S(2)}) %collective-permute-start.27) | collective-permute-done | bytes 786464 | tf_op jit(solution)/shard_map/ppermute | solution.py:804
  732.7 3.8 copy.256
  737.1 3.0 copy.267
  743.3 2.9 collective-permute-done.30
  (283 shorter events, 114.1 us)
Async XLA Ops:
  12.4 10.4 %slice-start.2 = ((s8[4718592]{0:T(1024)(128)(4,1)}), s8[4194304]{0:T(1024)(128)(4,1)S(1)}, s32[]{:S(2)}) async-start(s8[4718592]{0:T(1024)(128)(4,1)} %bitcast.203), calls=%async_computation.13 | async-start | bytes 8388608
  14.1 8.7 %copy-start.3 = (bf16[4,2,128,1536]{3,2,1,0:T(8,128)(2,1)}, bf16[4,2,128,1536]{3,2,1,0:T(8,128)(2,1)S(1)}, u32[]{:S(2)}) copy-start(bf16[4,2,128,1536]{3,2,1,0:T(8,128)(2,1)S(1)} %fusion.2) | copy-start | bytes 9437188
  14.1 8.7 %slice-start.3 = ((s8[4718592]{0:T(1024)(128)(4,1)}), s8[524288]{0:T(1024)(128)(4,1)S(1)}, s32[]{:S(2)}) async-start(s8[4718592]{0:T(1024)(128)(4,1)} %bitcast.203), calls=%async_computation.14 | async-start | bytes 1048576
  19.8 15.3 %collective-permute-start = (f32[2,8,1024]{2,1,0:T(8,128)}, f32[2,8,1024]{2,1,0:T(8,128)}, u32[]{:S(2)}, u32[]{:S(2)}) collective-permute-start(f32[2,8,1024]{2,1,0:T(8,128)} %fusion.24), channel_id=1, source_target_pairs={{0,4},{1,5},{2,6},{3,7},{8,12},{9,13},{10,14},{11,15},{16,20},{17,... | collective-permute-start | bytes 196616 | tf_op jit(solution)/shard_map/ppermute | solution.py:749
  27.1 5.7 copy-start.28
  28.1 4.6 copy-start.32
  28.1 4.6 copy-start.33
  35.1 18.0 %copy-start.35 = (f32[12]{0:T(128)S(1)}, f32[12]{0:T(128)}, u32[]{:S(2)}) copy-start(f32[12]{0:T(128)} %param.35) | copy-start | bytes 148
  35.1 18.7 %copy-start.31 = (f32[768]{0:T(1024)S(1)}, f32[768]{0:T(1024)}, u32[]{:S(2)}) copy-start(f32[768]{0:T(1024)} %param.36) | copy-start | bytes 9220
  49.5 4.9 collective-permute-start.1
  66.7 76.8 %all-to-all-start = ((bf16[4,2,128,1536]{3,2,1,0:T(8,128)(2,1)}), bf16[4,2,128,1536]{3,2,1,0:T(8,128)(2,1)}, u32[]{:S(2)}, u32[]{:S(2)}) async-start(bf16[4,2,128,1536]{3,2,1,0:T(8,128)(2,1)} %get-tuple-element.96), calls=%async_computation | async-start | bytes 6291456 | tf_op jit(solution)/shard_map/all_to_all | solution.py:790
  72.6 55.5 %copy-start.30 = (f32[1536]{0:T(1024)S(1)}, f32[1536]{0:T(1024)}, u32[]{:S(2)}) copy-start(f32[1536]{0:T(1024)} %param.38) | copy-start | bytes 18436
  72.6 56.1 %copy-start.19 = (bf16[1536,16]{0,1:T(8,128)(2,1)S(1)}, bf16[1536,16]{0,1:T(8,128)(2,1)}, u32[]{:S(2)}) copy-start(bf16[1536,16]{0,1:T(8,128)(2,1)} %param.39) | copy-start | bytes 147460
  76.4 67.1 %collective-permute-start.2 = (bf16[4,2,128,1536]{3,2,1,0:T(8,128)(2,1)}, bf16[4,2,128,1536]{3,2,1,0:T(8,128)(2,1)}, u32[]{:S(2)}, u32[]{:S(2)}) collective-permute-start(bf16[4,2,128,1536]{3,2,1,0:T(8,128)(2,1)} %bitcast.180), channel_id=1, source_target_pairs={{0,4},{4,0},{1,5},{5,1},{2,6},{6,2},{3,7},{7,3},{8,12},{12,8},{9,1... | collective-permute-start | bytes 9437192 | tf_op jit(solution)/shard_map/ppermute | solution.py:877
  78.7 44.0 %collective-permute-start.3 = (f32[4,2,128]{2,1,0:T(2,128)S(1)}, f32[4,2,128]{2,1,0:T(2,128)S(1)}, u32[]{:S(2)}, u32[]{:S(2)}) collective-permute-start(f32[4,2,128]{2,1,0:T(2,128)S(1)} %slice_reduce_fusion.2), channel_id=1, source_target_pairs={{0,1},{1,0},{2,3},{3,2},{4,5},{5,4},{6,7},{7,6},{8,9},{9,8},{10,11... | collective-permute-start | bytes 12296 | tf_op jit(solution)/shard_map/ppermute | solution.py:846
  122.7 20.0 %collective-permute-start.4 = (f32[4,2,128]{2,1,0:T(2,128)S(1)}, f32[4,2,128]{2,1,0:T(2,128)S(1)}, u32[]{:S(2)}, u32[]{:S(2)}) collective-permute-start(f32[4,2,128]{2,1,0:T(2,128)S(1)} %add.179), channel_id=1, source_target_pairs={{0,2},{1,3},{2,0},{3,1},{4,6},{5,7},{6,4},{7,5},{8,10},{9,11},{10,... | collective-permute-start | bytes 12296 | tf_op jit(solution)/shard_map/ppermute | solution.py:846
  147.7 21.0 %collective-permute-start.6 = (bf16[2,128,1664]{2,1,0:T(8,128)(2,1)}, bf16[2,128,1664]{2,1,0:T(8,128)(2,1)}, u32[]{:S(2)}, u32[]{:S(2)}) collective-permute-start(bf16[2,128,1664]{2,1,0:T(8,128)(2,1)} %get-tuple-element.101), channel_id=1, source_target_pairs={{0,1},{1,2},{2,3},{4,5},{5,6},{6,7},{8,9},{9,10},{10,11},{12,13},{... | collective-permute-start | bytes 2555912 | tf_op jit(solution)/shard_map/ppermute | solution.py:804
  149.9 43.5 %collective-permute-start.7 = (bf16[2,128,1664]{2,1,0:T(8,128)(2,1)}, bf16[2,128,1664]{2,1,0:T(8,128)(2,1)}, u32[]{:S(2)}, u32[]{:S(2)}) collective-permute-start(bf16[2,128,1664]{2,1,0:T(8,128)(2,1)} %get-tuple-element.101), channel_id=1, source_target_pairs={{0,3},{3,0},{4,7},{7,4},{8,11},{11,8},{12,15},{15,12},{16,19},{19,... | collective-permute-start | bytes 2555912 | tf_op jit(solution)/shard_map/ppermute | solution.py:808
  152.4 39.8 %collective-permute-start.10 = (bf16[2,128,1664]{2,1,0:T(8,128)(2,1)}, bf16[2,128,1664]{2,1,0:T(8,128)(2,1)}, u32[]{:S(2)}, u32[]{:S(2)}) collective-permute-start(bf16[2,128,1664]{2,1,0:T(8,128)(2,1)} %get-tuple-element.101), channel_id=1, source_target_pairs={{1,0},{2,1},{3,2},{5,4},{6,5},{7,6},{9,8},{10,9},{11,10},{13,12},{... | collective-permute-start | bytes 2555912 | tf_op jit(solution)/shard_map/ppermute | solution.py:804
  154.4 40.5 %collective-permute-start.5 = (bf16[2,128,1664]{2,1,0:T(8,128)(2,1)}, bf16[2,128,1664]{2,1,0:T(8,128)(2,1)S(1)}, u32[]{:S(2)}, u32[]{:S(2)}) collective-permute-start(bf16[2,128,1664]{2,1,0:T(8,128)(2,1)} %get-tuple-element.101), channel_id=1, source_target_pairs={{0,4},{4,0},{1,5},{5,1},{2,6},{6,2},{3,7},{7,3},{8,12},{12,8},{9,1... | collective-permute-start | bytes 2555912 | tf_op jit(solution)/shard_map/ppermute | solution.py:877
  168.7 29.3 %collective-permute-start.9 = (bf16[2,128,1664]{2,1,0:T(8,128)(2,1)}, bf16[2,128,1664]{2,1,0:T(8,128)(2,1)S(1)}, u32[]{:S(2)}, u32[]{:S(2)}) collective-permute-start(bf16[2,128,1664]{2,1,0:T(8,128)(2,1)} %collective-permute-done.6), channel_id=1, source_target_pairs={{1,2},{2,3},{5,6},{6,7},{9,10},{10,11},{13,14},{14,15},{17,18},{18... | collective-permute-start | bytes 2555912 | tf_op jit(solution)/shard_map/ppermute | solution.py:804
  192.1 23.0 %collective-permute-start.11 = (bf16[2,128,1664]{2,1,0:T(8,128)(2,1)}, bf16[2,128,1664]{2,1,0:T(8,128)(2,1)S(1)}, u32[]{:S(2)}, u32[]{:S(2)}) collective-permute-start(bf16[2,128,1664]{2,1,0:T(8,128)(2,1)} %collective-permute-done.10), channel_id=1, source_target_pairs={{1,0},{2,1},{5,4},{6,5},{9,8},{10,9},{13,12},{14,13},{17,16},{18,1... | collective-permute-start | bytes 2555912 | tf_op jit(solution)/shard_map/ppermute | solution.py:804
  194.9 22.6 %collective-permute-start.8 = (bf16[2,128,1664]{2,1,0:T(8,128)(2,1)S(1)}, bf16[2,128,1664]{2,1,0:T(8,128)(2,1)S(1)}, u32[]{:S(2)}, u32[]{:S(2)}) collective-permute-start(bf16[2,128,1664]{2,1,0:T(8,128)(2,1)S(1)} %get-tuple-element.331), channel_id=1, source_target_pairs={{0,4},{4,0},{1,5},{5,1},{2,6},{6,2},{3,7},{7,3},{8,12},{12,8},{9,1... | collective-permute-start | bytes 2555912 | tf_op jit(solution)/shard_map/ppermute | solution.py:877
  215.4 3.5 collective-permute-start.12
  216.9 22.4 %copy-start.1 = (bf16[4,2,128,1664]{3,2,1,0:T(8,128)(2,1)}, bf16[4,2,128,1664]{3,2,1,0:T(8,128)(2,1)S(1)}, u32[]{:S(2)}) copy-start(bf16[4,2,128,1664]{3,2,1,0:T(8,128)(2,1)S(1)} %get-tuple-element.326) | copy-start | bytes 10223620
  216.9 3.0 collective-permute-start.13
  239.3 21.4 %collective-permute-start.15 = (bf16[1024,1536]{1,0:T(8,128)(2,1)}, bf16[1024,1536]{1,0:T(8,128)(2,1)S(1)}, u32[]{:S(2)}, u32[]{:S(2)}) collective-permute-start(bf16[1024,1536]{1,0:T(8,128)(2,1)} %get-tuple-element.105), channel_id=1, source_target_pairs={{0,4},{4,0},{1,5},{5,1},{2,6},{6,2},{3,7},{7,3},{8,12},{12,8},{9,1... | collective-permute-start | bytes 9437192 | tf_op jit(solution)/shard_map/ppermute | solution.py:877
  265.0 76.7 %all-to-all-start.1 = ((bf16[4,2,128,1536]{3,2,1,0:T(8,128)(2,1)}), bf16[4,2,128,1536]{3,2,1,0:T(8,128)(2,1)}, u32[]{:S(2)}, u32[]{:S(2)}) async-start(bf16[4,2,128,1536]{3,2,1,0:T(8,128)(2,1)} %bitcast.190), calls=%async_computation.1 | async-start | bytes 6291456 | tf_op jit(solution)/shard_map/all_to_all | solution.py:790
  270.1 18.5 %copy-start.40 = (f32[1024,16]{1,0:T(8,128)S(1)}, f32[1024,16]{1,0:T(8,128)}, u32[]{:S(2)}) copy-start(f32[1024,16]{1,0:T(8,128)} %get-tuple-element.110) | copy-start | bytes 196612
  270.1 24.5 %copy-start.16 = (f32[1024,16]{1,0:T(8,128)S(1)}, f32[1024,16]{1,0:T(8,128)}, u32[]{:S(2)}) copy-start(f32[1024,16]{1,0:T(8,128)} %get-tuple-element.111) | copy-start | bytes 196612
  288.2 30.8 %collective-permute-start.14 = (bf16[1024,1536]{1,0:T(8,128)(2,1)}, bf16[1024,1536]{1,0:T(8,128)(2,1)S(1)}, u32[]{:S(2)}, u32[]{:S(2)}) collective-permute-start(bf16[1024,1536]{1,0:T(8,128)(2,1)} %get-tuple-element.103), channel_id=1, source_target_pairs={{0,4},{4,0},{1,5},{5,1},{2,6},{6,2},{3,7},{7,3},{8,12},{12,8},{9,1... | collective-permute-start | bytes 9437192 | tf_op jit(solution)/shard_map/ppermute | solution.py:877
  288.6 6.0 collective-permute-start.16
  341.7 75.5 %all-to-all-start.2 = ((bf16[4,2,128,1536]{3,2,1,0:T(8,128)(2,1)}), bf16[4,2,128,1536]{3,2,1,0:T(8,128)(2,1)}, u32[]{:S(2)}, u32[]{:S(2)}) async-start(bf16[4,2,128,1536]{3,2,1,0:T(8,128)(2,1)} %bitcast.191), calls=%async_computation.2 | async-start | bytes 6291456 | tf_op jit(solution)/shard_map/all_to_all | solution.py:790
  346.4 215.7 %reduce-scatter.4.cloned.1.call-start = ((), (), s32[]{:S(2)}) async-start(), calls=%async_computation.8 | async-start | bytes 11796480 | tf_op jit(solution)/shard_map/reduce_scatter | solution.py:957
  419.4 14.4 %copy-start.5 = (f32[2,128,1536]{2,1,0:T(8,128)S(1)}, f32[2,128,1536]{2,1,0:T(8,128)}, u32[]{:S(2)}) copy-start(f32[2,128,1536]{2,1,0:T(8,128)} %get-tuple-element.99.refs_1_) | copy-start | bytes 4718596
  424.3 27.9 %copy-start.13 = (bf16[2,128,1664]{2,1,0:T(8,128)(2,1)S(1)}, bf16[2,128,1664]{2,1,0:T(8,128)(2,1)}, u32[]{:S(2)}) copy-start(bf16[2,128,1664]{2,1,0:T(8,128)(2,1)} %get-tuple-element.125) | copy-start | bytes 2555908
  424.3 21.1 %collective-permute-start.17 = (bf16[2,128,1664]{2,1,0:T(8,128)(2,1)}, bf16[2,128,1664]{2,1,0:T(8,128)(2,1)S(1)}, u32[]{:S(2)}, u32[]{:S(2)}) collective-permute-start(bf16[2,128,1664]{2,1,0:T(8,128)(2,1)} %get-tuple-element.125), channel_id=1, source_target_pairs={{0,1},{1,2},{2,3},{4,5},{5,6},{6,7},{8,9},{9,10},{10,11},{12,13},{... | collective-permute-start | bytes 2555912 | tf_op jit(solution)/shard_map/ppermute | solution.py:804
  425.8 23.1 %collective-permute-start.20 = (bf16[2,128,1664]{2,1,0:T(8,128)(2,1)}, bf16[2,128,1664]{2,1,0:T(8,128)(2,1)S(1)}, u32[]{:S(2)}, u32[]{:S(2)}) collective-permute-start(bf16[2,128,1664]{2,1,0:T(8,128)(2,1)} %get-tuple-element.125), channel_id=1, source_target_pairs={{1,0},{2,1},{3,2},{5,4},{6,5},{7,6},{9,8},{10,9},{11,10},{13,12},{... | collective-permute-start | bytes 2555912 | tf_op jit(solution)/shard_map/ppermute | solution.py:804
  427.1 40.6 %collective-permute-start.18 = (bf16[2,128,1664]{2,1,0:T(8,128)(2,1)}, bf16[2,128,1664]{2,1,0:T(8,128)(2,1)S(1)}, u32[]{:S(2)}, u32[]{:S(2)}) collective-permute-start(bf16[2,128,1664]{2,1,0:T(8,128)(2,1)} %get-tuple-element.125), channel_id=1, source_target_pairs={{0,3},{3,0},{4,7},{7,4},{8,11},{11,8},{12,15},{15,12},{16,19},{19,... | collective-permute-start | bytes 2555912 | tf_op jit(solution)/shard_map/ppermute | solution.py:808
  445.4 23.4 %collective-permute-start.19 = (bf16[2,128,1664]{2,1,0:T(8,128)(2,1)S(1)}, bf16[2,128,1664]{2,1,0:T(8,128)(2,1)S(1)}, u32[]{:S(2)}, u32[]{:S(2)}) collective-permute-start(bf16[2,128,1664]{2,1,0:T(8,128)(2,1)S(1)} %collective-permute-done.17), channel_id=1, source_target_pairs={{1,2},{2,3},{5,6},{6,7},{9,10},{10,11},{13,14},{14,15},{17,18},{18... | collective-permute-start | bytes 2555912 | tf_op jit(solution)/shard_map/ppermute | solution.py:804
  448.9 36.2 %collective-permute-start.21 = (bf16[2,128,1664]{2,1,0:T(8,128)(2,1)S(1)}, bf16[2,128,1664]{2,1,0:T(8,128)(2,1)S(1)}, u32[]{:S(2)}, u32[]{:S(2)}) collective-permute-start(bf16[2,128,1664]{2,1,0:T(8,128)(2,1)S(1)} %collective-permute-done.20), channel_id=1, source_target_pairs={{1,0},{2,1},{5,4},{6,5},{9,8},{10,9},{13,12},{14,13},{17,16},{18,1... | collective-permute-start | bytes 2555912 | tf_op jit(solution)/shard_map/ppermute | solution.py:804
  489.5 83.2 %all-to-all-start.3 = ((bf16[4,2,128,1536]{3,2,1,0:T(8,128)(2,1)}), bf16[4,2,128,1536]{3,2,1,0:T(8,128)(2,1)}, u32[]{:S(2)}, u32[]{:S(2)}) async-start(bf16[4,2,128,1536]{3,2,1,0:T(8,128)(2,1)} %broadcast_in_dim.130), calls=%async_computation.4 | async-start | bytes 6291456 | tf_op jit(solution)/shard_map/all_to_all | solution.py:795
  494.1 169.1 %reduce-scatter.6.cloned.1.call-start = ((), (), s32[]{:S(2)}) async-start(), calls=%async_computation.9 | async-start | bytes 3981312 | tf_op jit(solution)/shard_map/reduce_scatter | solution.py:957
  511.4 13.7 %collective-permute-start.22 = (bf16[2,128,768]{2,1,0:T(8,128)(2,1)S(1)}, bf16[2,128,768]{2,1,0:T(8,128)(2,1)}, u32[]{:S(2)}, u32[]{:S(2)}) collective-permute-start(bf16[2,128,768]{2,1,0:T(8,128)(2,1)S(1)} %convert_element_type.139), channel_id=1, source_target_pairs={{4,0},{5,1},{6,2},{7,3},{12,8},{13,9},{14,10},{15,11},{20,16},{21,... | collective-permute-start | bytes 1179656 | tf_op jit(solution)/shard_map/ppermute | solution.py:749
  517.7 7.4 copy-start.24
  552.8 11.0 %copy-start.18 = (bf16[1536,128]{1,0:T(8,128)(2,1)S(1)}, bf16[1536,128]{1,0:T(8,128)(2,1)}, u32[]{:S(2)}) copy-start(bf16[1536,128]{1,0:T(8,128)(2,1)} %get-tuple-element.349) | copy-start | bytes 1179652
  552.8 9.3 %collective-permute-start.23 = (f32[2,8,1024]{2,1,0:T(8,128)}, f32[2,8,1024]{2,1,0:T(8,128)}, u32[]{:S(2)}, u32[]{:S(2)}) collective-permute-start(f32[2,8,1024]{2,1,0:T(8,128)} %get-tuple-element.137), channel_id=1, source_target_pairs={{4,0},{5,1},{6,2},{7,3},{12,8},{13,9},{14,10},{15,11},{20,16},{21,... | collective-permute-start | bytes 196616 | tf_op jit(solution)/shard_map/ppermute | solution.py:749
  555.0 5.0 copy-start.27
  562.1 8.0 %slice-start = ((s8[6291456]{0:T(1024)(128)(4,1)}), s8[2097152]{0:T(1024)(128)(4,1)S(1)}, s32[]{:S(2)}) async-start(s8[6291456]{0:T(1024)(128)(4,1)} %bitcast.196), calls=%async_computation.11 | async-start | bytes 4194304
  563.8 6.3 slice-start.1
  587.1 76.1 %all-to-all-start.4 = ((bf16[4,2,128,1536]{3,2,1,0:T(8,128)(2,1)}), bf16[4,2,128,1536]{3,2,1,0:T(8,128)(2,1)S(1)}, u32[]{:S(2)}, u32[]{:S(2)}) async-start(bf16[4,2,128,1536]{3,2,1,0:T(8,128)(2,1)} %get-tuple-element.144), calls=%async_computation.6 | async-start | bytes 6291456 | tf_op jit(solution)/shard_map/all_to_all | solution.py:790
  592.2 169.8 %reduce-scatter.8.cloned.1.call-start = ((), (), s32[]{:S(2)}) async-start(), calls=%async_computation.10 | async-start | bytes 7962624 | tf_op jit(solution)/shard_map/reduce_scatter | solution.py:957
  612.9 60.7 %copy-start.23 = (f32[1536]{0:T(1024)S(1)}, f32[1536]{0:T(1024)}, u32[]{:S(2)}) copy-start(f32[1536]{0:T(1024)} %param.26) | copy-start | bytes 18436
  665.8 6.7 collective-permute-start.24
  673.5 9.4 %collective-permute-start.25 = (bf16[192,384]{1,0:T(8,128)(2,1)S(1)}, bf16[192,384]{1,0:T(8,128)(2,1)S(1)}, u32[]{:S(2)}, u32[]{:S(2)}) collective-permute-start(bf16[192,384]{1,0:T(8,128)(2,1)S(1)} %add_convert_fusion.5), channel_id=1, source_target_pairs={{0,2},{1,3},{2,0},{3,1},{4,6},{5,7},{6,4},{7,5},{8,10},{9,11},{10,... | collective-permute-start | bytes 442376 | tf_op jit(solution)/shard_map/ppermute | solution.py:846
  682.9 28.5 %copy-start.14 = (bf16[192,384]{1,0:T(8,128)(2,1)}, bf16[192,384]{1,0:T(8,128)(2,1)S(1)}, u32[]{:S(2)}) copy-start(bf16[192,384]{1,0:T(8,128)(2,1)S(1)} %add_convert_fusion.4) | copy-start | bytes 442372
  682.9 24.5 %collective-permute-start.26 = (bf16[2,128,1536]{2,1,0:T(8,128)(2,1)}, bf16[2,128,1536]{2,1,0:T(8,128)(2,1)}, u32[]{:S(2)}, u32[]{:S(2)}) collective-permute-start(bf16[2,128,1536]{2,1,0:T(8,128)(2,1)} %shard_map.378), channel_id=1, source_target_pairs={{0,3},{3,0},{4,7},{7,4},{8,11},{11,8},{12,15},{15,12},{16,19},{19,... | collective-permute-start | bytes 2359304 | tf_op jit(solution)/shard_map/ppermute | solution.py:808
  686.5 34.2 %collective-permute-start.27 = (bf16[2,128,1536]{2,1,0:T(8,128)(2,1)}, bf16[2,128,1536]{2,1,0:T(8,128)(2,1)}, u32[]{:S(2)}, u32[]{:S(2)}) collective-permute-start(bf16[2,128,1536]{2,1,0:T(8,128)(2,1)} %shard_map.378), channel_id=1, source_target_pairs={{0,1},{1,2},{2,3},{4,5},{5,6},{6,7},{8,9},{9,10},{10,11},{12,13},{... | collective-permute-start | bytes 2359304 | tf_op jit(solution)/shard_map/ppermute | solution.py:804
  688.7 34.6 %collective-permute-start.29 = (bf16[2,128,1536]{2,1,0:T(8,128)(2,1)}, bf16[2,128,1536]{2,1,0:T(8,128)(2,1)}, u32[]{:S(2)}, u32[]{:S(2)}) collective-permute-start(bf16[2,128,1536]{2,1,0:T(8,128)(2,1)} %shard_map.378), channel_id=1, source_target_pairs={{1,0},{2,1},{3,2},{5,4},{6,5},{7,6},{9,8},{10,9},{11,10},{13,12},{... | collective-permute-start | bytes 2359304 | tf_op jit(solution)/shard_map/ppermute | solution.py:804
  707.4 21.2 %collective-permute-start.31 = (bf16[1,192,384]{2,1,0:T(8,128)(2,1)S(1)}, bf16[1,192,384]{2,1,0:T(8,128)(2,1)S(1)}, u32[]{:S(2)}, u32[]{:S(2)}) collective-permute-start(bf16[1,192,384]{2,1,0:T(8,128)(2,1)S(1)} %bitcast.205), channel_id=1, source_target_pairs={{0,8},{8,0},{16,24},{24,16},{1,9},{9,1},{17,25},{25,17},{2,10},{10... | collective-permute-start | bytes 442376 | tf_op jit(solution)/shard_map/ppermute | solution.py:846
  720.7 22.5 %collective-permute-start.28 = (bf16[2,128,1536]{2,1,0:T(8,128)(2,1)}, bf16[2,128,1536]{2,1,0:T(8,128)(2,1)}, u32[]{:S(2)}, u32[]{:S(2)}) collective-permute-start(bf16[2,128,1536]{2,1,0:T(8,128)(2,1)} %collective-permute-done.27), channel_id=1, source_target_pairs={{1,2},{2,3},{5,6},{6,7},{9,10},{10,11},{13,14},{14,15},{17,18},{18... | collective-permute-start | bytes 2359304 | tf_op jit(solution)/shard_map/ppermute | solution.py:804
  723.3 22.9 %collective-permute-start.30 = (bf16[2,128,1536]{2,1,0:T(8,128)(2,1)}, bf16[2,128,1536]{2,1,0:T(8,128)(2,1)}, u32[]{:S(2)}, u32[]{:S(2)}) collective-permute-start(bf16[2,128,1536]{2,1,0:T(8,128)(2,1)} %collective-permute-done.29), channel_id=1, source_target_pairs={{1,0},{2,1},{5,4},{6,5},{9,8},{10,9},{13,12},{14,13},{17,16},{18,1... | collective-permute-start | bytes 2359304 | tf_op jit(solution)/shard_map/ppermute | solution.py:804
  728.7 13.4 %collective-permute-start.32 = (bf16[2,192,384]{2,1,0:T(8,128)(2,1)S(1)}, bf16[2,192,384]{2,1,0:T(8,128)(2,1)}, u32[]{:S(2)}, u32[]{:S(2)}) collective-permute-start(bf16[2,192,384]{2,1,0:T(8,128)(2,1)S(1)} %maximum_select_fusion.2), channel_id=1, source_target_pairs={{0,16},{8,24},{16,0},{24,8},{1,17},{9,25},{17,1},{25,9},{2,18},{10... | collective-permute-start | bytes 884744 | tf_op jit(solution)/shard_map/ppermute | solution.py:846
  743.2 6.0 collective-permute-start.33
  (23 other events, 57.5 us)
Sparse Core Ops, SparseCore 0:
  417.4 94.2 reduce-scatter.3
  587.3 51.6 reduce-scatter.5
  663.4 67.2 reduce-scatter.7
